TPU v7x, 128 devices: a whole 4x4x4 slice. The times are simulated.
128 devices in a mesh: gx: 4 (over y), gy: 32 (over x, z, core).
Axes of the slice: x: 4, y: 4, z: 4, core: 2. Of those that a mesh axis runs over, the one named last changes fastest.
Arguments:
- state: float32 [128, 1024, 256], P('gx', 'gy'), may hold values from -6 to 6
- group_member: int32 [131072, 1], P(('gx', 'gy')), may hold values from 0 to 127; in each aligned block of 1024 rows (0 to 1023, 1024 to 2047, ...) at most 16 rows name the same one
- w_in: bfloat16 [128, 256, 1024], P(('gx', 'gy')), may hold values from -0.375 to 0.375
- bias_in: float32 [128, 1024], P(('gx', 'gy')), may hold values from -3 to 3
- w_mid: bfloat16 [128, 1024, 1024], P(('gx', 'gy')), may hold values from -0.1875 to 0.1875
- bias_mid: float32 [128, 1024], P(('gx', 'gy')), may hold values from -3 to 3
- w_out: bfloat16 [128, 1024, 264], P(('gx', 'gy')), may hold values from -0.1875 to 0.1875
- intersection_element: int32 [16384], P(('gx', 'gy')), may hold values from 0 to 63
- ocean_owner: int32 [16384, 1], P(('gx', 'gy')), may hold values from 0 to 127; in each aligned block of 128 rows (0 to 127, 128 to 255, ...) at most 2 rows name the same one
- ocean_block: int32 [16384], P(('gx', 'gy')), may hold values from 0 to 15
- regrid_weight: float32 [16384, 256], P(('gx', 'gy')), may hold values from 0 to 0.25
Outputs:
- new_state: float32 [128, 1024, 256], P('gx', 'gy')
- ocean_flux: float32 [2048, 128], P(('gx', 'gy'))
Inputs may be any that keep to these rules, and one draw needn't show every extreme that they name: `group_member`: in the columns of one device no member is named more than 16 times, and exactly 16 times for some member. `ocean_owner`: among the intersections of one device no owner is named more than 2 times, and exactly 2 times for some owner.
All inputs are finite; a program needn't handle non-finite values.
Results may differ from a plain program's by a relative error of at most 0.0046.
Values may be sent and summed in bfloat16 or wider, within the bound.
No kernel may reach another device: no remote copies, remote signals or barrier semaphores. Data moves between devices by JAX's collectives and lax.ppermute only.
A program may use at most 64 MiB of HBM per device.

v0:
```python
import math

import jax
import jax.numpy as jnp
import numpy as np
from jax import lax
from jax.sharding import PartitionSpec as P

LEV = 64
OB_DEV = 16


STEP_DT = 0.2
HIGHEST = lax.Precision.HIGHEST


def padded_2(value, sides, width):
    for axis, dim in sides:
        count, length = (lax.axis_size(axis), value.shape[dim])
        up = [(i, (i + 1) % count) for i in range(count)]
        down = [(j, i) for i, j in up]
        last = lax.slice_in_dim(value, length - width, length, axis=dim)
        leading = lax.slice_in_dim(value, 0, width, axis=dim)
        before = lax.ppermute(last, axis, up)
        after = lax.ppermute(leading, axis, down)
        value = jnp.concatenate([before, value, after], axis=dim)
    return value


def derivative_table():
    root = 1.0 / math.sqrt(5.0)
    nodes = np.array([-1.0, -root, root, 1.0])
    table = np.zeros((4, 4))
    for row_index in range(4):
        for col_index in range(4):
            if row_index == col_index:
                table[row_index, col_index] = sum(
                    (
                        1.0 / (nodes[row_index] - nodes[other])
                        for other in range(4)
                        if other != row_index
                    )
                )
            else:
                weight_row = np.prod(
                    [nodes[row_index] - nodes[other] for other in range(4) if other != row_index]
                )
                weight_col = np.prod(
                    [nodes[col_index] - nodes[other] for other in range(4) if other != col_index]
                )
                table[row_index, col_index] = weight_row / (
                    weight_col * (nodes[row_index] - nodes[col_index])
                )
    return table


def element_tendency(field, deriv_table, levels):
    size_x, size_y, features = field.shape
    along_x = jnp.einsum(
        "ij,ejyf->eiyf",
        deriv_table,
        field.reshape(size_x // 4, 4, size_y, features),
        precision=HIGHEST,
    )
    along_y = jnp.einsum(
        "ij,xejf->xeif",
        deriv_table,
        field.reshape(size_x, size_y // 4, 4, features),
        precision=HIGHEST,
    )
    grid = field.reshape(size_x, size_y, 4, levels)
    wind_u = grid[:, :, 2:3, :]
    wind_v = grid[:, :, 3:4, :]
    tendency = -(
        wind_u * along_x.reshape(size_x, size_y, 4, levels)
        + wind_v * along_y.reshape(size_x, size_y, 4, levels)
    )
    return tendency.reshape(size_x, size_y, features)


def slot_positions(owners, capacity, peer_count):
    one_hot = (owners[:, None] == jnp.arange(peer_count, dtype=jnp.int32)[None, :]).astype(
        jnp.int32
    )
    rank = jnp.sum(jnp.cumsum(one_hot, axis=0) * one_hot, axis=1) - 1
    return owners * capacity + rank


def run_member(flat_rows, weights):
    w_first, b_first, w_second, b_second, w_last = weights
    hidden_one = jax.nn.silu(
        jnp.dot(flat_rows, w_first, preferred_element_type=jnp.float32) + b_first
    ).astype(jnp.bfloat16)
    hidden_two = jax.nn.silu(
        jnp.dot(hidden_one, w_second, preferred_element_type=jnp.float32) + b_second
    ).astype(jnp.bfloat16)
    return jnp.dot(hidden_two, w_last, preferred_element_type=jnp.float32).astype(jnp.bfloat16)


def shards(
    state,
    group_member,
    w_in,
    bias_in,
    w_mid,
    bias_mid,
    w_out,
    intersection_element,
    ocean_owner,
    ocean_block,
    regrid_weight,
):
    size_x, size_y, features = state.shape
    deriv_table = jnp.asarray(derivative_table(), dtype=jnp.float32)
    tendency = element_tendency(state, deriv_table, LEV)
    padded = padded_2(tendency, (("gx", 0), ("gy", 1)), 1)
    row_phase = (jnp.arange(size_x) % 4)[:, None, None]
    middle = padded[1:-1]
    along_x = jnp.where(
        row_phase == 0,
        0.5 * (middle + padded[:-2]),
        jnp.where(row_phase == 3, 0.5 * (middle + padded[2:]), middle),
    )
    col_phase = (jnp.arange(size_y) % 4)[None, :, None]
    centre = along_x[:, 1:-1]
    smooth = jnp.where(
        col_phase == 0,
        0.5 * (centre + along_x[:, :-2]),
        jnp.where(col_phase == 3, 0.5 * (centre + along_x[:, 2:]), centre),
    )
    advanced = state + STEP_DT * smooth
    col_count = size_x * size_y
    columns = advanced.reshape(col_count, features).astype(jnp.bfloat16)
    grid_x = lax.axis_size("gx")
    grid_y = lax.axis_size("gy")
    devices = grid_x * grid_y
    capacity = 2 * col_count // devices
    slot_index = slot_positions(group_member[:, 0], capacity, devices)
    send_buffer = (
        jnp.zeros((devices * capacity, features), jnp.bfloat16).at[slot_index].set(columns)
    )
    weights = (w_in[0], bias_in[0], w_mid[0], bias_mid[0], w_out[0])
    received = lax.all_to_all(
        send_buffer.reshape(devices, capacity, features),
        ("gx", "gy"),
        split_axis=0,
        concat_axis=0,
        tiled=True,
    )
    lead_shape = received.shape[:-1]
    result_rows = run_member(received.reshape(-1, features), weights)
    answered = result_rows.reshape(lead_shape + (result_rows.shape[-1],))
    returned = lax.all_to_all(answered, ("gx", "gy"), split_axis=0, concat_axis=0, tiled=True)
    outputs = returned.reshape(devices * capacity, -1)[slot_index]
    new_state = advanced + outputs[:, :features].astype(jnp.float32).reshape(
        size_x, size_y, features
    )
    fluxes = outputs[:, features:]
    flux_count = fluxes.shape[1]
    flux_blocks = (
        fluxes.reshape(size_x // 4, 4, size_y // 4, 4, flux_count)
        .transpose(0, 2, 1, 3, 4)
        .reshape(-1, 16, flux_count)
    )
    picked = flux_blocks[intersection_element]
    intersection_count = picked.shape[0]
    regrid_blocks = regrid_weight.reshape(intersection_count, 16, -1)
    contribution = jnp.einsum(
        "kcf,kco->kfo", picked.astype(jnp.float32), regrid_blocks, precision=HIGHEST
    ).reshape(intersection_count, -1)
    owners = ocean_owner[:, 0]
    target = owners * OB_DEV + ocean_block
    dense_sum = jax.ops.segment_sum(contribution, target, num_segments=devices * OB_DEV)
    ocean_total = lax.psum_scatter(dense_sum, ("gx", "gy"), scatter_dimension=0, tiled=True)
    return (new_state, ocean_total)


def solution(mesh):
    return jax.shard_map(
        shards,
        mesh=mesh,
        in_specs=(
            P("gx", "gy", None),
            P(("gx", "gy"), None),
            P(("gx", "gy"), None, None),
            P(("gx", "gy"), None),
            P(("gx", "gy"), None, None),
            P(("gx", "gy"), None),
            P(("gx", "gy"), None, None),
            P(("gx", "gy")),
            P(("gx", "gy"), None),
            P(("gx", "gy")),
            P(("gx", "gy"), None),
        ),
        out_specs=(P("gx", "gy", None), P(("gx", "gy"), None)),
        check_vma=False,
    )
```

profile of v0, /device:TPU:1, one launch (start us, length us, event | category | flops | bytes accessed | tf_op | source)
XLA Modules:
  0.0 796.1 jit_solution(4181537968994907632)
XLA Ops:
  7.2 3.2 reshape.119
  11.7 4.4 fusion.33
  16.1 2.3 convolution_bitcast_fusion.1
  19.6 3.1 reshape.121
  22.6 4.0 convolution_bitcast_fusion
  26.7 3.2 reshape.123
  29.9 3.7 add_negate_fusion
  33.7 2.1 collective-permute-start
  37.6 2.6 reshape.125
  40.1 2.7 mul.75
  42.9 3.2 mul.80
  46.1 2.7 mul.78
  48.8 3.2 mul.82
  57.0 2.7 collective-permute-start.2
  60.8 2.6 collective-permute-done.3
  65.6 5.7 scatter_custom_fusion
  71.3 28.0 %all_to_all.10 = bf16[128,16,256]{2,1,0:T(8,128)(2,1)S(1)} all-to-all(bf16[128,16,256]{2,1,0:T(8,128)(2,1)S(1)} %bitcast.76), channel_id=1, replica_groups=mesh['gx'=4,'gy'=32] {'gx','gy'}, dimensions={0} | all-to-all | bytes 2097152 | tf_op jit(solution)/shard_map/all_to_all | solution.py:143
  99.3 4.0 multiply_convert_fusion.1
  103.3 9.6 %fusion.3 = bf16[2048,264]{0,1:T(8,128)(2,1)} fusion(f32[1024]{0:T(1024)S(1)} %bitcast.90, bf16[2048,1024]{1,0:T(8,128)(2,1)} %multiply_convert_fusion.1, bf16[1,1024,1024]{2,1,0:T(8,128)(2,1)S(1)} %copy-done, bf16[1,1024,264]{1,2,0:T(8,128)(2,1)S(1)} %copy-done.9), kind=kOutput, calls=%fused_computation.8 | convolution fusion | flops 5415387136 | bytes 7917568 | tf_op jit(solution)/shard_map/dot_general | solution.py:97
  112.9 2.5 copy.24
  115.4 5.8 all-to-all-start.1
  121.9 23.8 %all-to-all-done.1 = bf16[128,16,264]{2,1,0:T(8,128)(2,1)} async-done(((bf16[128,16,264]{2,1,0:T(8,128)(2,1)}), bf16[128,16,264]{2,1,0:T(8,128)(2,1)}, u32[]{:S(2)}, u32[]{:S(2)}) %all-to-all-start.1) | async-done | bytes 1081376 | tf_op jit(solution)/shard_map/all_to_all | solution.py:153
  145.7 6.5 gather_fusion
  163.2 626.0 %reduce-scatter.2.cloned.1.call-done = f32[16,128]{1,0:T(8,128)} async-done(((f32[2048,128]{1,0:T(8,128)}), f32[16,128]{1,0:T(8,128)}) %reduce-scatter.2.cloned.1.call-update) | async-done | bytes 8208 | tf_op jit(solution)/shard_map/reduce_scatter | solution.py:174
  (77 shorter events, 24.1 us)
Async XLA Ops:
  7.2 96.1 %copy-start = (bf16[1,1024,1024]{2,1,0:T(8,128)(2,1)S(1)}, bf16[1,1024,1024]{2,1,0:T(8,128)(2,1)}, u32[]{:S(2)}) copy-start(bf16[1,1024,1024]{2,1,0:T(8,128)(2,1)} %param.16) | copy-start | bytes 6291460
  7.2 3.2 copy-start.1
  10.4 5.6 copy-start.8
  33.7 23.3 %collective-permute-start = (f32[1,32,256]{2,1,0:T(8,128)S(1)}, f32[1,32,256]{2,1,0:T(8,128)S(1)}, u32[]{:S(2)}, u32[]{:S(2)}) collective-permute-start(f32[1,32,256]{2,1,0:T(8,128)S(1)} %slice.57), channel_id=1, source_target_pairs={{0,32},{32,64},{64,96},{96,0},{1,33},{33,65},{65,97},{97,1},{2,34}... | collective-permute-start | bytes 98312 | tf_op jit(solution)/shard_map/ppermute | solution.py:24
  35.9 21.0 %collective-permute-start.1 = (f32[1,32,256]{2,1,0:T(8,128)S(1)}, f32[1,32,256]{2,1,0:T(8,128)S(1)}, u32[]{:S(2)}, u32[]{:S(2)}) collective-permute-start(f32[1,32,256]{2,1,0:T(8,128)S(1)} %slice.59), channel_id=1, source_target_pairs={{32,0},{64,32},{96,64},{0,96},{33,1},{65,33},{97,65},{1,97},{34,2}... | collective-permute-start | bytes 98312 | tf_op jit(solution)/shard_map/ppermute | solution.py:25
  48.8 3.2 copy-start.7
  52.3 0.8 copy-start.5
  53.1 1.7 copy-start.2
  53.1 1.7 copy-start.3
  57.0 3.8 collective-permute-start.2
  59.7 3.7 collective-permute-start.3
  65.6 33.6 %copy-start.11 = (f32[1,1024]{1,0:T(1,128)S(1)}, f32[1,1024]{1,0:T(1,128)}, u32[]{:S(2)}) copy-start(f32[1,1024]{1,0:T(1,128)} %param.15) | copy-start | bytes 12292
  71.3 28.0 %copy-start.10 = (bf16[1,256,1024]{2,1,0:T(8,128)(2,1)S(1)}, bf16[1,256,1024]{2,1,0:T(8,128)(2,1)}, u32[]{:S(2)}) copy-start(bf16[1,256,1024]{2,1,0:T(8,128)(2,1)} %param.14) | copy-start | bytes 1572868
  99.3 4.0 copy-start.9
  99.3 4.0 copy-start.12
  115.4 5.8 copy-start.6
  115.4 6.4 copy-start.13
  115.4 6.5 copy-start.14
  115.4 6.5 copy-start.15
  115.4 30.3 %all-to-all-start.1 = ((bf16[128,16,264]{2,1,0:T(8,128)(2,1)}), bf16[128,16,264]{2,1,0:T(8,128)(2,1)}, u32[]{:S(2)}, u32[]{:S(2)}) async-start(bf16[128,16,264]{2,1,0:T(8,128)(2,1)} %bitcast.71), calls=%async_computation.1 | async-start | bytes 3145728 | tf_op jit(solution)/shard_map/all_to_all | solution.py:153
  121.1 668.1 %reduce-scatter.2.cloned.1.call-start = ((), (), s32[]{:S(2)}) async-start(), calls=%async_computation.3 | async-start | bytes 1056768 | tf_op jit(solution)/shard_map/reduce_scatter | solution.py:174
  157.5 4.5 copy-start.4
Sparse Core Ops, SparseCore 0:
  161.0 628.1 reduce-scatter.1
where the time goes:
time: 803 us; the launch traced here: 796 us
  waiting for transfers between devices  654 us (81%)
  local copies, waits for them, and re-layouts  53.6 us (7%)
  blocking collectives  28 us (3%)
  matrix products  21.4 us (3%)
  between operations  14.3 us (2%)
  other arithmetic  12.9 us (2%)
  starting transfers between devices  12.4 us (2%)
    reduce_scatter x1, waiting for transfers between devices, shards(): lax.psum_scatter(dense_sum, ('gx', 'gy'), scatter_dimension=0, tiled=True)  626 us
    all_to_all x1, blocking collectives, shards(): lax.all_to_all(send_buffer.reshape(devices, capacity, features), ('gx', '...  28 us
    all_to_all x1, waiting for transfers between devices, shards(): lax.all_to_all(answered, ('gx', 'gy'), split_axis=0, concat_axis=0, tiled...  23.8 us
  transfers between devices with their start and end apart: 6, of which 4 were waited for; matrix products, arithmetic and copies ran while one was open for 3% of the time, Pallas kernels for 0%

commit v1 on v0

--- a/solution.py
+++ b/solution.py
@@ -169,9 +169,28 @@
         "kcf,kco->kfo", picked.astype(jnp.float32), regrid_blocks, precision=HIGHEST
     ).reshape(intersection_count, -1)
     owners = ocean_owner[:, 0]
-    target = owners * OB_DEV + ocean_block
-    dense_sum = jax.ops.segment_sum(contribution, target, num_segments=devices * OB_DEV)
-    ocean_total = lax.psum_scatter(dense_sum, ("gx", "gy"), scatter_dimension=0, tiled=True)
+    ocean_capacity = 2 * intersection_count // devices
+    ocean_slot = slot_positions(owners, ocean_capacity, devices)
+    ocean_rows = devices * ocean_capacity
+    width = contribution.shape[1]
+    ocean_send = jnp.zeros((ocean_rows, width), jnp.float32).at[ocean_slot].set(contribution)
+    block_send = jnp.zeros((ocean_rows,), jnp.int32).at[ocean_slot].set(ocean_block)
+    block_got = lax.all_to_all(
+        block_send.reshape(devices, ocean_capacity),
+        ("gx", "gy"),
+        split_axis=0,
+        concat_axis=0,
+        tiled=True,
+    ).reshape(-1)
+    ocean_got = lax.all_to_all(
+        ocean_send.reshape(devices, ocean_capacity, width),
+        ("gx", "gy"),
+        split_axis=0,
+        concat_axis=0,
+        tiled=True,
+    ).reshape(ocean_rows, width)
+    pick = (block_got[None, :] == jnp.arange(OB_DEV, dtype=jnp.int32)[:, None]).astype(jnp.float32)
+    ocean_total = jnp.dot(pick, ocean_got, precision=HIGHEST)
     return (new_state, ocean_total)
 
 

time: 803 us -> 181 us (0.23)
  waiting for transfers between devices: 654 us -> 50.2 us
  blocking collectives: 28 us -> 0 us
  starting transfers between devices: 12.4 us -> 35 us
  between operations: 14.3 us -> 0.98 us
    reduce_scatter x1 -> x0, waiting for transfers between devices: 626 us -> none  [shards(): lax.psum_scatter(dense_sum, ('gx', 'gy'), scatter_dimension=0, tiled=True)]
    all_to_all x1 -> x0, blocking collectives: 28 us -> none  [shards(): lax.all_to_all(send_buffer.reshape(devices, capacity, features), ('gx', '...]
    all_to_all x0 -> x3, waiting for transfers between devices: none -> 24.3 us  [the longest x1 16.8 us: shards(): lax.all_to_all(send_buffer.reshape(devices, capacity, features), ('gx', '...]
    all_to_all x0 -> x3, starting transfers between devices: none -> 18.2 us  [the longest x1 8.98 us: shards(): lax.all_to_all(send_buffer.reshape(devices, capacity, features), ('gx', '...]
  transfers between devices with their start and end apart: 6 -> 8, of which waited for: 4 -> 5; matrix products, arithmetic and copies ran while one was open for 3% -> 22% of each run, Pallas kernels for 0% -> 0%
where the time goes in v1:
time: 181 us; the launch traced here: 180 us
  local copies, waits for them, and re-layouts  58.1 us (32%)
  waiting for transfers between devices  50.2 us (28%)
  starting transfers between devices  35 us (19%)
  matrix products  22.2 us (12%)
  other arithmetic  13.5 us (7%)
    all_to_all x1, waiting for transfers between devices, shards(): lax.all_to_all(answered, ('gx', 'gy'), split_axis=0, concat_axis=0, tiled...  22.3 us
    all_to_all x1, waiting for transfers between devices, shards(): lax.all_to_all(send_buffer.reshape(devices, capacity, features), ('gx', '...  16.8 us
    all_to_all x1, starting transfers between devices, shards(): lax.all_to_all(answered, ('gx', 'gy'), split_axis=0, concat_axis=0, tiled...  10.3 us
    all_to_all x1, starting transfers between devices, shards(): lax.all_to_all(send_buffer.reshape(devices, capacity, features), ('gx', '...  8.98 us
    dot_general x1, matrix products, run_member(): jnp.dot(hidden_two, w_last, preferred_element_type=jnp.float32)  8.67 us
    all_to_all x1, waiting for transfers between devices, shards(): lax.all_to_all(ocean_send.reshape(devices, ocean_capacity, width), ('gx',...  7.42 us
    gather x1, local copies, waits for them, and re-layouts, shards(): outputs = returned.reshape(devices * capacity, -1)[slot_index]  6.45 us
    scatter x1, local copies, waits for them, and re-layouts, shards(): jnp.zeros((devices * capacity, features), jnp.bfloat16).at[slot_index]  6.41 us
  transfers between devices with their start and end apart: 8, of which 5 were waited for; matrix products, arithmetic and copies ran while one was open for 22% of the time, Pallas kernels for 0%

profile of v1, /device:TPU:1, one launch (start us, length us, event | category | flops | bytes accessed | tf_op | source)
XLA Modules:
  0.0 180.0 jit_solution(10592055621586289008)
XLA Ops:
  0.7 3.2 %reshape.138 = f32[32,32,4,64]{3,2,1,0:T(4,128)} reshape(f32[32,32,256]{2,1,0:T(8,128)} %param.12) | data formatting | bytes 2097152 | tf_op jit(solution)/shard_map/reshape | solution.py:71
  5.2 4.4 %fusion.39 = (f32[32,32,1,64]{3,2,1,0:T(1,128)}, f32[32,32,1,64]{3,2,1,0:T(1,128)}) fusion(f32[32,32,4,64]{3,2,1,0:T(4,128)} %reshape.138), kind=kLoop, calls=%fused_computation.74 | loop fusion | bytes 1048576 | tf_op jit(solution)/shard_map/slice | solution.py:72
  13.1 3.1 %reshape.140 = f32[32,32,4,64]{3,2,1,0:T(4,128)} reshape(f32[8,4,32,256]{3,2,1,0:T(8,128)} %copy.46) | data formatting | bytes 2097152 | tf_op jit(solution)/shard_map/reshape | solution.py:75
  16.1 4.0 %convolution_bitcast_fusion = f32[32,8,4,256]{3,2,1,0:T(4,128)} fusion(f32[4,4,1,1]{1,0,3,2:T(4,128)S(1)} %copy-done.7, f32[32,8,4,256]{3,2,1,0:T(4,128)} %reshape.141), kind=kOutput, calls=%fused_computation.13 | convolution fusion | flops 12582912 | bytes 2097216 | tf_op jit(solution)/shard_map/ij,xejf->xeif/dot_general | solution.py:65
  20.2 3.2 %reshape.142 = f32[32,32,4,64]{3,2,1,0:T(4,128)} reshape(f32[32,8,4,256]{3,2,1,0:T(4,128)} %convolution_bitcast_fusion) | data formatting | bytes 2097152 | tf_op jit(solution)/shard_map/reshape | solution.py:76
  23.4 3.7 %add_negate_fusion = f32[32,32,4,64]{3,2,1,0:T(4,128)S(1)} fusion(f32[32,32,4,64]{3,2,1,0:T(4,128)} %reshape.142, f32[32,32,4,64]{3,2,1,0:T(4,128)} %reshape.140, f32[32,32,64]{2,1,0:T(8,128)} %bitcast.81, f32[32,32,64]{2,1,0:T(8,128)} %bitcast.83), kind=kLoop, calls=%fused_computation.11 | loop fusion | flops 1048576 | bytes 3670016 | tf_op jit(solution)/shard_map/neg | solution.py:74
  31.1 2.6 %reshape.144 = f32[32,32,256]{2,1,0:T(8,128)} reshape(f32[32,8,4,256]{3,2,1,0:T(4,128)} %convolution_bitcast_fusion) | data formatting | bytes 2097152 | tf_op jit(solution)/shard_map/reshape | solution.py:76
  33.6 2.8 %mul.76 = f32[32,32,4,64]{3,2,1,0:T(4,128)} broadcast(f32[32,32,64]{2,1,0:T(8,128)} %bitcast.84), dimensions={0,1,3} | broadcast | bytes 1310720 | tf_op jit(solution)/shard_map/mul | solution.py:75
  36.4 3.2 %mul.81 = f32[32,32,256]{2,1,0:T(8,128)} reshape(f32[32,32,4,64]{3,2,1,0:T(4,128)} %mul.76) | data formatting | bytes 2097152 | tf_op jit(solution)/shard_map/mul | solution.py:75
  39.6 2.8 %mul.79 = f32[32,32,4,64]{3,2,1,0:T(4,128)} broadcast(f32[32,32,64]{2,1,0:T(8,128)} %bitcast.82), dimensions={0,1,3} | broadcast | bytes 1310720 | tf_op jit(solution)/shard_map/mul | solution.py:76
  42.3 3.2 %mul.83 = f32[32,32,256]{2,1,0:T(8,128)} reshape(f32[32,32,4,64]{3,2,1,0:T(4,128)} %mul.79) | data formatting | bytes 2097152 | tf_op jit(solution)/shard_map/mul | solution.py:76
  50.5 2.7 %collective-permute-start.2 = (f32[34,1,256]{2,1,0:T(1,128)S(1)}, f32[34,1,256]{2,1,0:T(1,128)S(1)}, u32[]{:S(2)}, u32[]{:S(2)}) collective-permute-start(f32[34,1,256]{2,1,0:T(1,128)S(1)} %get-tuple-element.8), channel_id=1, source_target_pairs={{0,1},{1,2},{2,3},{3,4},{4,5},{5,6},{6,7},{7,8},{8,9},{9,10},{10,1... | collective-permute-start | bytes 104456 | tf_op jit(solution)/shard_map/ppermute | solution.py:24
  54.3 2.6 %collective-permute-done.3 = f32[34,1,256]{2,1,0:T(1,128)S(1)} collective-permute-done((f32[34,1,256]{2,1,0:T(1,128)S(1)}, f32[34,1,256]{2,1,0:T(1,128)S(1)}, u32[]{:S(2)}, u32[]{:S(2)}) %collective-permute-start.3) | collective-permute-done | bytes 34848 | tf_op jit(solution)/shard_map/ppermute | solution.py:25
  59.2 6.4 %scatter_custom_fusion = bf16[2048,256]{1,0:T(8,128)(2,1)} fusion(s32[1024]{0:T(1024)S(1)} %bitcast.95, bf16[1024,256]{1,0:T(8,128)(2,1)} %bitcast.89, bf16[]{:T(256)} %constant.59.clone.1), kind=kCustom, calls=%fused_computation.42 | custom fusion | bytes 1049088 | tf_op jit(solution)/shard_map/scatter | solution.py:140
  65.6 9.0 %all-to-all-start = ((bf16[128,16,256]{2,1,0:T(8,128)(2,1)}), bf16[128,16,256]{2,1,0:T(8,128)(2,1)S(1)}, u32[]{:S(2)}, u32[]{:S(2)}) async-start(bf16[128,16,256]{2,1,0:T(8,128)(2,1)} %bitcast.17), calls=%async_computation | async-start | bytes 2097152 | tf_op jit(solution)/shard_map/all_to_all | solution.py:143
  76.9 16.8 %all-to-all-done = bf16[128,16,256]{2,1,0:T(8,128)(2,1)S(1)} async-done(((bf16[128,16,256]{2,1,0:T(8,128)(2,1)}), bf16[128,16,256]{2,1,0:T(8,128)(2,1)S(1)}, u32[]{:S(2)}, u32[]{:S(2)}) %all-to-all-start) | async-done | bytes 1048608 | tf_op jit(solution)/shard_map/all_to_all | solution.py:143
  93.7 4.6 %all-to-all-start.2 = ((s32[128,1,2]{2,1,0:T(1,128)}), s32[128,1,2]{2,1,0:T(1,128)S(1)}, u32[]{:S(2)}, u32[]{:S(2)}) async-start(s32[128,1,2]{2,1,0:T(1,128)} %bitcast.30), calls=%async_computation.2 | async-start | bytes 131072 | tf_op jit(solution)/shard_map/all_to_all | solution.py:178
  98.3 5.0 %multiply_convert_fusion.1 = bf16[2048,1024]{1,0:T(8,128)(2,1)} fusion(bf16[2048,256]{1,0:T(8,128)(2,1)S(1)} %bitcast.86, f32[1024]{0:T(1024)S(1)} %bitcast.100, bf16[1,256,1024]{2,1,0:T(8,128)(2,1)} %param.14), kind=kOutput, calls=%fused_computation.6 | convolution fusion | flops 1086324736 | bytes 5771264 | tf_op jit(solution)/shard_map/dot_general | solution.py:92
  103.3 8.7 %fusion.3 = bf16[2048,264]{0,1:T(8,128)(2,1)S(1)} fusion(f32[1024]{0:T(1024)S(1)} %bitcast.101, bf16[2048,1024]{1,0:T(8,128)(2,1)} %multiply_convert_fusion.1, bf16[1,1024,1024]{2,1,0:T(8,128)(2,1)S(1)} %copy-done, bf16[1,1024,264]{1,2,0:T(8,128)(2,1)} %param.18), kind=kOutput, calls=%fused_computation.9 | convolution fusion | flops 5415387136 | bytes 7917568 | tf_op jit(solution)/shard_map/dot_general | solution.py:97
  113.5 10.3 %all-to-all-start.1 = ((bf16[128,16,264]{2,1,0:T(8,128)(2,1)}), bf16[128,16,264]{2,1,0:T(8,128)(2,1)}, u32[]{:S(2)}, u32[]{:S(2)}) async-start(bf16[128,16,264]{2,1,0:T(8,128)(2,1)} %bitcast.80), calls=%async_computation.1 | async-start | bytes 3145728 | tf_op jit(solution)/shard_map/all_to_all | solution.py:153
  125.9 22.3 %all-to-all-done.1 = bf16[128,16,264]{2,1,0:T(8,128)(2,1)} async-done(((bf16[128,16,264]{2,1,0:T(8,128)(2,1)}), bf16[128,16,264]{2,1,0:T(8,128)(2,1)}, u32[]{:S(2)}, u32[]{:S(2)}) %all-to-all-start.1) | async-done | bytes 1081376 | tf_op jit(solution)/shard_map/all_to_all | solution.py:153
  148.2 6.5 %gather_fusion = bf16[1024,264]{1,0:T(8,128)(2,1)} fusion(bf16[2048,264]{1,0:T(8,128)(2,1)} %bitcast.25, s32[1024]{0:T(1024)S(1)} %broadcast_clamp_fusion), kind=kCustom, calls=%fused_computation | custom fusion | bytes 1085440 | tf_op jit(solution)/shard_map/gather | solution.py:154
  164.7 4.6 %all-to-all-start.3 = ((f32[128,2,128]{2,1,0:T(2,128)}), f32[128,2,128]{2,1,0:T(2,128)S(1)}, u32[]{:S(2)}, u32[]{:S(2)}) async-start(f32[128,2,128]{2,1,0:T(2,128)} %bitcast.35), calls=%async_computation.3 | async-start | bytes 262144 | tf_op jit(solution)/shard_map/all_to_all | solution.py:185
  171.8 7.4 %all-to-all-done.3 = f32[128,2,128]{2,1,0:T(2,128)S(1)} async-done(((f32[128,2,128]{2,1,0:T(2,128)}), f32[128,2,128]{2,1,0:T(2,128)S(1)}, u32[]{:S(2)}, u32[]{:S(2)}) %all-to-all-start.3) | async-done | bytes 131104 | tf_op jit(solution)/shard_map/all_to_all | solution.py:185
  (80 shorter events, 36.1 us)
Async XLA Ops:
  0.6 102.7 %copy-start = (bf16[1,1024,1024]{2,1,0:T(8,128)(2,1)S(1)}, bf16[1,1024,1024]{2,1,0:T(8,128)(2,1)}, u32[]{:S(2)}) copy-start(bf16[1,1024,1024]{2,1,0:T(8,128)(2,1)} %param.16) | copy-start | bytes 6291460
  0.6 3.3 %copy-start.1 = (f32[32,32,256]{2,1,0:T(8,128)S(1)}, f32[32,32,256]{2,1,0:T(8,128)}, u32[]{:S(2)}) copy-start(f32[32,32,256]{2,1,0:T(8,128)} %param.12) | copy-start | bytes 3145732
  3.9 5.6 %copy-start.7 = (f32[4,4,1,1]{1,0,3,2:T(4,128)S(1)}, f32[4,4,1,1]{1,0,3,2:T(4,128)}, u32[]{:S(2)}) copy-start(f32[4,4,1,1]{1,0,3,2:T(4,128)} %constant.74) | copy-start | bytes 196
  27.1 23.3 %collective-permute-start = (f32[1,32,256]{2,1,0:T(8,128)S(1)}, f32[1,32,256]{2,1,0:T(8,128)S(1)}, u32[]{:S(2)}, u32[]{:S(2)}) collective-permute-start(f32[1,32,256]{2,1,0:T(8,128)S(1)} %slice.57), channel_id=1, source_target_pairs={{0,32},{32,64},{64,96},{96,0},{1,33},{33,65},{65,97},{97,1},{2,34}... | collective-permute-start | bytes 98312 | tf_op jit(solution)/shard_map/ppermute | solution.py:24
  29.4 21.1 %collective-permute-start.1 = (f32[1,32,256]{2,1,0:T(8,128)S(1)}, f32[1,32,256]{2,1,0:T(8,128)S(1)}, u32[]{:S(2)}, u32[]{:S(2)}) collective-permute-start(f32[1,32,256]{2,1,0:T(8,128)S(1)} %slice.59), channel_id=1, source_target_pairs={{32,0},{64,32},{96,64},{0,96},{33,1},{65,33},{97,65},{1,97},{34,2}... | collective-permute-start | bytes 98312 | tf_op jit(solution)/shard_map/ppermute | solution.py:25
  42.3 3.2 %copy-start.6 = (s32[1024,1]{0,1:T(1,128)S(1)}, s32[1024,1]{0,1:T(1,128)}, u32[]{:S(2)}) copy-start(s32[1024,1]{0,1:T(1,128)} %param.13) | copy-start | bytes 12292
  45.9 0.8 copy-start.4
  46.7 1.7 copy-start.2
  46.7 1.7 copy-start.3
  50.5 3.8 %collective-permute-start.2 = (f32[34,1,256]{2,1,0:T(1,128)S(1)}, f32[34,1,256]{2,1,0:T(1,128)S(1)}, u32[]{:S(2)}, u32[]{:S(2)}) collective-permute-start(f32[34,1,256]{2,1,0:T(1,128)S(1)} %get-tuple-element.8), channel_id=1, source_target_pairs={{0,1},{1,2},{2,3},{3,4},{4,5},{5,6},{6,7},{7,8},{8,9},{9,10},{10,1... | collective-permute-start | bytes 104456 | tf_op jit(solution)/shard_map/ppermute | solution.py:24
  53.3 3.7 %collective-permute-start.3 = (f32[34,1,256]{2,1,0:T(1,128)S(1)}, f32[34,1,256]{2,1,0:T(1,128)S(1)}, u32[]{:S(2)}, u32[]{:S(2)}) collective-permute-start(f32[34,1,256]{2,1,0:T(1,128)S(1)} %get-tuple-element.9), channel_id=1, source_target_pairs={{1,0},{2,1},{3,2},{4,3},{5,4},{6,5},{7,6},{8,7},{9,8},{10,9},{11,1... | collective-permute-start | bytes 104456 | tf_op jit(solution)/shard_map/ppermute | solution.py:25
  59.2 15.4 %copy-start.8 = (s32[128,1]{0,1:T(1,128)S(1)}, s32[128,1]{0,1:T(1,128)}, u32[]{:S(2)}) copy-start(s32[128,1]{0,1:T(1,128)} %param.20) | copy-start | bytes 1540
  59.2 39.1 %copy-start.9 = (f32[1,1024]{1,0:T(1,128)S(1)}, f32[1,1024]{1,0:T(1,128)}, u32[]{:S(2)}) copy-start(f32[1,1024]{1,0:T(1,128)} %param.15) | copy-start | bytes 12292
  65.6 28.2 %all-to-all-start = ((bf16[128,16,256]{2,1,0:T(8,128)(2,1)}), bf16[128,16,256]{2,1,0:T(8,128)(2,1)S(1)}, u32[]{:S(2)}, u32[]{:S(2)}) async-start(bf16[128,16,256]{2,1,0:T(8,128)(2,1)} %bitcast.17), calls=%async_computation | async-start | bytes 2097152 | tf_op jit(solution)/shard_map/all_to_all | solution.py:143
  93.7 19.8 %all-to-all-start.2 = ((s32[128,1,2]{2,1,0:T(1,128)}), s32[128,1,2]{2,1,0:T(1,128)S(1)}, u32[]{:S(2)}, u32[]{:S(2)}) async-start(s32[128,1,2]{2,1,0:T(1,128)} %bitcast.30), calls=%async_computation.2 | async-start | bytes 131072 | tf_op jit(solution)/shard_map/all_to_all | solution.py:178
  98.3 5.0 %copy-start.10 = (f32[1,1024]{1,0:T(1,128)S(1)}, f32[1,1024]{1,0:T(1,128)}, u32[]{:S(2)}) copy-start(f32[1,1024]{1,0:T(1,128)} %param.17) | copy-start | bytes 12292
  113.5 10.3 %copy-start.5 = (f32[128,256]{1,0:T(8,128)S(1)}, f32[128,256]{1,0:T(8,128)}, u32[]{:S(2)}) copy-start(f32[128,256]{1,0:T(8,128)} %param.22) | copy-start | bytes 393220
  113.5 10.9 %copy-start.11 = (s32[128]{0:T(128)S(1)}, s32[128]{0:T(128)}, u32[]{:S(2)}) copy-start(s32[128]{0:T(128)} %param.19) | copy-start | bytes 1540
  113.5 34.7 %all-to-all-start.1 = ((bf16[128,16,264]{2,1,0:T(8,128)(2,1)}), bf16[128,16,264]{2,1,0:T(8,128)(2,1)}, u32[]{:S(2)}, u32[]{:S(2)}) async-start(bf16[128,16,264]{2,1,0:T(8,128)(2,1)} %bitcast.80), calls=%async_computation.1 | async-start | bytes 3145728 | tf_op jit(solution)/shard_map/all_to_all | solution.py:153
  164.7 14.6 %all-to-all-start.3 = ((f32[128,2,128]{2,1,0:T(2,128)}), f32[128,2,128]{2,1,0:T(2,128)S(1)}, u32[]{:S(2)}, u32[]{:S(2)}) async-start(f32[128,2,128]{2,1,0:T(2,128)} %bitcast.35), calls=%async_computation.3 | async-start | bytes 262144 | tf_op jit(solution)/shard_map/all_to_all | solution.py:185

commit v2 on v0

v2 whole, which is shorter than its diff:
```python
import math

import jax
import jax.numpy as jnp
import numpy as np
from jax import lax
from jax.experimental import pallas as pl
from jax.experimental.pallas import tpu as pltpu
from jax.sharding import PartitionSpec as P

LEV = 64
OB_DEV = 16
STEP_DT = 0.2
HIGHEST = lax.Precision.HIGHEST
AXES = ("gx", "gy")
F32 = jnp.float32
BF16 = jnp.bfloat16
MIB = 1 << 20


def derivative_table():
    root = 1.0 / math.sqrt(5.0)
    nodes = np.array([-1.0, -root, root, 1.0])
    table = np.zeros((4, 4))
    for row_index in range(4):
        for col_index in range(4):
            if row_index == col_index:
                table[row_index, col_index] = sum(
                    (
                        1.0 / (nodes[row_index] - nodes[other])
                        for other in range(4)
                        if other != row_index
                    )
                )
            else:
                weight_row = np.prod(
                    [nodes[row_index] - nodes[other] for other in range(4) if other != row_index]
                )
                weight_col = np.prod(
                    [nodes[col_index] - nodes[other] for other in range(4) if other != col_index]
                )
                table[row_index, col_index] = weight_row / (
                    weight_col * (nodes[row_index] - nodes[col_index])
                )
    return table


TABLE = [[float(np.float32(v)) for v in row] for row in derivative_table()]


def iota(shape, dim):
    return lax.broadcasted_iota(jnp.int32, shape, dim)


def dot(a, b, precision=None):
    return jnp.dot(a, b, preferred_element_type=F32, precision=precision)


def along_rows(line):
    rows, features = line.shape
    groups = line.reshape(rows // 8, 8, features)
    phase = iota((1, 8, features), 1) % 4
    total = None
    for offset in range(-3, 4):
        weight = jnp.zeros((1, 8, features), F32)
        for p in range(4):
            if 0 <= p + offset < 4:
                weight = jnp.where(phase == p, TABLE[p][p + offset], weight)
        moved = groups if offset == 0 else pltpu.roll(groups, (-offset) % 8, 1)
        total = weight * moved if total is None else total + weight * moved
    return total.reshape(rows, features)


def winds(line):
    pair = line[:, 128:]
    swapped = pltpu.roll(pair, LEV, 1)
    first = iota(pair.shape, 1) < LEV
    return jnp.where(first, pair, swapped), jnp.where(first, swapped, pair)


def advect(line, along_x, along_y):
    u, v = winds(line)
    return jnp.concatenate(
        [
            -(u * along_x[:, :128] + v * along_y[:, :128]),
            -(u * along_x[:, 128:] + v * along_y[:, 128:]),
        ],
        axis=1,
    )


def across(lines, i):
    total = TABLE[i][0] * lines[0]
    for j in range(1, 4):
        total = total + TABLE[i][j] * lines[j]
    return total


def smooth_rows(line):
    rows, features = line.shape
    row = iota((rows, features), 0)
    phase = row % 4
    before = jnp.where(row == 0, 0.0, pltpu.roll(line, 1, 0))
    after = jnp.where(row == rows - 1, 0.0, pltpu.roll(line, rows - 1, 0))
    return jnp.where(
        phase == 0,
        0.5 * (line + before),
        jnp.where(phase == 3, 0.5 * (line + after), line),
    )


def edges_kernel(state, x_low, x_high, y_low, y_high):
    size_x, size_y, _ = state.shape
    for out, base, i in ((x_low, 0, 0), (x_high, size_x - 4, 3)):
        lines = [state[base + j] for j in range(4)]
        out[...] = advect(lines[i], across(lines, i), along_rows(lines[i]))
    for out, base, i in ((y_low, 0, 0), (y_high, size_y - 4, 3)):
        lines = [state[:, base + j, :] for j in range(4)]
        out[...] = advect(lines[i], along_rows(lines[i]), across(lines, i))


def sides_kernel(y_low, y_high, x_before, x_after, partial, low, high):
    size, features = y_low.shape
    row = iota((size, features), 0)
    for out, line, y in ((low, y_low, 0), (high, y_high, size - 1)):
        extra = jnp.where(
            row == 0,
            0.5 * x_before[y : y + 1, :],
            jnp.where(row == size - 1, 0.5 * x_after[y : y + 1, :], 0.0),
        )
        out[...] = smooth_rows(line[...]) + extra


def local_kernel(state, token, partial, tend):
    size_x, size_y, features = state.shape
    tend[0] = jnp.zeros((size_y, features), F32)
    tend[size_x + 1] = jnp.zeros((size_y, features), F32)

    @pl.loop(0, size_x // 4)
    def _(e):
        lines = [state[4 * e + j] for j in range(4)]
        for i in range(4):
            tend[4 * e + i + 1] = advect(lines[i], across(lines, i), along_rows(lines[i]))

    @pl.loop(0, size_x // 4)
    def _(e):
        low = 4 * e + 1
        values = [
            0.5 * (tend[low] + tend[low - 1]),
            tend[low + 1],
            tend[low + 2],
            0.5 * (tend[low + 3] + tend[low + 4]),
        ]
        for i in range(4):
            partial[4 * e + i] = state[4 * e + i] + STEP_DT * smooth_rows(values[i])


def owner_ranks(owners):
    count = owners.shape[1]
    earlier = (iota((count, count), 0) < iota((count, count), 1)).astype(F32).astype(BF16)
    hot = (iota((128, count), 0) == owners).astype(F32)
    rank = jnp.sum(dot(hot.astype(BF16), earlier) * hot, axis=0, keepdims=True)
    return hot, rank.astype(jnp.int32)


def route_kernel(capacity, member_row, slot_row, hot_rows):
    columns = member_row.shape[1]
    earlier = (iota((128, 128), 0) < iota((128, 128), 1)).astype(F32).astype(BF16)
    seen = jnp.zeros((128, 1), F32)
    for b in range(columns // 128):
        part = slice(b * 128, (b + 1) * 128)
        members = member_row[:, part]
        hot = (iota((128, 128), 0) == members).astype(F32)
        count = dot(hot.astype(BF16), earlier) + seen
        rank = jnp.sum(count * hot, axis=0, keepdims=True).astype(jnp.int32)
        slots = members * capacity + rank
        slot_row[:, part] = slots
        seen = seen + jnp.sum(hot, axis=1, keepdims=True)
    step = 256
    slots = slot_row[...]
    for b in range(hot_rows.shape[0] // step):
        hot = iota((step, columns), 0) + b * step == slots
        hot_rows[b * step : (b + 1) * step, :] = hot.astype(F32).astype(BF16)


def add_outside(advanced, partial, x_before, x_after, y_before, y_after):
    size_x, size_y, _ = partial.shape
    advanced[...] = partial[...]
    half = 0.5 * STEP_DT
    advanced[0] = advanced[0] + half * smooth_rows(x_before[...])
    advanced[size_x - 1] = advanced[size_x - 1] + half * smooth_rows(x_after[...])
    advanced[:, 0, :] = advanced[:, 0, :] + half * y_before[...]
    advanced[:, size_y - 1, :] = advanced[:, size_y - 1, :] + half * y_after[...]


def pack_kernel(
    partial, x_before, x_after, y_before, y_after, hot_rows, send_out, advanced, send, sems
):
    size_x, size_y, features = partial.shape
    add_outside(advanced, partial, x_before, x_after, y_before, y_after)
    columns = advanced[...].reshape(size_x * size_y, features).astype(BF16)
    step = 256
    copies = []
    for b in range(send.shape[0] // step):
        part = slice(b * step, (b + 1) * step)
        send[part, :] = dot(hot_rows[part, :], columns).astype(BF16)
        copy = pltpu.make_async_copy(send.at[part], send_out.at[part], sems.at[b])
        copy.start()
        copies.append(copy)
    for copy in copies:
        copy.wait()


def as_column(row):
    wide = jnp.where(iota((128, 128), 0) == iota((128, 128), 1), row, 0)
    return jnp.sum(wide, axis=1, keepdims=True)


def prepare_kernel(capacity, element_row, weight, slot_row, token, places, tiled):
    count = element_row.shape[1]
    lane = iota((count, 128), 1)
    for c in range(16):
        part = weight[:, (c // 8) * 128 : (c // 8 + 1) * 128]
        part = jnp.where(lane // 16 == c % 8, part, 0.0)
        for distance in (64, 32, 16):
            part = part + pltpu.roll(part, distance, 1)
        tiled[c] = part

    columns = slot_row.shape[1]
    lane = iota((128, 128), 1)
    table = []
    for b in range(columns // 128):
        slots = as_column(slot_row[:, b * 128 : (b + 1) * 128])
        both = jnp.where(lane == 0, slots // capacity, jnp.where(lane == 1, slots % capacity, 0))
        table.append(both.astype(F32).astype(BF16))
    table = jnp.concatenate(table, axis=0)
    element = as_column(element_row[...])
    base = (element // 8) * 128 + (element % 8) * 4
    place = iota((count, columns), 1)
    slots = jnp.zeros((count, 128), F32)
    for c in range(16):
        hot = (place == base + (c // 4) * 32 + c % 4).astype(F32).astype(BF16)
        both = dot(hot, table)
        slots = jnp.where(lane == c, both[:, 0:1] * capacity + both[:, 1:2], slots)
    places[...] = slots.astype(jnp.int32)


def silu(x):
    half = 0.5 * x
    return half + half * jnp.tanh(half)


def first_kernel(rows, w_in, b_in, owner_row, block_row, out, blocks):
    owners = owner_row[...]
    hot, rank = owner_ranks(owners)
    values = block_row[...].astype(F32)
    lane = iota(blocks.shape, 1)
    first = jnp.sum(jnp.where(rank == 0, hot, 0.0) * values, axis=1, keepdims=True)
    second = jnp.sum(jnp.where(rank == 1, hot, 0.0) * values, axis=1, keepdims=True)
    blocks[...] = jnp.where(lane == 0, first, jnp.where(lane == 1, second, 0.0))

    step = 512
    for b in range(rows.shape[0] // step):
        part = slice(b * step, (b + 1) * step)
        out[part, :] = silu(dot(rows[part, :], w_in[0]) + b_in[...]).astype(BF16)


def second_kernel(first, w_mid, b_mid, w_out, w_flux, blocks, answer, token):
    step = 512
    sources = step // 16
    lane = iota((step, 128), 1)
    own = lane // 8 == iota((step, 128), 0) % 16
    line = iota((sources, 8, 128), 1)
    for b in range(first.shape[0] // step):
        hidden = dot(first[b * step : (b + 1) * step, :], w_mid[0])
        hidden = silu(hidden + b_mid[...]).astype(BF16)
        tends = dot(hidden, w_out[0, :, 0:256]).astype(BF16)
        part = slice(b * sources, (b + 1) * sources)
        answer[part, 0:16, :] = tends[:, :128].reshape(sources, 16, 128)
        answer[part, 16:32, :] = tends[:, 128:].reshape(sources, 16, 128)
        flux = jnp.where(own, dot(hidden, w_flux[...]), 0.0)
        flux = jnp.sum(flux.reshape(sources, 16, 128), axis=1, keepdims=True)
        names = blocks[part, :].reshape(sources, 1, 128)
        tail = jnp.where(line == 0, flux, jnp.where(line == 1, names, 0.0))
        answer[part, 32:40, :] = tail.astype(BF16)
    token[...] = blocks[0:8, :]


def contribution_kernel(capacity, answer, places, tiled, owner_row, send):
    flux = answer[:, 32:40, :].astype(F32)[:, 0, :].astype(BF16)
    spread = (iota((128, 128), 0) % 8 == iota((128, 128), 1) // 16).astype(F32).astype(BF16)
    lane = iota((128, 128), 1)
    total = None
    for c in range(16):
        slots = places[:, c : c + 1]
        pick = (lane == slots // capacity).astype(F32).astype(BF16)
        value = jnp.where(lane // 8 == slots % capacity, dot(pick, flux), 0.0)
        term = dot(value.astype(BF16), spread) * tiled[c]
        total = term if total is None else total + term
    owners = owner_row[...]
    _, rank = owner_ranks(owners)
    hot = (iota(send.shape, 0) == owners * 2 + rank).astype(F32)
    send[...] = dot(hot, total, HIGHEST)


def columns_kernel(
    answer,
    slot_row,
    partial,
    x_before,
    x_after,
    y_before,
    y_after,
    new_state,
    sums,
    rows,
    advanced,
):
    sources = answer.shape[0]
    slots = sources * 16
    size_x, size_y, features = partial.shape
    add_outside(advanced, partial, x_before, x_after, y_before, y_after)
    rows[:, 0:128] = answer[:, 0:16, :].reshape(slots, 128)
    rows[:, 128:256] = answer[:, 16:32, :].reshape(slots, 128)
    step = 128
    lines = step // size_y
    for b in range(size_x // lines):
        hot = iota((step, slots), 1) == as_column(slot_row[:, b * step : (b + 1) * step])
        tends = dot(hot.astype(F32).astype(BF16), rows[...])
        part = slice(b * lines, (b + 1) * lines)
        new_state[part] = advanced[part] + tends.reshape(lines, size_y, features)
    names = answer[:, 32:40, :].astype(F32)[:, 1, :]
    lane = iota((sources, 128), 1)
    for j in range(2):
        hot = (names[:, j : j + 1].astype(jnp.int32) == lane).astype(F32)
        sums[j] = jnp.transpose(hot)[:OB_DEV, :]


def ocean_kernel(received, sums, out):
    out[...] = dot(sums[0], received[:, 0, :], HIGHEST) + dot(sums[1], received[:, 1, :], HIGHEST)


def call(kernel, outs, *args, flops=0, nbytes=0, transcendentals=0, scratch=(), limit=16, spaces=None, out_spaces=None):
    return pl.pallas_call(
        kernel,
        out_shape=[jax.ShapeDtypeStruct(s, d) for s, d in outs],
        in_specs=[
            pl.BlockSpec(memory_space=(spaces or {}).get(i, pltpu.VMEM)) for i in range(len(args))
        ],
        out_specs=[
            pl.BlockSpec(memory_space=(out_spaces or {}).get(i, pltpu.VMEM))
            for i in range(len(outs))
        ],
        scratch_shapes=list(scratch),
        compiler_params=pltpu.CompilerParams(vmem_limit_bytes=limit * MIB),
        cost_estimate=pl.CostEstimate(
            flops=flops, bytes_accessed=nbytes, transcendentals=transcendentals
        ),
    )(*args)


def shift(value, axis, step):
    size = lax.axis_size(axis)
    return lax.ppermute(value, axis, [(i, (i + step) % size) for i in range(size)])


def exchange(value):
    return lax.all_to_all(value, AXES, split_axis=0, concat_axis=0, tiled=True)


def shards(
    state,
    group_member,
    w_in,
    bias_in,
    w_mid,
    bias_mid,
    w_out,
    intersection_element,
    ocean_owner,
    ocean_block,
    regrid_weight,
):
    size_x, size_y, features = state.shape
    devices = lax.axis_size("gx") * lax.axis_size("gy")
    columns = size_x * size_y
    capacity = 2 * columns // devices
    slots = devices * capacity
    count = intersection_element.shape[0]
    line = ((size_x, features), F32)

    x_low, x_high, y_low, y_high = call(
        edges_kernel,
        [line] * 4,
        state,
        nbytes=2 * MIB,
        flops=MIB,
    )
    x_before, x_after = shift(x_high, "gx", 1), shift(x_low, "gx", -1)

    def local(token):
        return call(
            local_kernel,
            [(state.shape, F32)],
            state,
            token,
            nbytes=8 * MIB,
            flops=64 * MIB,
            spaces={1: pl.ANY},
            scratch=[pltpu.VMEM((size_x + 2, size_y, features), F32)],
        )[0]

    partial = local(x_low)
    low, high = call(
        sides_kernel,
        [line] * 2,
        y_low,
        y_high,
        x_before,
        x_after,
        partial,
        spaces={4: pl.ANY},
    )
    y_before, y_after = shift(high, "gy", 1), shift(low, "gy", -1)
    slot_row, hot_rows = call(
        lambda *refs: route_kernel(capacity, *refs),
        [((1, columns), jnp.int32), ((slots, columns), BF16)],
        group_member.reshape(1, columns),
        nbytes=8 * MIB,
        flops=64 * MIB,
    )
    (send,) = call(
        pack_kernel,
        [((slots, features), BF16)],
        partial,
        x_before,
        x_after,
        y_before,
        y_after,
        hot_rows,
        nbytes=4 * MIB,
        flops=2 * slots * columns * features,
        out_spaces={0: pl.ANY},
        scratch=[
            pltpu.VMEM(state.shape, F32),
            pltpu.VMEM((slots, features), BF16),
            pltpu.SemaphoreType.DMA((8,)),
        ],
    )
    received = exchange(send.reshape(devices, capacity, features)).reshape(slots, features)

    w_flux = jnp.tile(w_out[0, :, features:], (1, 16))
    hidden = w_in.shape[2]
    owner_row = ocean_owner.reshape(1, count)
    first, blocks = call(
        first_kernel,
        [((slots, hidden), BF16), ((devices, 128), F32)],
        received,
        w_in,
        bias_in,
        owner_row,
        ocean_block.reshape(1, count),
        nbytes=6 * MIB,
        flops=2 * slots * features * hidden,
        transcendentals=slots * hidden,
    )
    answered, token = call(
        second_kernel,
        [((devices, 40, 128), BF16), ((8, 128), F32)],
        first,
        w_mid,
        bias_mid,
        w_out,
        w_flux,
        blocks,
        nbytes=8 * MIB,
        flops=2 * slots * hidden * (hidden + 384),
        transcendentals=slots * hidden,
        limit=20,
    )
    answer = exchange(answered)
    places, tiled = call(
        lambda *refs: prepare_kernel(capacity, *refs),
        [((count, 128), jnp.int32), ((16, count, 128), F32)],
        intersection_element.reshape(1, count),
        regrid_weight,
        slot_row,
        token,
        nbytes=12 * MIB,
        flops=2 * 16 * count * columns * 256,
    )
    (ocean_send,) = call(
        lambda *refs: contribution_kernel(capacity, *refs),
        [((2 * devices, 128), F32)],
        answer,
        places,
        tiled,
        owner_row,
        nbytes=4 * MIB,
        flops=2 * 2 * 2048 * 128 * 128,
    )
    ocean_got = exchange(ocean_send.reshape(devices, 2, 128))
    partial = local(ocean_send)
    new_state, sums = call(
        columns_kernel,
        [(state.shape, F32), ((2, OB_DEV, devices), F32)],
        answer,
        slot_row,
        partial,
        x_before,
        x_after,
        y_before,
        y_after,
        nbytes=12 * MIB,
        flops=2 * slots * columns * features,
        scratch=[pltpu.VMEM((slots, features), BF16), pltpu.VMEM(state.shape, F32)],
    )
    (ocean_total,) = call(
        ocean_kernel, [((OB_DEV, 128), F32)], ocean_got, sums, nbytes=MIB, flops=MIB
    )
    return (new_state, ocean_total)


def solution(mesh):
    return jax.shard_map(
        shards,
        mesh=mesh,
        in_specs=(
            P("gx", "gy", None),
            P(("gx", "gy"), None),
            P(("gx", "gy"), None, None),
            P(("gx", "gy"), None),
            P(("gx", "gy"), None, None),
            P(("gx", "gy"), None),
            P(("gx", "gy"), None, None),
            P(("gx", "gy")),
            P(("gx", "gy"), None),
            P(("gx", "gy")),
            P(("gx", "gy"), None),
        ),
        out_specs=(P("gx", "gy", None), P(("gx", "gy"), None)),
        check_vma=False,
    )
```

time: 803 us -> 101 us (0.13)
  waiting for transfers between devices: 654 us -> 46.1 us
  local copies, waits for them, and re-layouts: 53.6 us -> 1.84 us
  blocking collectives: 28 us -> 0 us
  Pallas kernels: 0 us -> 27.5 us
  matrix products: 21.4 us -> 0 us
  between operations: 14.3 us -> 0.92 us
  other arithmetic: 12.9 us -> 0 us
  starting transfers between devices: 12.4 us -> 24.3 us
    reduce_scatter x1 -> x0, waiting for transfers between devices: 626 us -> none  [shards(): lax.psum_scatter(dense_sum, ('gx', 'gy'), scatter_dimension=0, tiled=True)]
    all_to_all x1 -> x0, blocking collectives: 28 us -> none  [shards(): lax.all_to_all(send_buffer.reshape(devices, capacity, features), ('gx', '...]
    pallas_call x0 -> x12, Pallas kernels: none -> 27.5 us  [call(): pl.pallas_call(kernel, out_shape=[jax.ShapeDtypeStruct(s, d) for s, d in...]
    dot_general x5 -> x0, matrix products: 21.4 us -> none  [the longest x1 9.56 us: run_member(): jnp.dot(hidden_two, w_last, preferred_element_type=jnp.float32)]
    all_to_all x1 -> x3, waiting for transfers between devices: 23.8 us -> 41.5 us  [exchange(): return lax.all_to_all(value, AXES, split_axis=0, concat_axis=0, tiled=True)]
    reshape x10 -> x0, local copies, waits for them, and re-layouts: 15.5 us -> none  [the longest x2 5.77 us: element_tendency(): along_y.reshape(size_x, size_y, 4, levels)]
    mul x4 -> x0, local copies, waits for them, and re-layouts: 11.9 us -> none  [the longest x2 5.94 us: element_tendency(): wind_u * along_x.reshape(size_x, size_y, 4, levels)]
    all_to_all x1 -> x3, starting transfers between devices: 5.77 us -> 16.9 us  [exchange(): return lax.all_to_all(value, AXES, split_axis=0, concat_axis=0, tiled=True)]
  transfers between devices with their start and end apart: 6 -> 7, of which waited for: 4 -> 5; matrix products, arithmetic and copies ran while one was open for 3% -> 1% of each run, Pallas kernels for 0% -> 12%
where the time goes in v2:
time: 101 us
  waiting for transfers between devices  46.1 us (46%)
  Pallas kernels  27.5 us (27%)
  starting transfers between devices  24.3 us (24%)
  local copies, waits for them, and re-layouts  1.84 us (2%)
    all_to_all x3, waiting for transfers between devices, exchange(): return lax.all_to_all(value, AXES, split_axis=0, concat_axis=0, tiled=True)  41.5 us
    pallas_call x12, Pallas kernels, call(): pl.pallas_call(kernel, out_shape=[jax.ShapeDtypeStruct(s, d) for s, d in...  27.5 us
    all_to_all x3, starting transfers between devices, exchange(): return lax.all_to_all(value, AXES, split_axis=0, concat_axis=0, tiled=True)  16.9 us
    ppermute x4, starting transfers between devices, shift(): lax.ppermute(value, axis, [(i, (i + step) % size) for i in range(size)])  7.33 us
    ppermute x4, waiting for transfers between devices, shift(): lax.ppermute(value, axis, [(i, (i + step) % size) for i in range(size)])  4.61 us
  transfers between devices with their start and end apart: 7, of which 5 were waited for; matrix products, arithmetic and copies ran while one was open for 1% of the time, Pallas kernels for 12%

profile of v2, /device:TPU:1, one launch (start us, length us, event | category | flops | bytes accessed | tf_op | source)
XLA Modules:
  0.0 100.6 jit_solution(2929915057564885102)
XLA Ops:
  0.6 1.2 %copy-done = f32[32,32,256]{2,1,0:T(8,128)S(1)} copy-done((f32[32,32,256]{2,1,0:T(8,128)S(1)}, f32[32,32,256]{2,1,0:T(8,128)}, u32[]{:S(2)}) %copy-start) | copy-done | bytes 1048600
  1.9 0.3 shard_map.122
  2.1 3.6 %collective-permute-start.1 = (f32[32,256]{1,0:T(8,128)S(1)}, f32[32,256]{1,0:T(8,128)S(1)}, u32[]{:S(2)}, u32[]{:S(2)}) collective-permute-start(f32[32,256]{1,0:T(8,128)S(1)} %get-tuple-element.18.token), channel_id=1, source_target_pairs={{0,96},{32,0},{64,32},{96,64},{1,97},{33,1},{65,33},{97,65},{2,98}... | collective-permute-start | bytes 98312 | tf_op jit(solution)/shard_map/ppermute | solution.py:364
  5.7 1.7 %shard_map.123.partial = f32[32,32,256]{2,1,0:T(8,128)S(1)} custom-call(f32[32,32,256]{2,1,0:T(8,128)S(1)} %copy-done, f32[32,256]{1,0:T(8,128)S(1)} %get-tuple-element.18.token), custom_call_target="tpu_custom_call" | custom-call | flops 67108864 | bytes 8388608 | tf_op jit(solution)/shard_map/pallas_call | solution.py:344
  7.4 2.3 %collective-permute-done.x_before = f32[32,256]{1,0:T(8,128)S(1)} collective-permute-done((f32[32,256]{1,0:T(8,128)S(1)}, f32[32,256]{1,0:T(8,128)S(1)}, u32[]{:S(2)}, u32[]{:S(2)}) %collective-permute-start) | collective-permute-done | bytes 32800 | tf_op jit(solution)/shard_map/ppermute | solution.py:364
  9.8 3.7 %collective-permute-start.2 = (f32[32,256]{1,0:T(8,128)S(1)}, f32[32,256]{1,0:T(8,128)S(1)}, u32[]{:S(2)}, u32[]{:S(2)}) collective-permute-start(f32[32,256]{1,0:T(8,128)S(1)} %get-tuple-element.22), channel_id=1, source_target_pairs={{0,1},{1,2},{2,3},{3,4},{4,5},{5,6},{6,7},{7,8},{8,9},{9,10},{10,1... | collective-permute-start | bytes 98312 | tf_op jit(solution)/shard_map/ppermute | solution.py:364
  13.5 1.3 %shard_map.125 = (s32[1,1024]{1,0:T(1,128)S(1)}, bf16[2048,1024]{1,0:T(8,128)(2,1)S(1)}) custom-call(s32[1,1024]{1,0:T(1,128)S(1)} %bitcast.14), custom_call_target="tpu_custom_call" | custom-call | flops 67108864 | bytes 8388608 | tf_op jit(solution)/shard_map/pallas_call | solution.py:344
  14.8 2.3 %collective-permute-done.3.y_after = f32[32,256]{1,0:T(8,128)S(1)} collective-permute-done((f32[32,256]{1,0:T(8,128)S(1)}, f32[32,256]{1,0:T(8,128)S(1)}, u32[]{:S(2)}, u32[]{:S(2)}) %collective-permute-start.3) | collective-permute-done | bytes 32800 | tf_op jit(solution)/shard_map/ppermute | solution.py:364
  17.1 2.1 %shard_map.126 = bf16[2048,256]{1,0:T(8,128)(2,1)} custom-call(f32[32,32,256]{2,1,0:T(8,128)S(1)} %shard_map.123.partial, f32[32,256]{1,0:T(8,128)S(1)} %collective-permute-done.x_before, f32[32,256]{1,0:T(8,128)S(1)} %collective-permute-done.1.x_after, f32[32,256]{1,0:T(8,128)S(1)} %collective-permute-done.2.y_before, ...), custom_call_target="tpu_custom_call" | custom-call | flops 1073741824 | bytes 4194304 | tf_op jit(solution)/shard_map/pallas_call | solution.py:344
  19.3 7.4 %all-to-all-start = ((bf16[128,16,256]{2,1,0:T(8,128)(2,1)}), bf16[128,16,256]{2,1,0:T(8,128)(2,1)S(1)}, u32[]{:S(2)}, u32[]{:S(2)}) async-start(bf16[128,16,256]{2,1,0:T(8,128)(2,1)} %bitcast.1), calls=%async_computation | async-start | bytes 2097152 | tf_op jit(solution)/shard_map/all_to_all | solution.py:368
  26.7 0.4 copy.15.w_out
  27.1 0.2 copy.16.w_flux
  27.3 18.6 %all-to-all-done = bf16[128,16,256]{2,1,0:T(8,128)(2,1)S(1)} async-done(((bf16[128,16,256]{2,1,0:T(8,128)(2,1)}), bf16[128,16,256]{2,1,0:T(8,128)(2,1)S(1)}, u32[]{:S(2)}, u32[]{:S(2)}) %all-to-all-start) | async-done | bytes 1048608 | tf_op jit(solution)/shard_map/all_to_all | solution.py:368
  45.9 2.3 %shard_map.127 = (bf16[2048,1024]{1,0:T(8,128)(2,1)S(1)}, f32[128,128]{1,0:T(8,128)S(1)}) custom-call(bf16[2048,256]{1,0:T(8,128)(2,1)S(1)} %bitcast.11, bf16[1,256,1024]{2,1,0:T(8,128)(2,1)S(1)} %copy-done.8, f32[1,1024]{1,0:T(1,128)S(1)} %copy-done.11, s32[1,128]{1,0:T(1,128)S(1)} %bitcast.12, s32[1,128]{1,0:T(1,128)S(1)} %bitcast.15), custom_call_target="tpu_custom_call" | custom-call | flops 1073741824 | bytes 6291456 | tf_op jit(solution)/shard_map/pallas_call | solution.py:344
  48.2 8.2 %shard_map.128 = (bf16[128,40,128]{2,1,0:T(8,128)(2,1)}, f32[8,128]{1,0:T(8,128)S(1)}) custom-call(bf16[2048,1024]{1,0:T(8,128)(2,1)S(1)} %get-tuple-element.25.first, bf16[1,1024,1024]{2,1,0:T(8,128)(2,1)S(1)} %copy-done.7, f32[1,1024]{1,0:T(1,128)S(1)} %copy-done.12, bf16[1,1024,264]{2,1,0:T(8,128)(2,1)S(1)} %copy.15.w_out, ...), custom_call_target="tpu_custom_call" | custom-call | flops 5905580032 | bytes 8388608 | tf_op jit(solution)/shard_map/pallas_call | solution.py:344
  56.4 4.8 %all-to-all-start.1 = ((bf16[128,40,128]{2,1,0:T(8,128)(2,1)}), bf16[128,40,128]{2,1,0:T(8,128)(2,1)S(1)}, u32[]{:S(2)}, u32[]{:S(2)}) async-start(bf16[128,40,128]{2,1,0:T(8,128)(2,1)} %get-tuple-element.27), calls=%async_computation.1 | async-start | bytes 2621440 | tf_op jit(solution)/shard_map/all_to_all | solution.py:368
  61.2 4.9 %shard_map.129 = (s32[128,128]{1,0:T(8,128)S(1)}, f32[16,128,128]{2,1,0:T(8,128)S(1)}) custom-call(s32[1,128]{1,0:T(1,128)S(1)} %bitcast.16, f32[128,256]{1,0:T(8,128)S(1)} %copy-done.9, s32[1,1024]{1,0:T(1,128)S(1)} %get-tuple-element.28.refs_2_.slot_row, f32[8,128]{1,0:T(8,128)S(1)} %get-tuple-element.29.refs_3_), custom_call_target="tpu_custom_call" | custom-call | flops 1073741824 | bytes 12582912 | tf_op jit(solution)/shard_map/pallas_call | solution.py:344
  66.1 17.1 %all-to-all-done.1.refs_0_.answer = bf16[128,40,128]{2,1,0:T(8,128)(2,1)S(1)} async-done(((bf16[128,40,128]{2,1,0:T(8,128)(2,1)}), bf16[128,40,128]{2,1,0:T(8,128)(2,1)S(1)}, u32[]{:S(2)}, u32[]{:S(2)}) %all-to-all-start.1) | async-done | bytes 1310752 | tf_op jit(solution)/shard_map/all_to_all | solution.py:368
  83.2 1.8 %shard_map.130.token = f32[256,128]{1,0:T(8,128)} custom-call(bf16[128,40,128]{2,1,0:T(8,128)(2,1)S(1)} %all-to-all-done.1.refs_0_.answer, s32[128,128]{1,0:T(8,128)S(1)} %get-tuple-element.30.refs_1_, f32[16,128,128]{2,1,0:T(8,128)S(1)} %get-tuple-element.31.refs_2_, s32[1,128]{1,0:T(1,128)S(1)} %bitcast.13), custom_call_target="tpu_custom_call" | custom-call | flops 134217728 | bytes 4194304 | tf_op jit(solution)/shard_map/pallas_call | solution.py:344
  85.0 4.7 %all-to-all-start.2 = ((f32[128,2,128]{2,1,0:T(2,128)}), f32[128,2,128]{2,1,0:T(2,128)S(1)}, u32[]{:S(2)}, u32[]{:S(2)}) async-start(f32[128,2,128]{2,1,0:T(2,128)} %bitcast.8), calls=%async_computation.2 | async-start | bytes 262144 | tf_op jit(solution)/shard_map/all_to_all | solution.py:368
  89.7 1.7 %shard_map.131.partial = f32[32,32,256]{2,1,0:T(8,128)S(1)} custom-call(f32[32,32,256]{2,1,0:T(8,128)S(1)} %copy-done.1, f32[256,128]{1,0:T(8,128)} %shard_map.130.token), custom_call_target="tpu_custom_call" | custom-call | flops 67108864 | bytes 8388608 | tf_op jit(solution)/shard_map/pallas_call | solution.py:344
  91.4 2.5 %shard_map.132 = (f32[32,32,256]{2,1,0:T(8,128)}, f32[2,16,128]{2,1,0:T(8,128)S(1)}) custom-call(bf16[128,40,128]{2,1,0:T(8,128)(2,1)S(1)} %all-to-all-done.1.refs_0_.answer, s32[1,1024]{1,0:T(1,128)S(1)} %get-tuple-element.28.refs_2_.slot_row, f32[32,32,256]{2,1,0:T(8,128)S(1)} %shard_map.131.partial, f32[32,256]{1,0:T(8,128)S(1)} %collective-permute-done.x_before, ...), custom_call_target="tpu_custom_call" | custom-call | flops 1073741824 | bytes 12582912 | tf_op jit(solution)/shard_map/pallas_call | solution.py:344
  93.9 5.8 %all-to-all-done.2.received = f32[128,2,128]{2,1,0:T(2,128)S(1)} async-done(((f32[128,2,128]{2,1,0:T(2,128)}), f32[128,2,128]{2,1,0:T(2,128)S(1)}, u32[]{:S(2)}, u32[]{:S(2)}) %all-to-all-start.2) | async-done | bytes 131104 | tf_op jit(solution)/shard_map/all_to_all | solution.py:368
  99.7 0.9 shard_map.133
  (38 shorter events, 0.1 us)
Async XLA Ops:
  0.6 1.2 %copy-start = (f32[32,32,256]{2,1,0:T(8,128)S(1)}, f32[32,32,256]{2,1,0:T(8,128)}, u32[]{:S(2)}) copy-start(f32[32,32,256]{2,1,0:T(8,128)} %state.5) | copy-start | bytes 3145732
  1.9 11.6 %copy-start.10 = (s32[1024,1]{0,1:T(1,128)S(1)}, s32[1024,1]{0,1:T(1,128)}, u32[]{:S(2)}) copy-start(s32[1024,1]{0,1:T(1,128)} %param.12) | copy-start | bytes 12292
  2.1 5.3 %collective-permute-start.1 = (f32[32,256]{1,0:T(8,128)S(1)}, f32[32,256]{1,0:T(8,128)S(1)}, u32[]{:S(2)}, u32[]{:S(2)}) collective-permute-start(f32[32,256]{1,0:T(8,128)S(1)} %get-tuple-element.18.token), channel_id=1, source_target_pairs={{0,96},{32,0},{64,32},{96,64},{1,97},{33,1},{65,33},{97,65},{2,98}... | collective-permute-start | bytes 98312 | tf_op jit(solution)/shard_map/ppermute | solution.py:364
  5.7 4.0 %collective-permute-start = (f32[32,256]{1,0:T(8,128)S(1)}, f32[32,256]{1,0:T(8,128)S(1)}, u32[]{:S(2)}, u32[]{:S(2)}) collective-permute-start(f32[32,256]{1,0:T(8,128)S(1)} %get-tuple-element.19), channel_id=1, source_target_pairs={{0,32},{32,64},{64,96},{96,0},{1,33},{33,65},{65,97},{97,1},{2,34}... | collective-permute-start | bytes 98312 | tf_op jit(solution)/shard_map/ppermute | solution.py:364
  9.8 5.0 %collective-permute-start.2 = (f32[32,256]{1,0:T(8,128)S(1)}, f32[32,256]{1,0:T(8,128)S(1)}, u32[]{:S(2)}, u32[]{:S(2)}) collective-permute-start(f32[32,256]{1,0:T(8,128)S(1)} %get-tuple-element.22), channel_id=1, source_target_pairs={{0,1},{1,2},{2,3},{3,4},{4,5},{5,6},{6,7},{7,8},{8,9},{9,10},{10,1... | collective-permute-start | bytes 98312 | tf_op jit(solution)/shard_map/ppermute | solution.py:364
  13.5 3.6 %collective-permute-start.3 = (f32[32,256]{1,0:T(8,128)S(1)}, f32[32,256]{1,0:T(8,128)S(1)}, u32[]{:S(2)}, u32[]{:S(2)}) collective-permute-start(f32[32,256]{1,0:T(8,128)S(1)} %get-tuple-element.23), channel_id=1, source_target_pairs={{0,31},{1,0},{2,1},{3,2},{4,3},{5,4},{6,5},{7,6},{8,7},{9,8},{10,9... | collective-permute-start | bytes 98312 | tf_op jit(solution)/shard_map/ppermute | solution.py:364
  14.8 4.4 %copy-start.2 = (f32[32,256]{1,0:T(8,128)}, f32[32,256]{1,0:T(8,128)S(1)}, u32[]{:S(2)}) copy-start(f32[32,256]{1,0:T(8,128)S(1)} %collective-permute-done.2.y_before) | copy-start | bytes 98308
  17.1 2.1 %copy-start.4 = (f32[32,256]{1,0:T(8,128)}, f32[32,256]{1,0:T(8,128)S(1)}, u32[]{:S(2)}) copy-start(f32[32,256]{1,0:T(8,128)S(1)} %collective-permute-done.3.y_after) | copy-start | bytes 98308
  19.2 7.5 %copy-start.15 = (bf16[1,1024,264]{1,2,0:T(8,128)(2,1)S(1)}, bf16[1,1024,264]{1,2,0:T(8,128)(2,1)}, u32[]{:S(2)}) copy-start(bf16[1,1024,264]{1,2,0:T(8,128)(2,1)} %param.17) | copy-start | bytes 1622020
  19.2 26.7 %copy-start.6 = (s32[128,1]{0,1:T(1,128)S(1)}, s32[128,1]{0,1:T(1,128)}, u32[]{:S(2)}) copy-start(s32[128,1]{0,1:T(1,128)} %param.19) | copy-start | bytes 1540
  19.2 26.7 %copy-start.8 = (bf16[1,256,1024]{2,1,0:T(8,128)(2,1)S(1)}, bf16[1,256,1024]{2,1,0:T(8,128)(2,1)}, u32[]{:S(2)}) copy-start(bf16[1,256,1024]{2,1,0:T(8,128)(2,1)} %w_in.1) | copy-start | bytes 1572868
  19.2 26.6 %copy-start.11 = (f32[1,1024]{1,0:T(1,128)S(1)}, f32[1,1024]{1,0:T(1,128)}, u32[]{:S(2)}) copy-start(f32[1,1024]{1,0:T(1,128)} %b_in.1) | copy-start | bytes 12292
  19.3 26.6 %copy-start.13 = (s32[128]{0:T(128)S(1)}, s32[128]{0:T(128)}, u32[]{:S(2)}) copy-start(s32[128]{0:T(128)} %param.20) | copy-start | bytes 1540
  19.3 26.6 %all-to-all-start = ((bf16[128,16,256]{2,1,0:T(8,128)(2,1)}), bf16[128,16,256]{2,1,0:T(8,128)(2,1)S(1)}, u32[]{:S(2)}, u32[]{:S(2)}) async-start(bf16[128,16,256]{2,1,0:T(8,128)(2,1)} %bitcast.1), calls=%async_computation | async-start | bytes 2097152 | tf_op jit(solution)/shard_map/all_to_all | solution.py:368
  27.3 20.9 %copy-start.12 = (f32[1,1024]{1,0:T(1,128)S(1)}, f32[1,1024]{1,0:T(1,128)}, u32[]{:S(2)}) copy-start(f32[1,1024]{1,0:T(1,128)} %b_mid.1) | copy-start | bytes 12292
  45.9 2.3 %copy-start.7 = (bf16[1,1024,1024]{2,1,0:T(8,128)(2,1)S(1)}, bf16[1,1024,1024]{2,1,0:T(8,128)(2,1)}, u32[]{:S(2)}) copy-start(bf16[1,1024,1024]{2,1,0:T(8,128)(2,1)} %w_mid.1) | copy-start | bytes 6291460
  56.4 4.8 %copy-start.9 = (f32[128,256]{1,0:T(8,128)S(1)}, f32[128,256]{1,0:T(8,128)}, u32[]{:S(2)}) copy-start(f32[128,256]{1,0:T(8,128)} %refs_1_.1) | copy-start | bytes 393220
  56.4 4.8 %copy-start.14 = (s32[128]{0:T(128)S(1)}, s32[128]{0:T(128)}, u32[]{:S(2)}) copy-start(s32[128]{0:T(128)} %param.18) | copy-start | bytes 1540
  56.4 26.8 %all-to-all-start.1 = ((bf16[128,40,128]{2,1,0:T(8,128)(2,1)}), bf16[128,40,128]{2,1,0:T(8,128)(2,1)S(1)}, u32[]{:S(2)}, u32[]{:S(2)}) async-start(bf16[128,40,128]{2,1,0:T(8,128)(2,1)} %get-tuple-element.27), calls=%async_computation.1 | async-start | bytes 2621440 | tf_op jit(solution)/shard_map/all_to_all | solution.py:368
  66.1 23.7 %copy-start.1 = (f32[32,32,256]{2,1,0:T(8,128)S(1)}, f32[32,32,256]{2,1,0:T(8,128)}, u32[]{:S(2)}) copy-start(f32[32,32,256]{2,1,0:T(8,128)} %state.5) | copy-start | bytes 3145732
  85.0 6.4 %copy-start.3 = (f32[32,256]{1,0:T(8,128)S(1)}, f32[32,256]{1,0:T(8,128)}, u32[]{:S(2)}) copy-start(f32[32,256]{1,0:T(8,128)} %copy-done.2) | copy-start | bytes 98308
  85.0 6.4 %copy-start.5 = (f32[32,256]{1,0:T(8,128)S(1)}, f32[32,256]{1,0:T(8,128)}, u32[]{:S(2)}) copy-start(f32[32,256]{1,0:T(8,128)} %copy-done.4) | copy-start | bytes 98308
  85.0 14.7 %all-to-all-start.2 = ((f32[128,2,128]{2,1,0:T(2,128)}), f32[128,2,128]{2,1,0:T(2,128)S(1)}, u32[]{:S(2)}, u32[]{:S(2)}) async-start(f32[128,2,128]{2,1,0:T(2,128)} %bitcast.8), calls=%async_computation.2 | async-start | bytes 262144 | tf_op jit(solution)/shard_map/all_to_all | solution.py:368

commit v3 on v2

--- a/solution.py
+++ b/solution.py
@@ -119,7 +119,7 @@
         out[...] = advect(lines[i], along_rows(lines[i]), across(lines, i))
 
 
-def sides_kernel(y_low, y_high, x_before, x_after, partial, low, high):
+def sides_kernel(y_low, y_high, x_before, x_after, partial, slot_row, low, high):
     size, features = y_low.shape
     row = iota((size, features), 0)
     for out, line, y in ((low, y_low, 0), (high, y_high, size - 1)):
@@ -163,8 +163,9 @@
     return hot, rank.astype(jnp.int32)
 
 
-def route_kernel(capacity, member_row, slot_row, hot_rows):
+def route_kernel(capacity, size_y, member_row, slot_row, hot_rows, hot_sides):
     columns = member_row.shape[1]
+    size_x = columns // size_y
     earlier = (iota((128, 128), 0) < iota((128, 128), 1)).astype(F32).astype(BF16)
     seen = jnp.zeros((128, 1), F32)
     for b in range(columns // 128):
@@ -173,37 +174,63 @@
         hot = (iota((128, 128), 0) == members).astype(F32)
         count = dot(hot.astype(BF16), earlier) + seen
         rank = jnp.sum(count * hot, axis=0, keepdims=True).astype(jnp.int32)
-        slots = members * capacity + rank
-        slot_row[:, part] = slots
+        slot_row[:, part] = members * capacity + rank
         seen = seen + jnp.sum(hot, axis=1, keepdims=True)
     step = 256
     slots = slot_row[...]
     for b in range(hot_rows.shape[0] // step):
         hot = iota((step, columns), 0) + b * step == slots
         hot_rows[b * step : (b + 1) * step, :] = hot.astype(F32).astype(BF16)
-
-
-def add_outside(advanced, partial, x_before, x_after, y_before, y_after):
-    size_x, size_y, _ = partial.shape
+    lane = iota((columns, 128), 1)
+    place = (lane % size_x) * size_y + (lane // size_x) * (size_y - 1)
+    choose = ((iota((columns, 128), 0) == place) & (lane < 2 * size_x)).astype(F32).astype(BF16)
+    row = iota((8, columns), 0)
+    both = jnp.where(row == 0, slots // capacity, jnp.where(row == 1, slots % capacity, 0))
+    both = dot(both.astype(F32).astype(BF16), choose).astype(jnp.int32)
+    side = both[0:1, :] * capacity + both[1:2, :]
+    side = jnp.where(iota((1, 128), 1) < 2 * size_x, side, -1)
+    for b in range(hot_sides.shape[0] // step):
+        hot = iota((step, 128), 0) + b * step == side
+        hot_sides[b * step : (b + 1) * step, :] = hot.astype(F32).astype(BF16)
+
+
+def add_before_after(advanced, partial, x_before, x_after):
+    size_x, _, _ = partial.shape
     advanced[...] = partial[...]
     half = 0.5 * STEP_DT
     advanced[0] = advanced[0] + half * smooth_rows(x_before[...])
     advanced[size_x - 1] = advanced[size_x - 1] + half * smooth_rows(x_after[...])
-    advanced[:, 0, :] = advanced[:, 0, :] + half * y_before[...]
-    advanced[:, size_y - 1, :] = advanced[:, size_y - 1, :] + half * y_after[...]
-
-
-def pack_kernel(
-    partial, x_before, x_after, y_before, y_after, hot_rows, send_out, advanced, send, sems
-):
+
+
+def inner_kernel(partial, x_before, x_after, hot_rows, send, sides, advanced):
     size_x, size_y, features = partial.shape
-    add_outside(advanced, partial, x_before, x_after, y_before, y_after)
+    add_before_after(advanced, partial, x_before, x_after)
+    for i, y in enumerate((0, size_y - 1)):
+        sides[i * size_x : (i + 1) * size_x, :] = advanced[:, y, :]
+        advanced[:, y, :] = jnp.zeros((size_x, features), F32)
     columns = advanced[...].reshape(size_x * size_y, features).astype(BF16)
     step = 256
-    copies = []
     for b in range(send.shape[0] // step):
         part = slice(b * step, (b + 1) * step)
         send[part, :] = dot(hot_rows[part, :], columns).astype(BF16)
+
+
+def pack_kernel(inner, sides, y_before, y_after, hot_sides, send_out, send, sems):
+    half = 0.5 * STEP_DT
+    size, features = y_before.shape
+    columns = jnp.concatenate(
+        [
+            sides[0:size, :] + half * y_before[...],
+            sides[size : 2 * size, :] + half * y_after[...],
+            jnp.zeros((128 - 2 * size, features), F32),
+        ],
+        axis=0,
+    ).astype(BF16)
+    step = send.shape[0] // sems.shape[0]
+    copies = []
+    for b in range(sems.shape[0]):
+        part = slice(b * step, (b + 1) * step)
+        send[part, :] = inner[part, :] + dot(hot_sides[part, :], columns).astype(BF16)
         copy = pltpu.make_async_copy(send.at[part], send_out.at[part], sems.at[b])
         copy.start()
         copies.append(copy)
@@ -245,12 +272,11 @@
     places[...] = slots.astype(jnp.int32)
 
 
-def silu(x):
-    half = 0.5 * x
+def silu_of_half(half):
     return half + half * jnp.tanh(half)
 
 
-def first_kernel(rows, w_in, b_in, owner_row, block_row, out, blocks):
+def first_kernel(rows, w_in, b_in, owner_row, block_row, out, blocks, w_half):
     owners = owner_row[...]
     hot, rank = owner_ranks(owners)
     values = block_row[...].astype(F32)
@@ -259,31 +285,41 @@
     second = jnp.sum(jnp.where(rank == 1, hot, 0.0) * values, axis=1, keepdims=True)
     blocks[...] = jnp.where(lane == 0, first, jnp.where(lane == 1, second, 0.0))
 
+    w_half[...] = w_in[0] * jnp.asarray(0.5, BF16)
+    b_half = 0.5 * b_in[...]
     step = 512
     for b in range(rows.shape[0] // step):
         part = slice(b * step, (b + 1) * step)
-        out[part, :] = silu(dot(rows[part, :], w_in[0]) + b_in[...]).astype(BF16)
-
-
-def second_kernel(first, w_mid, b_mid, w_out, w_flux, blocks, answer, token):
-    step = 512
+        out[part, :] = silu_of_half(dot(rows[part, :], w_half[...]) + b_half).astype(BF16)
+
+
+def second_kernel(first, w_mid, b_mid, w_out, w_flux, blocks, answer, token, w_half, out, sems):
+    step = first.shape[0] // sems.shape[0]
     sources = step // 16
     lane = iota((step, 128), 1)
     own = lane // 8 == iota((step, 128), 0) % 16
     line = iota((sources, 8, 128), 1)
-    for b in range(first.shape[0] // step):
-        hidden = dot(first[b * step : (b + 1) * step, :], w_mid[0])
-        hidden = silu(hidden + b_mid[...]).astype(BF16)
+    w_half[...] = w_mid[0] * jnp.asarray(0.5, BF16)
+    b_half = 0.5 * b_mid[...]
+    copies = []
+    for b in range(sems.shape[0]):
+        hidden = dot(first[b * step : (b + 1) * step, :], w_half[...])
+        hidden = silu_of_half(hidden + b_half).astype(BF16)
         tends = dot(hidden, w_out[0, :, 0:256]).astype(BF16)
         part = slice(b * sources, (b + 1) * sources)
-        answer[part, 0:16, :] = tends[:, :128].reshape(sources, 16, 128)
-        answer[part, 16:32, :] = tends[:, 128:].reshape(sources, 16, 128)
+        out[part, 0:16, :] = tends[:, :128].reshape(sources, 16, 128)
+        out[part, 16:32, :] = tends[:, 128:].reshape(sources, 16, 128)
         flux = jnp.where(own, dot(hidden, w_flux[...]), 0.0)
         flux = jnp.sum(flux.reshape(sources, 16, 128), axis=1, keepdims=True)
         names = blocks[part, :].reshape(sources, 1, 128)
         tail = jnp.where(line == 0, flux, jnp.where(line == 1, names, 0.0))
-        answer[part, 32:40, :] = tail.astype(BF16)
+        out[part, 32:40, :] = tail.astype(BF16)
+        copy = pltpu.make_async_copy(out.at[part], answer.at[part], sems.at[b])
+        copy.start()
+        copies.append(copy)
     token[...] = blocks[0:8, :]
+    for copy in copies:
+        copy.wait()
 
 
 def contribution_kernel(capacity, answer, places, tiled, owner_row, send):
@@ -319,7 +355,10 @@
     sources = answer.shape[0]
     slots = sources * 16
     size_x, size_y, features = partial.shape
-    add_outside(advanced, partial, x_before, x_after, y_before, y_after)
+    add_before_after(advanced, partial, x_before, x_after)
+    half = 0.5 * STEP_DT
+    advanced[:, 0, :] = advanced[:, 0, :] + half * y_before[...]
+    advanced[:, size_y - 1, :] = advanced[:, size_y - 1, :] + half * y_after[...]
     rows[:, 0:128] = answer[:, 0:16, :].reshape(slots, 128)
     rows[:, 128:256] = answer[:, 16:32, :].reshape(slots, 128)
     step = 128
@@ -411,6 +450,13 @@
         )[0]
 
     partial = local(x_low)
+    slot_row, hot_rows, hot_sides = call(
+        lambda *refs: route_kernel(capacity, size_y, *refs),
+        [((1, columns), jnp.int32), ((slots, columns), BF16), ((slots, 128), BF16)],
+        group_member.reshape(1, columns),
+        nbytes=8 * MIB,
+        flops=64 * MIB,
+    )
     low, high = call(
         sides_kernel,
         [line] * 2,
@@ -419,33 +465,33 @@
         x_before,
         x_after,
         partial,
-        spaces={4: pl.ANY},
+        slot_row,
+        spaces={4: pl.ANY, 5: pl.ANY},
     )
     y_before, y_after = shift(high, "gy", 1), shift(low, "gy", -1)
-    slot_row, hot_rows = call(
-        lambda *refs: route_kernel(capacity, *refs),
-        [((1, columns), jnp.int32), ((slots, columns), BF16)],
-        group_member.reshape(1, columns),
+    inner, sides = call(
+        inner_kernel,
+        [((slots, features), BF16), ((2 * size_x, features), F32)],
+        partial,
+        x_before,
+        x_after,
+        hot_rows,
         nbytes=8 * MIB,
-        flops=64 * MIB,
+        flops=2 * slots * columns * features,
+        scratch=[pltpu.VMEM(state.shape, F32)],
     )
     (send,) = call(
         pack_kernel,
         [((slots, features), BF16)],
-        partial,
-        x_before,
-        x_after,
+        inner,
+        sides,
         y_before,
         y_after,
-        hot_rows,
+        hot_sides,
         nbytes=4 * MIB,
-        flops=2 * slots * columns * features,
+        flops=2 * slots * 128 * features,
         out_spaces={0: pl.ANY},
-        scratch=[
-            pltpu.VMEM(state.shape, F32),
-            pltpu.VMEM((slots, features), BF16),
-            pltpu.SemaphoreType.DMA((8,)),
-        ],
+        scratch=[pltpu.VMEM((slots, features), BF16), pltpu.SemaphoreType.DMA((4,))],
     )
     received = exchange(send.reshape(devices, capacity, features)).reshape(slots, features)
 
@@ -463,6 +509,7 @@
         nbytes=6 * MIB,
         flops=2 * slots * features * hidden,
         transcendentals=slots * hidden,
+        scratch=[pltpu.VMEM((features, hidden), BF16)],
     )
     answered, token = call(
         second_kernel,
@@ -476,7 +523,13 @@
         nbytes=8 * MIB,
         flops=2 * slots * hidden * (hidden + 384),
         transcendentals=slots * hidden,
-        limit=20,
+        limit=24,
+        out_spaces={0: pl.ANY},
+        scratch=[
+            pltpu.VMEM((hidden, hidden), BF16),
+            pltpu.VMEM((devices, 40, 128), BF16),
+            pltpu.SemaphoreType.DMA((4,)),
+        ],
     )
     answer = exchange(answered)
     places, tiled = call(

time: 101 us -> 99.5 us (0.985)
  waiting for transfers between devices: 46.1 us -> 44.7 us
    ppermute x4, waiting for transfers between devices: 4.61 us -> 3.2 us  [shift(): lax.ppermute(value, axis, [(i, (i + step) % size) for i in range(size)])]
    pallas_call x12 -> x13, Pallas kernels: 27.5 us -> 26.5 us  [call(): pl.pallas_call(kernel, out_shape=[jax.ShapeDtypeStruct(s, d) for s, d in...]
  transfers between devices with their start and end apart: 7 -> 7, of which waited for: 5 -> 5; matrix products, arithmetic and copies ran while one was open for 1% -> 1% of each run, Pallas kernels for 12% -> 13%
where the time goes in v3:
time: 99.5 us; the launch traced here: 99.1 us
  waiting for transfers between devices  44.7 us (45%)
  Pallas kernels  26.5 us (27%)
  starting transfers between devices  25.1 us (25%)
  local copies, waits for them, and re-layouts  1.93 us (2%)
    all_to_all x3, waiting for transfers between devices, exchange(): return lax.all_to_all(value, AXES, split_axis=0, concat_axis=0, tiled=True)  41.5 us
    pallas_call x13, Pallas kernels, call(): pl.pallas_call(kernel, out_shape=[jax.ShapeDtypeStruct(s, d) for s, d in...  26.5 us
    all_to_all x3, starting transfers between devices, exchange(): return lax.all_to_all(value, AXES, split_axis=0, concat_axis=0, tiled=True)  17.7 us
    ppermute x4, starting transfers between devices, shift(): lax.ppermute(value, axis, [(i, (i + step) % size) for i in range(size)])  7.33 us
    ppermute x4, waiting for transfers between devices, shift(): lax.ppermute(value, axis, [(i, (i + step) % size) for i in range(size)])  3.2 us
  transfers between devices with their start and end apart: 7, of which 5 were waited for; matrix products, arithmetic and copies ran while one was open for 1% of the time, Pallas kernels for 13%

profile of v3, /device:TPU:1, one launch (start us, length us, event | category | flops | bytes accessed | tf_op | source)
XLA Modules:
  0.0 99.1 jit_solution(2999329625427306509)
XLA Ops:
  0.6 1.2 %copy-done = f32[32,32,256]{2,1,0:T(8,128)S(1)} copy-done((f32[32,32,256]{2,1,0:T(8,128)S(1)}, f32[32,32,256]{2,1,0:T(8,128)}, u32[]{:S(2)}) %copy-start) | copy-done | bytes 1048600
  1.9 0.3 shard_map.122
  2.1 3.6 %collective-permute-start.1 = (f32[32,256]{1,0:T(8,128)S(1)}, f32[32,256]{1,0:T(8,128)S(1)}, u32[]{:S(2)}, u32[]{:S(2)}) collective-permute-start(f32[32,256]{1,0:T(8,128)S(1)} %get-tuple-element.21.token), channel_id=1, source_target_pairs={{0,96},{32,0},{64,32},{96,64},{1,97},{33,1},{65,33},{97,65},{2,98}... | collective-permute-start | bytes 98312 | tf_op jit(solution)/shard_map/ppermute | solution.py:403
  5.7 1.7 %shard_map.123.partial = f32[32,32,256]{2,1,0:T(8,128)S(1)} custom-call(f32[32,32,256]{2,1,0:T(8,128)S(1)} %copy-done, f32[32,256]{1,0:T(8,128)S(1)} %get-tuple-element.21.token), custom_call_target="tpu_custom_call" | custom-call | flops 67108864 | bytes 8388608 | tf_op jit(solution)/shard_map/pallas_call | solution.py:383
  7.4 1.4 %shard_map.124 = (s32[1,1024]{1,0:T(1,128)S(1)}, bf16[2048,1024]{1,0:T(8,128)(2,1)S(1)}, bf16[2048,128]{1,0:T(8,128)(2,1)S(1)}) custom-call(s32[1,1024]{1,0:T(1,128)S(1)} %bitcast.14), custom_call_target="tpu_custom_call" | custom-call | flops 67108864 | bytes 8388608 | tf_op jit(solution)/shard_map/pallas_call | solution.py:383
  8.8 0.9 collective-permute-done.x_before
  9.8 3.7 %collective-permute-start.2 = (f32[32,256]{1,0:T(8,128)S(1)}, f32[32,256]{1,0:T(8,128)S(1)}, u32[]{:S(2)}, u32[]{:S(2)}) collective-permute-start(f32[32,256]{1,0:T(8,128)S(1)} %get-tuple-element.29), channel_id=1, source_target_pairs={{0,1},{1,2},{2,3},{3,4},{4,5},{5,6},{6,7},{7,8},{8,9},{9,10},{10,1... | collective-permute-start | bytes 98312 | tf_op jit(solution)/shard_map/ppermute | solution.py:403
  13.5 1.3 %shard_map.125 = (bf16[2048,256]{1,0:T(8,128)(2,1)S(1)}, f32[64,256]{1,0:T(8,128)S(1)}) custom-call(f32[32,32,256]{2,1,0:T(8,128)S(1)} %shard_map.123.partial, f32[32,256]{1,0:T(8,128)S(1)} %collective-permute-done.x_before, f32[32,256]{1,0:T(8,128)S(1)} %collective-permute-done.1.x_after, bf16[2048,1024]{1,0:T(8,128)(2,1)S(1)} %get-tuple-element.23.hot_rows), custom_call_target="tpu_custom_call" | custom-call | flops 1073741824 | bytes 8388608 | tf_op jit(solution)/shard_map/pallas_call | solution.py:383
  14.8 2.3 %collective-permute-done.3.y_after = f32[32,256]{1,0:T(8,128)S(1)} collective-permute-done((f32[32,256]{1,0:T(8,128)S(1)}, f32[32,256]{1,0:T(8,128)S(1)}, u32[]{:S(2)}, u32[]{:S(2)}) %collective-permute-start.3) | collective-permute-done | bytes 32800 | tf_op jit(solution)/shard_map/ppermute | solution.py:403
  17.1 1.3 %shard_map.127 = bf16[2048,256]{1,0:T(8,128)(2,1)} custom-call(bf16[2048,256]{1,0:T(8,128)(2,1)S(1)} %get-tuple-element.24.inner, f32[64,256]{1,0:T(8,128)S(1)} %get-tuple-element.25.sides, f32[32,256]{1,0:T(8,128)S(1)} %collective-permute-done.2.y_before, f32[32,256]{1,0:T(8,128)S(1)} %collective-permute-done.3.y_after, ...), custom_call_target="tpu_custom_call" | custom-call | flops 134217728 | bytes 4194304 | tf_op jit(solution)/shard_map/pallas_call | solution.py:383
  18.5 8.2 %all-to-all-start = ((bf16[128,16,256]{2,1,0:T(8,128)(2,1)}), bf16[128,16,256]{2,1,0:T(8,128)(2,1)S(1)}, u32[]{:S(2)}, u32[]{:S(2)}) async-start(bf16[128,16,256]{2,1,0:T(8,128)(2,1)} %bitcast.1), calls=%async_computation | async-start | bytes 2097152 | tf_op jit(solution)/shard_map/all_to_all | solution.py:407
  26.7 0.4 copy.15.w_out
  27.3 18.6 %all-to-all-done = bf16[128,16,256]{2,1,0:T(8,128)(2,1)S(1)} async-done(((bf16[128,16,256]{2,1,0:T(8,128)(2,1)}), bf16[128,16,256]{2,1,0:T(8,128)(2,1)S(1)}, u32[]{:S(2)}, u32[]{:S(2)}) %all-to-all-start) | async-done | bytes 1048608 | tf_op jit(solution)/shard_map/all_to_all | solution.py:407
  45.8 1.5 %shard_map.128 = (bf16[2048,1024]{1,0:T(8,128)(2,1)S(1)}, f32[128,128]{1,0:T(8,128)S(1)}) custom-call(bf16[2048,256]{1,0:T(8,128)(2,1)S(1)} %bitcast.11, bf16[1,256,1024]{2,1,0:T(8,128)(2,1)S(1)} %copy-done.8, f32[1,1024]{1,0:T(1,128)S(1)} %copy-done.11, s32[1,128]{1,0:T(1,128)S(1)} %bitcast.12, s32[1,128]{1,0:T(1,128)S(1)} %bitcast.15), custom_call_target="tpu_custom_call" | custom-call | flops 1073741824 | bytes 6291456 | tf_op jit(solution)/shard_map/pallas_call | solution.py:383
  47.4 7.4 %shard_map.129 = (bf16[128,40,128]{2,1,0:T(8,128)(2,1)}, f32[8,128]{1,0:T(8,128)S(1)}) custom-call(bf16[2048,1024]{1,0:T(8,128)(2,1)S(1)} %get-tuple-element.32.first, bf16[1,1024,1024]{2,1,0:T(8,128)(2,1)S(1)} %copy-done.7, f32[1,1024]{1,0:T(1,128)S(1)} %copy-done.12, bf16[1,1024,264]{2,1,0:T(8,128)(2,1)S(1)} %copy.15.w_out, ...), custom_call_target="tpu_custom_call" | custom-call | flops 5905580032 | bytes 8388608 | tf_op jit(solution)/shard_map/pallas_call | solution.py:383
  54.9 4.8 %all-to-all-start.1 = ((bf16[128,40,128]{2,1,0:T(8,128)(2,1)}), bf16[128,40,128]{2,1,0:T(8,128)(2,1)S(1)}, u32[]{:S(2)}, u32[]{:S(2)}) async-start(bf16[128,40,128]{2,1,0:T(8,128)(2,1)} %get-tuple-element.34), calls=%async_computation.1 | async-start | bytes 2621440 | tf_op jit(solution)/shard_map/all_to_all | solution.py:407
  59.7 4.9 %shard_map.130 = (s32[128,128]{1,0:T(8,128)S(1)}, f32[16,128,128]{2,1,0:T(8,128)S(1)}) custom-call(s32[1,128]{1,0:T(1,128)S(1)} %bitcast.16, f32[128,256]{1,0:T(8,128)S(1)} %copy-done.9, s32[1,1024]{1,0:T(1,128)S(1)} %get-tuple-element.28.slot_row.refs_2_, f32[8,128]{1,0:T(8,128)S(1)} %get-tuple-element.35.refs_3_), custom_call_target="tpu_custom_call" | custom-call | flops 1073741824 | bytes 12582912 | tf_op jit(solution)/shard_map/pallas_call | solution.py:383
  64.6 17.1 %all-to-all-done.1.refs_0_.answer = bf16[128,40,128]{2,1,0:T(8,128)(2,1)S(1)} async-done(((bf16[128,40,128]{2,1,0:T(8,128)(2,1)}), bf16[128,40,128]{2,1,0:T(8,128)(2,1)S(1)}, u32[]{:S(2)}, u32[]{:S(2)}) %all-to-all-start.1) | async-done | bytes 1310752 | tf_op jit(solution)/shard_map/all_to_all | solution.py:407
  81.7 1.8 %shard_map.131.token = f32[256,128]{1,0:T(8,128)} custom-call(bf16[128,40,128]{2,1,0:T(8,128)(2,1)S(1)} %all-to-all-done.1.refs_0_.answer, s32[128,128]{1,0:T(8,128)S(1)} %get-tuple-element.36.refs_1_, f32[16,128,128]{2,1,0:T(8,128)S(1)} %get-tuple-element.37.refs_2_, s32[1,128]{1,0:T(1,128)S(1)} %bitcast.13), custom_call_target="tpu_custom_call" | custom-call | flops 134217728 | bytes 4194304 | tf_op jit(solution)/shard_map/pallas_call | solution.py:383
  83.5 4.8 %all-to-all-start.2 = ((f32[128,2,128]{2,1,0:T(2,128)}), f32[128,2,128]{2,1,0:T(2,128)S(1)}, u32[]{:S(2)}, u32[]{:S(2)}) async-start(f32[128,2,128]{2,1,0:T(2,128)} %bitcast.8), calls=%async_computation.2 | async-start | bytes 262144 | tf_op jit(solution)/shard_map/all_to_all | solution.py:407
  88.3 1.7 %shard_map.132.partial = f32[32,32,256]{2,1,0:T(8,128)S(1)} custom-call(f32[32,32,256]{2,1,0:T(8,128)S(1)} %copy-done.1, f32[256,128]{1,0:T(8,128)} %shard_map.131.token), custom_call_target="tpu_custom_call" | custom-call | flops 67108864 | bytes 8388608 | tf_op jit(solution)/shard_map/pallas_call | solution.py:383
  90.0 2.5 %shard_map.133 = (f32[32,32,256]{2,1,0:T(8,128)}, f32[2,16,128]{2,1,0:T(8,128)S(1)}) custom-call(bf16[128,40,128]{2,1,0:T(8,128)(2,1)S(1)} %all-to-all-done.1.refs_0_.answer, s32[1,1024]{1,0:T(1,128)S(1)} %get-tuple-element.28.slot_row.refs_2_, f32[32,32,256]{2,1,0:T(8,128)S(1)} %shard_map.132.partial, f32[32,256]{1,0:T(8,128)S(1)} %collective-permute-done.x_before, ...), custom_call_target="tpu_custom_call" | custom-call | flops 1073741824 | bytes 12582912 | tf_op jit(solution)/shard_map/pallas_call | solution.py:383
  92.4 5.8 %all-to-all-done.2.received = f32[128,2,128]{2,1,0:T(2,128)S(1)} async-done(((f32[128,2,128]{2,1,0:T(2,128)}), f32[128,2,128]{2,1,0:T(2,128)S(1)}, u32[]{:S(2)}, u32[]{:S(2)}) %all-to-all-start.2) | async-done | bytes 131104 | tf_op jit(solution)/shard_map/all_to_all | solution.py:407
  98.2 0.9 shard_map.134
  (39 shorter events, 0.4 us)
Async XLA Ops:
  0.6 1.2 %copy-start = (f32[32,32,256]{2,1,0:T(8,128)S(1)}, f32[32,32,256]{2,1,0:T(8,128)}, u32[]{:S(2)}) copy-start(f32[32,32,256]{2,1,0:T(8,128)} %state.5) | copy-start | bytes 3145732
  1.9 5.6 %copy-start.10 = (s32[1024,1]{0,1:T(1,128)S(1)}, s32[1024,1]{0,1:T(1,128)}, u32[]{:S(2)}) copy-start(s32[1024,1]{0,1:T(1,128)} %param.12) | copy-start | bytes 12292
  2.1 6.7 %collective-permute-start.1 = (f32[32,256]{1,0:T(8,128)S(1)}, f32[32,256]{1,0:T(8,128)S(1)}, u32[]{:S(2)}, u32[]{:S(2)}) collective-permute-start(f32[32,256]{1,0:T(8,128)S(1)} %get-tuple-element.21.token), channel_id=1, source_target_pairs={{0,96},{32,0},{64,32},{96,64},{1,97},{33,1},{65,33},{97,65},{2,98}... | collective-permute-start | bytes 98312 | tf_op jit(solution)/shard_map/ppermute | solution.py:403
  5.7 4.0 %collective-permute-start = (f32[32,256]{1,0:T(8,128)S(1)}, f32[32,256]{1,0:T(8,128)S(1)}, u32[]{:S(2)}, u32[]{:S(2)}) collective-permute-start(f32[32,256]{1,0:T(8,128)S(1)} %get-tuple-element.22), channel_id=1, source_target_pairs={{0,32},{32,64},{64,96},{96,0},{1,33},{33,65},{65,97},{97,1},{2,34}... | collective-permute-start | bytes 98312 | tf_op jit(solution)/shard_map/ppermute | solution.py:403
  9.8 5.0 %collective-permute-start.2 = (f32[32,256]{1,0:T(8,128)S(1)}, f32[32,256]{1,0:T(8,128)S(1)}, u32[]{:S(2)}, u32[]{:S(2)}) collective-permute-start(f32[32,256]{1,0:T(8,128)S(1)} %get-tuple-element.29), channel_id=1, source_target_pairs={{0,1},{1,2},{2,3},{3,4},{4,5},{5,6},{6,7},{7,8},{8,9},{9,10},{10,1... | collective-permute-start | bytes 98312 | tf_op jit(solution)/shard_map/ppermute | solution.py:403
  13.5 3.6 %collective-permute-start.3 = (f32[32,256]{1,0:T(8,128)S(1)}, f32[32,256]{1,0:T(8,128)S(1)}, u32[]{:S(2)}, u32[]{:S(2)}) collective-permute-start(f32[32,256]{1,0:T(8,128)S(1)} %get-tuple-element.30), channel_id=1, source_target_pairs={{0,31},{1,0},{2,1},{3,2},{4,3},{5,4},{6,5},{7,6},{8,7},{9,8},{10,9... | collective-permute-start | bytes 98312 | tf_op jit(solution)/shard_map/ppermute | solution.py:403
  14.8 3.6 %copy-start.2 = (f32[32,256]{1,0:T(8,128)}, f32[32,256]{1,0:T(8,128)S(1)}, u32[]{:S(2)}) copy-start(f32[32,256]{1,0:T(8,128)S(1)} %collective-permute-done.2.y_before) | copy-start | bytes 98308
  17.1 1.3 %copy-start.4 = (f32[32,256]{1,0:T(8,128)}, f32[32,256]{1,0:T(8,128)S(1)}, u32[]{:S(2)}) copy-start(f32[32,256]{1,0:T(8,128)S(1)} %collective-permute-done.3.y_after) | copy-start | bytes 98308
  17.1 9.6 %copy-start.15 = (bf16[1,1024,264]{1,2,0:T(8,128)(2,1)S(1)}, bf16[1,1024,264]{1,2,0:T(8,128)(2,1)}, u32[]{:S(2)}) copy-start(bf16[1,1024,264]{1,2,0:T(8,128)(2,1)} %param.17) | copy-start | bytes 1622020
  18.4 27.4 %copy-start.6 = (s32[128,1]{0,1:T(1,128)S(1)}, s32[128,1]{0,1:T(1,128)}, u32[]{:S(2)}) copy-start(s32[128,1]{0,1:T(1,128)} %param.19) | copy-start | bytes 1540
  18.4 27.4 %copy-start.8 = (bf16[1,256,1024]{2,1,0:T(8,128)(2,1)S(1)}, bf16[1,256,1024]{2,1,0:T(8,128)(2,1)}, u32[]{:S(2)}) copy-start(bf16[1,256,1024]{2,1,0:T(8,128)(2,1)} %w_in.1) | copy-start | bytes 1572868
  18.4 27.4 %copy-start.11 = (f32[1,1024]{1,0:T(1,128)S(1)}, f32[1,1024]{1,0:T(1,128)}, u32[]{:S(2)}) copy-start(f32[1,1024]{1,0:T(1,128)} %b_in.1) | copy-start | bytes 12292
  18.4 27.4 %copy-start.13 = (s32[128]{0:T(128)S(1)}, s32[128]{0:T(128)}, u32[]{:S(2)}) copy-start(s32[128]{0:T(128)} %param.20) | copy-start | bytes 1540
  18.5 27.4 %all-to-all-start = ((bf16[128,16,256]{2,1,0:T(8,128)(2,1)}), bf16[128,16,256]{2,1,0:T(8,128)(2,1)S(1)}, u32[]{:S(2)}, u32[]{:S(2)}) async-start(bf16[128,16,256]{2,1,0:T(8,128)(2,1)} %bitcast.1), calls=%async_computation | async-start | bytes 2097152 | tf_op jit(solution)/shard_map/all_to_all | solution.py:407
  27.3 20.1 %copy-start.12 = (f32[1,1024]{1,0:T(1,128)S(1)}, f32[1,1024]{1,0:T(1,128)}, u32[]{:S(2)}) copy-start(f32[1,1024]{1,0:T(1,128)} %b_mid.1) | copy-start | bytes 12292
  45.8 1.6 %copy-start.7 = (bf16[1,1024,1024]{2,1,0:T(8,128)(2,1)S(1)}, bf16[1,1024,1024]{2,1,0:T(8,128)(2,1)}, u32[]{:S(2)}) copy-start(bf16[1,1024,1024]{2,1,0:T(8,128)(2,1)} %w_mid.1) | copy-start | bytes 6291460
  54.9 4.8 %copy-start.9 = (f32[128,256]{1,0:T(8,128)S(1)}, f32[128,256]{1,0:T(8,128)}, u32[]{:S(2)}) copy-start(f32[128,256]{1,0:T(8,128)} %refs_1_.1) | copy-start | bytes 393220
  54.9 4.8 %copy-start.14 = (s32[128]{0:T(128)S(1)}, s32[128]{0:T(128)}, u32[]{:S(2)}) copy-start(s32[128]{0:T(128)} %param.18) | copy-start | bytes 1540
  54.9 26.8 %all-to-all-start.1 = ((bf16[128,40,128]{2,1,0:T(8,128)(2,1)}), bf16[128,40,128]{2,1,0:T(8,128)(2,1)S(1)}, u32[]{:S(2)}, u32[]{:S(2)}) async-start(bf16[128,40,128]{2,1,0:T(8,128)(2,1)} %get-tuple-element.34), calls=%async_computation.1 | async-start | bytes 2621440 | tf_op jit(solution)/shard_map/all_to_all | solution.py:407
  64.6 23.7 %copy-start.1 = (f32[32,32,256]{2,1,0:T(8,128)S(1)}, f32[32,32,256]{2,1,0:T(8,128)}, u32[]{:S(2)}) copy-start(f32[32,32,256]{2,1,0:T(8,128)} %state.5) | copy-start | bytes 3145732
  83.5 6.5 %copy-start.3 = (f32[32,256]{1,0:T(8,128)S(1)}, f32[32,256]{1,0:T(8,128)}, u32[]{:S(2)}) copy-start(f32[32,256]{1,0:T(8,128)} %copy-done.2) | copy-start | bytes 98308
  83.5 6.5 %copy-start.5 = (f32[32,256]{1,0:T(8,128)S(1)}, f32[32,256]{1,0:T(8,128)}, u32[]{:S(2)}) copy-start(f32[32,256]{1,0:T(8,128)} %copy-done.4) | copy-start | bytes 98308
  83.5 14.7 %all-to-all-start.2 = ((f32[128,2,128]{2,1,0:T(2,128)}), f32[128,2,128]{2,1,0:T(2,128)S(1)}, u32[]{:S(2)}, u32[]{:S(2)}) async-start(f32[128,2,128]{2,1,0:T(2,128)} %bitcast.8), calls=%async_computation.2 | async-start | bytes 262144 | tf_op jit(solution)/shard_map/all_to_all | solution.py:407

commit v4 on v3

--- a/solution.py
+++ b/solution.py
@@ -12,7 +12,7 @@
 OB_DEV = 16
 STEP_DT = 0.2
 HIGHEST = lax.Precision.HIGHEST
-AXES = ("gx", "gy")
+AXES = ("gy", "gx")
 F32 = jnp.float32
 BF16 = jnp.bfloat16
 MIB = 1 << 20
@@ -163,14 +163,19 @@
     return hot, rank.astype(jnp.int32)
 
 
-def route_kernel(capacity, size_y, member_row, slot_row, hot_rows, hot_sides):
+def position(device, sizes):
+    size_gx, size_gy = sizes
+    return device % size_gy * size_gx + device // size_gy
+
+
+def route_kernel(sizes, capacity, size_y, member_row, slot_row, hot_rows, hot_sides):
     columns = member_row.shape[1]
     size_x = columns // size_y
     earlier = (iota((128, 128), 0) < iota((128, 128), 1)).astype(F32).astype(BF16)
     seen = jnp.zeros((128, 1), F32)
     for b in range(columns // 128):
         part = slice(b * 128, (b + 1) * 128)
-        members = member_row[:, part]
+        members = position(member_row[:, part], sizes)
         hot = (iota((128, 128), 0) == members).astype(F32)
         count = dot(hot.astype(BF16), earlier) + seen
         rank = jnp.sum(count * hot, axis=0, keepdims=True).astype(jnp.int32)
@@ -243,15 +248,17 @@
     return jnp.sum(wide, axis=1, keepdims=True)
 
 
-def prepare_kernel(capacity, element_row, weight, slot_row, token, places, tiled):
+def prepare_kernel(capacity, element_row, weight, slot_row, places, tiled):
     count = element_row.shape[1]
     lane = iota((count, 128), 1)
-    for c in range(16):
-        part = weight[:, (c // 8) * 128 : (c // 8 + 1) * 128]
-        part = jnp.where(lane // 16 == c % 8, part, 0.0)
+    for c in range(8):
+        part = weight[:, (c // 4) * 128 : (c // 4 + 1) * 128]
+        low = jnp.where(lane // 16 == 2 * c % 8, part, 0.0)
+        high = jnp.where(lane // 16 == 2 * c % 8 + 1, part, 0.0)
         for distance in (64, 32, 16):
-            part = part + pltpu.roll(part, distance, 1)
-        tiled[c] = part
+            low = low + pltpu.roll(low, distance, 1)
+            high = high + pltpu.roll(high, distance, 1)
+        tiled[c] = jnp.where(lane < 64, low, high)
 
     columns = slot_row.shape[1]
     lane = iota((128, 128), 1)
@@ -276,8 +283,8 @@
     return half + half * jnp.tanh(half)
 
 
-def first_kernel(rows, w_in, b_in, owner_row, block_row, out, blocks, w_half):
-    owners = owner_row[...]
+def first_kernel(sizes, rows, w_in, b_in, owner_row, block_row, places, out, blocks, w_half):
+    owners = position(owner_row[...], sizes)
     hot, rank = owner_ranks(owners)
     values = block_row[...].astype(F32)
     lane = iota(blocks.shape, 1)
@@ -293,47 +300,49 @@
         out[part, :] = silu_of_half(dot(rows[part, :], w_half[...]) + b_half).astype(BF16)
 
 
-def second_kernel(first, w_mid, b_mid, w_out, w_flux, blocks, answer, token, w_half, out, sems):
-    step = first.shape[0] // sems.shape[0]
+def dot_by_output(a, b):
+    return lax.dot_general(a, b, (((1,), (1,)), ((), ())), preferred_element_type=F32)
+
+
+def second_kernel(first, w_mid, b_mid, w_last, blocks, out, w_half, w_flux):
+    step = 512
     sources = step // 16
     lane = iota((step, 128), 1)
     own = lane // 8 == iota((step, 128), 0) % 16
     line = iota((sources, 8, 128), 1)
     w_half[...] = w_mid[0] * jnp.asarray(0.5, BF16)
+    w_flux[...] = jnp.concatenate([w_last[0, 256:264, :].astype(F32)] * 16).astype(BF16)
     b_half = 0.5 * b_mid[...]
-    copies = []
-    for b in range(sems.shape[0]):
+    for b in range(first.shape[0] // step):
         hidden = dot(first[b * step : (b + 1) * step, :], w_half[...])
         hidden = silu_of_half(hidden + b_half).astype(BF16)
-        tends = dot(hidden, w_out[0, :, 0:256]).astype(BF16)
+        tends = dot_by_output(hidden, w_last[0, 0:256, :]).astype(BF16)
         part = slice(b * sources, (b + 1) * sources)
         out[part, 0:16, :] = tends[:, :128].reshape(sources, 16, 128)
         out[part, 16:32, :] = tends[:, 128:].reshape(sources, 16, 128)
-        flux = jnp.where(own, dot(hidden, w_flux[...]), 0.0)
+        flux = jnp.where(own, dot_by_output(hidden, w_flux[...]), 0.0)
         flux = jnp.sum(flux.reshape(sources, 16, 128), axis=1, keepdims=True)
         names = blocks[part, :].reshape(sources, 1, 128)
         tail = jnp.where(line == 0, flux, jnp.where(line == 1, names, 0.0))
         out[part, 32:40, :] = tail.astype(BF16)
-        copy = pltpu.make_async_copy(out.at[part], answer.at[part], sems.at[b])
-        copy.start()
-        copies.append(copy)
-    token[...] = blocks[0:8, :]
-    for copy in copies:
-        copy.wait()
-
-
-def contribution_kernel(capacity, answer, places, tiled, owner_row, send):
+
+
+def contribution_kernel(sizes, capacity, answer, places, tiled, owner_row, send):
     flux = answer[:, 32:40, :].astype(F32)[:, 0, :].astype(BF16)
     spread = (iota((128, 128), 0) % 8 == iota((128, 128), 1) // 16).astype(F32).astype(BF16)
     lane = iota((128, 128), 1)
     total = None
     for c in range(16):
+        if c % 2 == 0:
+            pair = tiled[c // 2]
+            swapped = pltpu.roll(pair, 64, 1)
+        weights = jnp.where(lane < 64, *((pair, swapped) if c % 2 == 0 else (swapped, pair)))
         slots = places[:, c : c + 1]
         pick = (lane == slots // capacity).astype(F32).astype(BF16)
         value = jnp.where(lane // 8 == slots % capacity, dot(pick, flux), 0.0)
-        term = dot(value.astype(BF16), spread) * tiled[c]
+        term = dot(value.astype(BF16), spread) * weights
         total = term if total is None else total + term
-    owners = owner_row[...]
+    owners = position(owner_row[...], sizes)
     _, rank = owner_ranks(owners)
     hot = (iota(send.shape, 0) == owners * 2 + rank).astype(F32)
     send[...] = dot(hot, total, HIGHEST)
@@ -421,7 +430,8 @@
     regrid_weight,
 ):
     size_x, size_y, features = state.shape
-    devices = lax.axis_size("gx") * lax.axis_size("gy")
+    sizes = lax.axis_size("gx"), lax.axis_size("gy")
+    devices = sizes[0] * sizes[1]
     columns = size_x * size_y
     capacity = 2 * columns // devices
     slots = devices * capacity
@@ -451,7 +461,7 @@
 
     partial = local(x_low)
     slot_row, hot_rows, hot_sides = call(
-        lambda *refs: route_kernel(capacity, size_y, *refs),
+        lambda *refs: route_kernel(sizes, capacity, size_y, *refs),
         [((1, columns), jnp.int32), ((slots, columns), BF16), ((slots, 128), BF16)],
         group_member.reshape(1, columns),
         nbytes=8 * MIB,
@@ -495,55 +505,49 @@
     )
     received = exchange(send.reshape(devices, capacity, features)).reshape(slots, features)
 
-    w_flux = jnp.tile(w_out[0, :, features:], (1, 16))
+    places, tiled = call(
+        lambda *refs: prepare_kernel(capacity, *refs),
+        [((count, 128), jnp.int32), ((8, count, 128), F32)],
+        intersection_element.reshape(1, count),
+        regrid_weight,
+        slot_row,
+        nbytes=12 * MIB,
+        flops=2 * 16 * count * columns * 256,
+    )
     hidden = w_in.shape[2]
     owner_row = ocean_owner.reshape(1, count)
     first, blocks = call(
-        first_kernel,
+        lambda *refs: first_kernel(sizes, *refs),
         [((slots, hidden), BF16), ((devices, 128), F32)],
         received,
         w_in,
         bias_in,
         owner_row,
         ocean_block.reshape(1, count),
+        places,
+        spaces={5: pl.ANY},
         nbytes=6 * MIB,
         flops=2 * slots * features * hidden,
         transcendentals=slots * hidden,
         scratch=[pltpu.VMEM((features, hidden), BF16)],
     )
-    answered, token = call(
+    (answered,) = call(
         second_kernel,
-        [((devices, 40, 128), BF16), ((8, 128), F32)],
+        [((devices, 40, 128), BF16)],
         first,
         w_mid,
         bias_mid,
-        w_out,
-        w_flux,
+        jnp.swapaxes(w_out, 1, 2),
         blocks,
         nbytes=8 * MIB,
         flops=2 * slots * hidden * (hidden + 384),
         transcendentals=slots * hidden,
         limit=24,
-        out_spaces={0: pl.ANY},
-        scratch=[
-            pltpu.VMEM((hidden, hidden), BF16),
-            pltpu.VMEM((devices, 40, 128), BF16),
-            pltpu.SemaphoreType.DMA((4,)),
-        ],
+        scratch=[pltpu.VMEM((hidden, hidden), BF16), pltpu.VMEM((128, hidden), BF16)],
     )
     answer = exchange(answered)
-    places, tiled = call(
-        lambda *refs: prepare_kernel(capacity, *refs),
-        [((count, 128), jnp.int32), ((16, count, 128), F32)],
-        intersection_element.reshape(1, count),
-        regrid_weight,
-        slot_row,
-        token,
-        nbytes=12 * MIB,
-        flops=2 * 16 * count * columns * 256,
-    )
     (ocean_send,) = call(
-        lambda *refs: contribution_kernel(capacity, *refs),
+        lambda *refs: contribution_kernel(sizes, capacity, *refs),
         [((2 * devices, 128), F32)],
         answer,
         places,

time: 99.5 us -> 96.3 us (0.968)
  blocking collectives: 0 us -> 25.9 us
  waiting for transfers between devices: 44.7 us -> 24 us
  starting transfers between devices: 25.1 us -> 19 us
  Pallas kernels: 26.5 us -> 24.9 us
    all_to_all x0 -> x1, blocking collectives: none -> 25.9 us  [exchange(): return lax.all_to_all(value, AXES, split_axis=0, concat_axis=0, tiled=True)]
    all_to_all x3 -> x2, waiting for transfers between devices: 41.5 us -> 21.7 us  [exchange(): return lax.all_to_all(value, AXES, split_axis=0, concat_axis=0, tiled=True)]
    all_to_all x3 -> x2, starting transfers between devices: 17.7 us -> 12.6 us  [exchange(): return lax.all_to_all(value, AXES, split_axis=0, concat_axis=0, tiled=True)]
    pallas_call x13, Pallas kernels: 26.5 us -> 24.9 us  [call(): pl.pallas_call(kernel, out_shape=[jax.ShapeDtypeStruct(s, d) for s, d in...]
  transfers between devices with their start and end apart: 7 -> 6, of which waited for: 5 -> 3; matrix products, arithmetic and copies ran while one was open for 1% -> 0% of each run, Pallas kernels for 13% -> 13%
where the time goes in v4:
time: 96.3 us; the launch traced here: 96 us
  blocking collectives  25.9 us (27%)
  Pallas kernels  24.9 us (26%)
  waiting for transfers between devices  24 us (25%)
  starting transfers between devices  19 us (20%)
  local copies, waits for them, and re-layouts  1.35 us (1%)
    all_to_all x1, blocking collectives, exchange(): return lax.all_to_all(value, AXES, split_axis=0, concat_axis=0, tiled=True)  25.9 us
    pallas_call x13, Pallas kernels, call(): pl.pallas_call(kernel, out_shape=[jax.ShapeDtypeStruct(s, d) for s, d in...  24.9 us
    all_to_all x2, waiting for transfers between devices, exchange(): return lax.all_to_all(value, AXES, split_axis=0, concat_axis=0, tiled=True)  21.7 us
    all_to_all x2, starting transfers between devices, exchange(): return lax.all_to_all(value, AXES, split_axis=0, concat_axis=0, tiled=True)  12.6 us
    ppermute x4, starting transfers between devices, shift(): lax.ppermute(value, axis, [(i, (i + step) % size) for i in range(size)])  6.4 us
    ppermute x4, waiting for transfers between devices, shift(): lax.ppermute(value, axis, [(i, (i + step) % size) for i in range(size)])  2.3 us
  transfers between devices with their start and end apart: 6, of which 3 were waited for; matrix products, arithmetic and copies ran while one was open for 0% of the time, Pallas kernels for 13%

profile of v4, /device:TPU:1, one launch (start us, length us, event | category | flops | bytes accessed | tf_op | source)
XLA Modules:
  0.0 96.0 jit_solution(8155279192996367348)
XLA Ops:
  0.6 0.0 copy-start
  0.6 1.2 %copy-done = f32[32,32,256]{2,1,0:T(8,128)S(1)} copy-done((f32[32,32,256]{2,1,0:T(8,128)S(1)}, f32[32,32,256]{2,1,0:T(8,128)}, u32[]{:S(2)}) %copy-start) | copy-done | bytes 1048600
  1.9 0.3 shard_map.122
  2.1 2.2 %collective-permute-start = (f32[32,256]{1,0:T(8,128)S(1)}, f32[32,256]{1,0:T(8,128)S(1)}, u32[]{:S(2)}, u32[]{:S(2)}) collective-permute-start(f32[32,256]{1,0:T(8,128)S(1)} %get-tuple-element.20), channel_id=1, source_target_pairs={{0,32},{32,64},{64,96},{96,0},{1,33},{33,65},{65,97},{97,1},{2,34}... | collective-permute-start | bytes 98312 | tf_op jit(solution)/shard_map/ppermute | solution.py:412
  4.3 1.5 %collective-permute-start.1 = (f32[32,256]{1,0:T(8,128)S(1)}, f32[32,256]{1,0:T(8,128)S(1)}, u32[]{:S(2)}, u32[]{:S(2)}) collective-permute-start(f32[32,256]{1,0:T(8,128)S(1)} %get-tuple-element.19.token), channel_id=1, source_target_pairs={{0,96},{32,0},{64,32},{96,64},{1,97},{33,1},{65,33},{97,65},{2,98}... | collective-permute-start | bytes 98312 | tf_op jit(solution)/shard_map/ppermute | solution.py:412
  5.8 1.7 %shard_map.123.partial = f32[32,32,256]{2,1,0:T(8,128)S(1)} custom-call(f32[32,32,256]{2,1,0:T(8,128)S(1)} %copy-done, f32[32,256]{1,0:T(8,128)S(1)} %get-tuple-element.19.token), custom_call_target="tpu_custom_call" | custom-call | flops 67108864 | bytes 8388608 | tf_op jit(solution)/shard_map/pallas_call | solution.py:392
  7.5 1.4 %shard_map.124 = (s32[1,1024]{1,0:T(1,128)S(1)}, bf16[2048,1024]{1,0:T(8,128)(2,1)S(1)}, bf16[2048,128]{1,0:T(8,128)(2,1)S(1)}) custom-call(s32[1,1024]{1,0:T(1,128)S(1)} %bitcast.12), custom_call_target="tpu_custom_call" | custom-call | flops 67108864 | bytes 8388608 | tf_op jit(solution)/shard_map/pallas_call | solution.py:392
  9.0 2.7 %collective-permute-start.2 = (f32[32,256]{1,0:T(8,128)S(1)}, f32[32,256]{1,0:T(8,128)S(1)}, u32[]{:S(2)}, u32[]{:S(2)}) collective-permute-start(f32[32,256]{1,0:T(8,128)S(1)} %get-tuple-element.27), channel_id=1, source_target_pairs={{0,1},{1,2},{2,3},{3,4},{4,5},{5,6},{6,7},{7,8},{8,9},{9,10},{10,1... | collective-permute-start | bytes 98312 | tf_op jit(solution)/shard_map/ppermute | solution.py:412
  11.7 1.3 %shard_map.125 = (bf16[2048,256]{1,0:T(8,128)(2,1)S(1)}, f32[64,256]{1,0:T(8,128)S(1)}) custom-call(f32[32,32,256]{2,1,0:T(8,128)S(1)} %shard_map.123.partial, f32[32,256]{1,0:T(8,128)S(1)} %collective-permute-done.x_before, f32[32,256]{1,0:T(8,128)S(1)} %collective-permute-done.1.x_after, bf16[2048,1024]{1,0:T(8,128)(2,1)S(1)} %get-tuple-element.21.hot_rows), custom_call_target="tpu_custom_call" | custom-call | flops 1073741824 | bytes 8388608 | tf_op jit(solution)/shard_map/pallas_call | solution.py:392
  13.0 2.3 %collective-permute-done.3.y_after = f32[32,256]{1,0:T(8,128)S(1)} collective-permute-done((f32[32,256]{1,0:T(8,128)S(1)}, f32[32,256]{1,0:T(8,128)S(1)}, u32[]{:S(2)}, u32[]{:S(2)}) %collective-permute-start.3) | collective-permute-done | bytes 32800 | tf_op jit(solution)/shard_map/ppermute | solution.py:412
  15.3 1.3 %shard_map.127 = bf16[2048,256]{1,0:T(8,128)(2,1)} custom-call(bf16[2048,256]{1,0:T(8,128)(2,1)S(1)} %get-tuple-element.22.inner, f32[64,256]{1,0:T(8,128)S(1)} %get-tuple-element.23.sides, f32[32,256]{1,0:T(8,128)S(1)} %collective-permute-done.2.y_before, f32[32,256]{1,0:T(8,128)S(1)} %collective-permute-done.3.y_after, ...), custom_call_target="tpu_custom_call" | custom-call | flops 134217728 | bytes 4194304 | tf_op jit(solution)/shard_map/pallas_call | solution.py:392
  16.6 9.0 %all-to-all-start = ((bf16[128,16,256]{2,1,0:T(8,128)(2,1)}), bf16[128,16,256]{2,1,0:T(8,128)(2,1)S(1)}, u32[]{:S(2)}, u32[]{:S(2)}) async-start(bf16[128,16,256]{2,1,0:T(8,128)(2,1)} %bitcast.1), calls=%async_computation | async-start | bytes 2097152 | tf_op jit(solution)/shard_map/all_to_all | solution.py:416
  25.6 4.0 %shard_map.128 = (s32[128,128]{1,0:T(8,128)S(1)}, f32[8,128,128]{2,1,0:T(8,128)S(1)}) custom-call(s32[1,128]{1,0:T(1,128)S(1)} %bitcast.13, f32[128,256]{1,0:T(8,128)S(1)} %copy-done.6, s32[1,1024]{1,0:T(1,128)S(1)} %get-tuple-element.26.slot_row.refs_2_), custom_call_target="tpu_custom_call" | custom-call | flops 1073741824 | bytes 12582912 | tf_op jit(solution)/shard_map/pallas_call | solution.py:392
  29.6 15.7 %all-to-all-done = bf16[128,16,256]{2,1,0:T(8,128)(2,1)S(1)} async-done(((bf16[128,16,256]{2,1,0:T(8,128)(2,1)}), bf16[128,16,256]{2,1,0:T(8,128)(2,1)S(1)}, u32[]{:S(2)}, u32[]{:S(2)}) %all-to-all-start) | async-done | bytes 1048608 | tf_op jit(solution)/shard_map/all_to_all | solution.py:416
  45.3 1.5 %shard_map.129 = (bf16[2048,1024]{1,0:T(8,128)(2,1)S(1)}, f32[128,128]{1,0:T(8,128)S(1)}) custom-call(bf16[2048,256]{1,0:T(8,128)(2,1)S(1)} %bitcast.8, bf16[1,256,1024]{2,1,0:T(8,128)(2,1)S(1)} %copy-done.5, f32[1,1024]{1,0:T(1,128)S(1)} %copy-done.8, s32[1,128]{1,0:T(1,128)S(1)} %bitcast.9, s32[1,128]{1,0:T(1,128)S(1)} %bitcast.14, ...), custom_call_target="tpu_custom_call" | custom-call | flops 1073741824 | bytes 6291456 | tf_op jit(solution)/shard_map/pallas_call | solution.py:392
  46.8 0.1 copy-done.3
  46.9 6.7 %shard_map.130 = bf16[128,40,128]{2,1,0:T(8,128)(2,1)S(1)} custom-call(bf16[2048,1024]{1,0:T(8,128)(2,1)S(1)} %get-tuple-element.31.first, bf16[1,1024,1024]{2,1,0:T(8,128)(2,1)S(1)} %copy-done.3, f32[1,1024]{1,0:T(1,128)S(1)} %copy-done.9, bf16[1,264,1024]{2,1,0:T(8,128)(2,1)S(1)} %bitcast.11, f32[128,128]{1,0:T(8,128)S(1)} %get-tuple-element.32.blocks), custom_call_target="tpu_custom_call" | custom-call | flops 5905580032 | bytes 8388608 | tf_op jit(solution)/shard_map/pallas_call | solution.py:392
  53.6 25.9 %all_to_all.15.refs_0_.answer = bf16[128,40,128]{2,1,0:T(8,128)(2,1)S(1)} all-to-all(bf16[128,40,128]{2,1,0:T(8,128)(2,1)S(1)} %shard_map.130), channel_id=1, replica_groups=mesh['gx'=4,'gy'=32] {'gy','gx'}, dimensions={0} | all-to-all | bytes 2621440 | tf_op jit(solution)/shard_map/all_to_all | solution.py:416
  79.5 1.8 %shard_map.131.token = f32[256,128]{1,0:T(8,128)} custom-call(bf16[128,40,128]{2,1,0:T(8,128)(2,1)S(1)} %all_to_all.15.refs_0_.answer, s32[128,128]{1,0:T(8,128)S(1)} %get-tuple-element.30.refs_5_.refs_1_, f32[8,128,128]{2,1,0:T(8,128)S(1)} %get-tuple-element.33.refs_2_, s32[1,128]{1,0:T(1,128)S(1)} %bitcast.10), custom_call_target="tpu_custom_call" | custom-call | flops 134217728 | bytes 4194304 | tf_op jit(solution)/shard_map/pallas_call | solution.py:392
  81.3 3.6 %all-to-all-start.2 = ((f32[128,2,128]{2,1,0:T(2,128)}), f32[128,2,128]{2,1,0:T(2,128)S(1)}, u32[]{:S(2)}, u32[]{:S(2)}) async-start(f32[128,2,128]{2,1,0:T(2,128)} %bitcast.7), calls=%async_computation.2 | async-start | bytes 262144 | tf_op jit(solution)/shard_map/all_to_all | solution.py:416
  85.0 1.7 %shard_map.132.partial = f32[32,32,256]{2,1,0:T(8,128)S(1)} custom-call(f32[32,32,256]{2,1,0:T(8,128)S(1)} %copy-done.1, f32[256,128]{1,0:T(8,128)} %shard_map.131.token), custom_call_target="tpu_custom_call" | custom-call | flops 67108864 | bytes 8388608 | tf_op jit(solution)/shard_map/pallas_call | solution.py:392
  86.6 2.5 %shard_map.133 = (f32[32,32,256]{2,1,0:T(8,128)}, f32[2,16,128]{2,1,0:T(8,128)S(1)}) custom-call(bf16[128,40,128]{2,1,0:T(8,128)(2,1)S(1)} %all_to_all.15.refs_0_.answer, s32[1,1024]{1,0:T(1,128)S(1)} %get-tuple-element.26.slot_row.refs_2_, f32[32,32,256]{2,1,0:T(8,128)S(1)} %shard_map.132.partial, f32[32,256]{1,0:T(8,128)S(1)} %collective-permute-done.x_before, ...), custom_call_target="tpu_custom_call" | custom-call | flops 1073741824 | bytes 12582912 | tf_op jit(solution)/shard_map/pallas_call | solution.py:392
  89.1 6.1 %all-to-all-done.2.received = f32[128,2,128]{2,1,0:T(2,128)S(1)} async-done(((f32[128,2,128]{2,1,0:T(2,128)}), f32[128,2,128]{2,1,0:T(2,128)S(1)}, u32[]{:S(2)}, u32[]{:S(2)}) %all-to-all-start.2) | async-done | bytes 131104 | tf_op jit(solution)/shard_map/all_to_all | solution.py:416
  95.2 0.9 shard_map.134
  (26 shorter events, 0.1 us)
Async XLA Ops:
  0.6 1.2 %copy-start = (f32[32,32,256]{2,1,0:T(8,128)S(1)}, f32[32,32,256]{2,1,0:T(8,128)}, u32[]{:S(2)}) copy-start(f32[32,32,256]{2,1,0:T(8,128)} %state.5) | copy-start | bytes 3145732
  1.9 5.6 %copy-start.7 = (s32[1024,1]{0,1:T(1,128)S(1)}, s32[1024,1]{0,1:T(1,128)}, u32[]{:S(2)}) copy-start(s32[1024,1]{0,1:T(1,128)} %param.12) | copy-start | bytes 12292
  2.1 6.8 %collective-permute-start = (f32[32,256]{1,0:T(8,128)S(1)}, f32[32,256]{1,0:T(8,128)S(1)}, u32[]{:S(2)}, u32[]{:S(2)}) collective-permute-start(f32[32,256]{1,0:T(8,128)S(1)} %get-tuple-element.20), channel_id=1, source_target_pairs={{0,32},{32,64},{64,96},{96,0},{1,33},{33,65},{65,97},{97,1},{2,34}... | collective-permute-start | bytes 98312 | tf_op jit(solution)/shard_map/ppermute | solution.py:412
  4.3 4.6 %collective-permute-start.1 = (f32[32,256]{1,0:T(8,128)S(1)}, f32[32,256]{1,0:T(8,128)S(1)}, u32[]{:S(2)}, u32[]{:S(2)}) collective-permute-start(f32[32,256]{1,0:T(8,128)S(1)} %get-tuple-element.19.token), channel_id=1, source_target_pairs={{0,96},{32,0},{64,32},{96,64},{1,97},{33,1},{65,33},{97,65},{2,98}... | collective-permute-start | bytes 98312 | tf_op jit(solution)/shard_map/ppermute | solution.py:412
  9.0 4.0 %collective-permute-start.2 = (f32[32,256]{1,0:T(8,128)S(1)}, f32[32,256]{1,0:T(8,128)S(1)}, u32[]{:S(2)}, u32[]{:S(2)}) collective-permute-start(f32[32,256]{1,0:T(8,128)S(1)} %get-tuple-element.27), channel_id=1, source_target_pairs={{0,1},{1,2},{2,3},{3,4},{4,5},{5,6},{6,7},{7,8},{8,9},{9,10},{10,1... | collective-permute-start | bytes 98312 | tf_op jit(solution)/shard_map/ppermute | solution.py:412
  11.6 3.6 %collective-permute-start.3 = (f32[32,256]{1,0:T(8,128)S(1)}, f32[32,256]{1,0:T(8,128)S(1)}, u32[]{:S(2)}, u32[]{:S(2)}) collective-permute-start(f32[32,256]{1,0:T(8,128)S(1)} %get-tuple-element.28), channel_id=1, source_target_pairs={{0,31},{1,0},{2,1},{3,2},{4,3},{5,4},{6,5},{7,6},{8,7},{9,8},{10,9... | collective-permute-start | bytes 98312 | tf_op jit(solution)/shard_map/ppermute | solution.py:412
  15.3 10.3 %copy-start.6 = (f32[128,256]{1,0:T(8,128)S(1)}, f32[128,256]{1,0:T(8,128)}, u32[]{:S(2)}) copy-start(f32[128,256]{1,0:T(8,128)} %refs_1_.2) | copy-start | bytes 393220
  15.3 10.4 %copy-start.10 = (s32[128]{0:T(128)S(1)}, s32[128]{0:T(128)}, u32[]{:S(2)}) copy-start(s32[128]{0:T(128)} %param.18) | copy-start | bytes 1540
  16.6 28.7 %all-to-all-start = ((bf16[128,16,256]{2,1,0:T(8,128)(2,1)}), bf16[128,16,256]{2,1,0:T(8,128)(2,1)S(1)}, u32[]{:S(2)}, u32[]{:S(2)}) async-start(bf16[128,16,256]{2,1,0:T(8,128)(2,1)} %bitcast.1), calls=%async_computation | async-start | bytes 2097152 | tf_op jit(solution)/shard_map/all_to_all | solution.py:416
  25.6 19.8 %copy-start.2 = (s32[128,1]{0,1:T(1,128)S(1)}, s32[128,1]{0,1:T(1,128)}, u32[]{:S(2)}) copy-start(s32[128,1]{0,1:T(1,128)} %param.19) | copy-start | bytes 1540
  25.6 19.7 %copy-start.5 = (bf16[1,256,1024]{2,1,0:T(8,128)(2,1)S(1)}, bf16[1,256,1024]{2,1,0:T(8,128)(2,1)}, u32[]{:S(2)}) copy-start(bf16[1,256,1024]{2,1,0:T(8,128)(2,1)} %refs_1_.3) | copy-start | bytes 1572868
  25.6 19.7 %copy-start.8 = (f32[1,1024]{1,0:T(1,128)S(1)}, f32[1,1024]{1,0:T(1,128)}, u32[]{:S(2)}) copy-start(f32[1,1024]{1,0:T(1,128)} %refs_2_.1) | copy-start | bytes 12292
  25.6 19.7 %copy-start.11 = (s32[128]{0:T(128)S(1)}, s32[128]{0:T(128)}, u32[]{:S(2)}) copy-start(s32[128]{0:T(128)} %param.20) | copy-start | bytes 1540
  29.6 17.2 %copy-start.4 = (bf16[1,1024,264]{1,2,0:T(8,128)(2,1)S(1)}, bf16[1,1024,264]{1,2,0:T(8,128)(2,1)}, u32[]{:S(2)}) copy-start(bf16[1,1024,264]{1,2,0:T(8,128)(2,1)} %param.17) | copy-start | bytes 1622020
  29.6 17.2 %copy-start.9 = (f32[1,1024]{1,0:T(1,128)S(1)}, f32[1,1024]{1,0:T(1,128)}, u32[]{:S(2)}) copy-start(f32[1,1024]{1,0:T(1,128)} %b_mid.1) | copy-start | bytes 12292
  45.3 1.6 %copy-start.3 = (bf16[1,1024,1024]{2,1,0:T(8,128)(2,1)S(1)}, bf16[1,1024,1024]{2,1,0:T(8,128)(2,1)}, u32[]{:S(2)}) copy-start(bf16[1,1024,1024]{2,1,0:T(8,128)(2,1)} %w_mid.1) | copy-start | bytes 6291460
  53.6 31.3 %copy-start.1 = (f32[32,32,256]{2,1,0:T(8,128)S(1)}, f32[32,32,256]{2,1,0:T(8,128)}, u32[]{:S(2)}) copy-start(f32[32,32,256]{2,1,0:T(8,128)} %state.5) | copy-start | bytes 3145732
  81.3 13.8 %all-to-all-start.2 = ((f32[128,2,128]{2,1,0:T(2,128)}), f32[128,2,128]{2,1,0:T(2,128)S(1)}, u32[]{:S(2)}, u32[]{:S(2)}) async-start(f32[128,2,128]{2,1,0:T(2,128)} %bitcast.7), calls=%async_computation.2 | async-start | bytes 262144 | tf_op jit(solution)/shard_map/all_to_all | solution.py:416

commit v5 on v4

--- a/solution.py
+++ b/solution.py
@@ -153,6 +153,16 @@
         ]
         for i in range(4):
             partial[4 * e + i] = state[4 * e + i] + STEP_DT * smooth_rows(values[i])
+
+
+def dot_parts(hot, values):
+    total = None
+    for _ in range(3):
+        part = values.astype(BF16)
+        term = dot(hot, part)
+        total = term if total is None else total + term
+        values = values - part.astype(F32)
+    return total
 
 
 def owner_ranks(owners):
@@ -220,7 +230,7 @@
         send[part, :] = dot(hot_rows[part, :], columns).astype(BF16)
 
 
-def pack_kernel(inner, sides, y_before, y_after, hot_sides, send_out, send, sems):
+def pack_kernel(inner, sides, y_before, y_after, hot_sides, members, send):
     half = 0.5 * STEP_DT
     size, features = y_before.shape
     columns = jnp.concatenate(
@@ -231,16 +241,10 @@
         ],
         axis=0,
     ).astype(BF16)
-    step = send.shape[0] // sems.shape[0]
-    copies = []
-    for b in range(sems.shape[0]):
+    step = 512
+    for b in range(send.shape[0] // step):
         part = slice(b * step, (b + 1) * step)
         send[part, :] = inner[part, :] + dot(hot_sides[part, :], columns).astype(BF16)
-        copy = pltpu.make_async_copy(send.at[part], send_out.at[part], sems.at[b])
-        copy.start()
-        copies.append(copy)
-    for copy in copies:
-        copy.wait()
 
 
 def as_column(row):
@@ -248,7 +252,7 @@
     return jnp.sum(wide, axis=1, keepdims=True)
 
 
-def prepare_kernel(capacity, element_row, weight, slot_row, places, tiled):
+def prepare_kernel(capacity, size_y, element_row, weight, slot_row, sides, members, ranks, tiled):
     count = element_row.shape[1]
     lane = iota((count, 128), 1)
     for c in range(8):
@@ -261,29 +265,30 @@
         tiled[c] = jnp.where(lane < 64, low, high)
 
     columns = slot_row.shape[1]
-    lane = iota((128, 128), 1)
+    elements_y = size_y // 4
     table = []
     for b in range(columns // 128):
         slots = as_column(slot_row[:, b * 128 : (b + 1) * 128])
-        both = jnp.where(lane == 0, slots // capacity, jnp.where(lane == 1, slots % capacity, 0))
-        table.append(both.astype(F32).astype(BF16))
-    table = jnp.concatenate(table, axis=0)
-    element = as_column(element_row[...])
-    base = (element // 8) * 128 + (element % 8) * 4
-    place = iota((count, columns), 1)
-    slots = jnp.zeros((count, 128), F32)
-    for c in range(16):
-        hot = (place == base + (c // 4) * 32 + c % 4).astype(F32).astype(BF16)
-        both = dot(hot, table)
-        slots = jnp.where(lane == c, both[:, 0:1] * capacity + both[:, 1:2], slots)
-    places[...] = slots.astype(jnp.int32)
+        column = iota((128, 128), 0) + b * 128
+        here = column // size_y % 4 * 4 + column % 4 == lane
+        member = jnp.where(here, slots // capacity, 0).astype(F32)
+        rank = jnp.where(here, slots % capacity, 0).astype(F32)
+        table.append(jnp.concatenate([member, rank], axis=1).astype(BF16))
+    column = iota((128, columns), 1)
+    element = column // (4 * size_y) * elements_y + column % size_y // 4
+    hot = (iota((128, columns), 0) == element).astype(F32).astype(BF16)
+    by_element = dot(hot, jnp.concatenate(table, axis=0)).astype(BF16)
+    hot = (lane == as_column(element_row[...])).astype(F32).astype(BF16)
+    both = dot(hot, by_element)
+    members[...] = both[:, :128].astype(jnp.int32)
+    ranks[...] = both[:, 128:].astype(jnp.int32)
 
 
 def silu_of_half(half):
     return half + half * jnp.tanh(half)
 
 
-def first_kernel(sizes, rows, w_in, b_in, owner_row, block_row, places, out, blocks, w_half):
+def first_kernel(sizes, rows, w_in, b_in, owner_row, block_row, out, blocks, w_half):
     owners = position(owner_row[...], sizes)
     hot, rank = owner_ranks(owners)
     values = block_row[...].astype(F32)
@@ -327,25 +332,25 @@
         out[part, 32:40, :] = tail.astype(BF16)
 
 
-def contribution_kernel(sizes, capacity, answer, places, tiled, owner_row, send):
+def contribution_kernel(sizes, answer, members, ranks, tiled, owner_row, send):
     flux = answer[:, 32:40, :].astype(F32)[:, 0, :].astype(BF16)
     spread = (iota((128, 128), 0) % 8 == iota((128, 128), 1) // 16).astype(F32).astype(BF16)
     lane = iota((128, 128), 1)
+    group = lane // 8
+    owners = position(owner_row[...], sizes)
+    _, rank = owner_ranks(owners)
+    hot = (iota(send.shape, 0) == owners * 2 + rank).astype(F32).astype(BF16)
     total = None
     for c in range(16):
         if c % 2 == 0:
             pair = tiled[c // 2]
             swapped = pltpu.roll(pair, 64, 1)
         weights = jnp.where(lane < 64, *((pair, swapped) if c % 2 == 0 else (swapped, pair)))
-        slots = places[:, c : c + 1]
-        pick = (lane == slots // capacity).astype(F32).astype(BF16)
-        value = jnp.where(lane // 8 == slots % capacity, dot(pick, flux), 0.0)
+        pick = (lane == members[:, c : c + 1]).astype(F32).astype(BF16)
+        value = jnp.where(group == ranks[:, c : c + 1], dot(pick, flux), 0.0)
         term = dot(value.astype(BF16), spread) * weights
         total = term if total is None else total + term
-    owners = position(owner_row[...], sizes)
-    _, rank = owner_ranks(owners)
-    hot = (iota(send.shape, 0) == owners * 2 + rank).astype(F32)
-    send[...] = dot(hot, total, HIGHEST)
+    send[...] = dot_parts(hot, total)
 
 
 def columns_kernel(
@@ -490,6 +495,17 @@
         flops=2 * slots * columns * features,
         scratch=[pltpu.VMEM(state.shape, F32)],
     )
+    members, ranks, tiled = call(
+        lambda *refs: prepare_kernel(capacity, size_y, *refs),
+        [((count, 128), jnp.int32)] * 2 + [((8, count, 128), F32)],
+        intersection_element.reshape(1, count),
+        regrid_weight,
+        slot_row,
+        sides,
+        spaces={3: pl.ANY},
+        nbytes=12 * MIB,
+        flops=2 * 16 * count * columns * 256,
+    )
     (send,) = call(
         pack_kernel,
         [((slots, features), BF16)],
@@ -498,22 +514,13 @@
         y_before,
         y_after,
         hot_sides,
+        members,
         nbytes=4 * MIB,
         flops=2 * slots * 128 * features,
-        out_spaces={0: pl.ANY},
-        scratch=[pltpu.VMEM((slots, features), BF16), pltpu.SemaphoreType.DMA((4,))],
+        spaces={5: pl.ANY},
     )
     received = exchange(send.reshape(devices, capacity, features)).reshape(slots, features)
 
-    places, tiled = call(
-        lambda *refs: prepare_kernel(capacity, *refs),
-        [((count, 128), jnp.int32), ((8, count, 128), F32)],
-        intersection_element.reshape(1, count),
-        regrid_weight,
-        slot_row,
-        nbytes=12 * MIB,
-        flops=2 * 16 * count * columns * 256,
-    )
     hidden = w_in.shape[2]
     owner_row = ocean_owner.reshape(1, count)
     first, blocks = call(
@@ -524,8 +531,6 @@
         bias_in,
         owner_row,
         ocean_block.reshape(1, count),
-        places,
-        spaces={5: pl.ANY},
         nbytes=6 * MIB,
         flops=2 * slots * features * hidden,
         transcendentals=slots * hidden,
@@ -547,10 +552,11 @@
     )
     answer = exchange(answered)
     (ocean_send,) = call(
-        lambda *refs: contribution_kernel(sizes, capacity, *refs),
+        lambda *refs: contribution_kernel(sizes, *refs),
         [((2 * devices, 128), F32)],
         answer,
-        places,
+        members,
+        ranks,
         tiled,
         owner_row,
         nbytes=4 * MIB,

time: 96.3 us -> 95.5 us (level)
  blocking collectives: 25.9 us -> 54.5 us
  waiting for transfers between devices: 24 us -> 6.07 us
  starting transfers between devices: 19 us -> 10 us
  Pallas kernels: 24.9 us -> 22.4 us
    all_to_all x1 -> x2, blocking collectives: 25.9 us -> 54.5 us  [exchange(): return lax.all_to_all(value, AXES, split_axis=0, concat_axis=0, tiled=True)]
    all_to_all x2 -> x1, waiting for transfers between devices: 21.7 us -> 6.06 us  [exchange(): return lax.all_to_all(value, AXES, split_axis=0, concat_axis=0, tiled=True)]
    all_to_all x2 -> x1, starting transfers between devices: 12.6 us -> 3.59 us  [exchange(): return lax.all_to_all(value, AXES, split_axis=0, concat_axis=0, tiled=True)]
    pallas_call x13, Pallas kernels: 24.9 us -> 22.4 us  [call(): pl.pallas_call(kernel, out_shape=[jax.ShapeDtypeStruct(s, d) for s, d in...]
    ppermute x4, waiting for transfers between devices: 2.3 us -> 0.01 us  [shift(): lax.ppermute(value, axis, [(i, (i + step) % size) for i in range(size)])]
  transfers between devices with their start and end apart: 6 -> 5, of which waited for: 3 -> 1; matrix products, arithmetic and copies ran while one was open for 0% -> 0% of each run, Pallas kernels for 13% -> 11%
where the time goes in v5:
time: 95.5 us; the launch traced here: 95.2 us
  blocking collectives  54.5 us (57%)
  Pallas kernels  22.4 us (23%)
  starting transfers between devices  10 us (10%)
  waiting for transfers between devices  6.07 us (6%)
  local copies, waits for them, and re-layouts  1.43 us (1%)
    all_to_all x2, blocking collectives, exchange(): return lax.all_to_all(value, AXES, split_axis=0, concat_axis=0, tiled=True)  54.5 us
    pallas_call x13, Pallas kernels, call(): pl.pallas_call(kernel, out_shape=[jax.ShapeDtypeStruct(s, d) for s, d in...  22.4 us
    ppermute x4, starting transfers between devices, shift(): lax.ppermute(value, axis, [(i, (i + step) % size) for i in range(size)])  6.4 us
    all_to_all x1, waiting for transfers between devices, exchange(): return lax.all_to_all(value, AXES, split_axis=0, concat_axis=0, tiled=True)  6.06 us
    all_to_all x1, starting transfers between devices, exchange(): return lax.all_to_all(value, AXES, split_axis=0, concat_axis=0, tiled=True)  3.59 us
  transfers between devices with their start and end apart: 5, of which 1 were waited for; matrix products, arithmetic and copies ran while one was open for 0% of the time, Pallas kernels for 11%

profile of v5, /device:TPU:1, one launch (start us, length us, event | category | flops | bytes accessed | tf_op | source)
XLA Modules:
  0.0 95.2 jit_solution(4026879777242678234)
XLA Ops:
  0.6 0.0 copy-start
  0.6 1.2 %copy-done = f32[32,32,256]{2,1,0:T(8,128)S(1)} copy-done((f32[32,32,256]{2,1,0:T(8,128)S(1)}, f32[32,32,256]{2,1,0:T(8,128)}, u32[]{:S(2)}) %copy-start) | copy-done | bytes 1048600
  1.9 0.3 shard_map.122
  2.1 2.2 %collective-permute-start = (f32[32,256]{1,0:T(8,128)S(1)}, f32[32,256]{1,0:T(8,128)S(1)}, u32[]{:S(2)}, u32[]{:S(2)}) collective-permute-start(f32[32,256]{1,0:T(8,128)S(1)} %get-tuple-element.21), channel_id=1, source_target_pairs={{0,32},{32,64},{64,96},{96,0},{1,33},{33,65},{65,97},{97,1},{2,34}... | collective-permute-start | bytes 98312 | tf_op jit(solution)/shard_map/ppermute | solution.py:417
  4.3 1.5 %collective-permute-start.1 = (f32[32,256]{1,0:T(8,128)S(1)}, f32[32,256]{1,0:T(8,128)S(1)}, u32[]{:S(2)}, u32[]{:S(2)}) collective-permute-start(f32[32,256]{1,0:T(8,128)S(1)} %get-tuple-element.20.token), channel_id=1, source_target_pairs={{0,96},{32,0},{64,32},{96,64},{1,97},{33,1},{65,33},{97,65},{2,98}... | collective-permute-start | bytes 98312 | tf_op jit(solution)/shard_map/ppermute | solution.py:417
  5.8 1.7 %shard_map.123.partial = f32[32,32,256]{2,1,0:T(8,128)S(1)} custom-call(f32[32,32,256]{2,1,0:T(8,128)S(1)} %copy-done, f32[32,256]{1,0:T(8,128)S(1)} %get-tuple-element.20.token), custom_call_target="tpu_custom_call" | custom-call | flops 67108864 | bytes 8388608 | tf_op jit(solution)/shard_map/pallas_call | solution.py:397
  7.5 1.4 %shard_map.124 = (s32[1,1024]{1,0:T(1,128)S(1)}, bf16[2048,1024]{1,0:T(8,128)(2,1)S(1)}, bf16[2048,128]{1,0:T(8,128)(2,1)S(1)}) custom-call(s32[1,1024]{1,0:T(1,128)S(1)} %bitcast.13), custom_call_target="tpu_custom_call" | custom-call | flops 67108864 | bytes 8388608 | tf_op jit(solution)/shard_map/pallas_call | solution.py:397
  9.0 2.7 %collective-permute-start.2 = (f32[32,256]{1,0:T(8,128)S(1)}, f32[32,256]{1,0:T(8,128)S(1)}, u32[]{:S(2)}, u32[]{:S(2)}) collective-permute-start(f32[32,256]{1,0:T(8,128)S(1)} %get-tuple-element.28), channel_id=1, source_target_pairs={{0,1},{1,2},{2,3},{3,4},{4,5},{5,6},{6,7},{7,8},{8,9},{9,10},{10,1... | collective-permute-start | bytes 98312 | tf_op jit(solution)/shard_map/ppermute | solution.py:417
  11.7 1.3 %shard_map.125 = (bf16[2048,256]{1,0:T(8,128)(2,1)S(1)}, f32[64,256]{1,0:T(8,128)S(1)}) custom-call(f32[32,32,256]{2,1,0:T(8,128)S(1)} %shard_map.123.partial, f32[32,256]{1,0:T(8,128)S(1)} %collective-permute-done.x_before, f32[32,256]{1,0:T(8,128)S(1)} %collective-permute-done.1.x_after, bf16[2048,1024]{1,0:T(8,128)(2,1)S(1)} %get-tuple-element.22.hot_rows), custom_call_target="tpu_custom_call" | custom-call | flops 1073741824 | bytes 8388608 | tf_op jit(solution)/shard_map/pallas_call | solution.py:397
  13.0 2.3 %shard_map.127 = (s32[128,128]{1,0:T(8,128)S(1)}, s32[128,128]{1,0:T(8,128)S(1)}, f32[8,128,128]{2,1,0:T(8,128)S(1)}) custom-call(s32[1,128]{1,0:T(1,128)S(1)} %bitcast.14, f32[128,256]{1,0:T(8,128)S(1)} %copy-done.6, s32[1,1024]{1,0:T(1,128)S(1)} %get-tuple-element.27.slot_row.refs_2_, f32[64,256]{1,0:T(8,128)S(1)} %get-tuple-element.24.refs_3_.sides), custom_call_target="tpu_custom_call" | custom-call | flops 1073741824 | bytes 12582912 | tf_op jit(solution)/shard_map/pallas_call | solution.py:397
  15.4 0.0 copy-start.2
  15.4 0.4 shard_map.128
  15.8 28.6 %all_to_all.15 = bf16[128,16,256]{2,1,0:T(8,128)(2,1)S(1)} all-to-all(bf16[128,16,256]{2,1,0:T(8,128)(2,1)S(1)} %bitcast.8), channel_id=1, replica_groups=mesh['gx'=4,'gy'=32] {'gy','gx'}, dimensions={0} | all-to-all | bytes 2097152 | tf_op jit(solution)/shard_map/all_to_all | solution.py:421
  44.5 1.5 %shard_map.129 = (bf16[2048,1024]{1,0:T(8,128)(2,1)S(1)}, f32[128,128]{1,0:T(8,128)S(1)}) custom-call(bf16[2048,256]{1,0:T(8,128)(2,1)S(1)} %bitcast.9, bf16[1,256,1024]{2,1,0:T(8,128)(2,1)S(1)} %copy-done.5, f32[1,1024]{1,0:T(1,128)S(1)} %copy-done.8, s32[1,128]{1,0:T(1,128)S(1)} %bitcast.10, s32[1,128]{1,0:T(1,128)S(1)} %bitcast.15), custom_call_target="tpu_custom_call" | custom-call | flops 1073741824 | bytes 6291456 | tf_op jit(solution)/shard_map/pallas_call | solution.py:397
  46.0 0.1 copy-done.3
  46.1 0.1 copy-done.4
  46.2 6.7 %shard_map.130 = bf16[128,40,128]{2,1,0:T(8,128)(2,1)S(1)} custom-call(bf16[2048,1024]{1,0:T(8,128)(2,1)S(1)} %get-tuple-element.32.first, bf16[1,1024,1024]{2,1,0:T(8,128)(2,1)S(1)} %copy-done.3, f32[1,1024]{1,0:T(1,128)S(1)} %copy-done.9, bf16[1,264,1024]{2,1,0:T(8,128)(2,1)S(1)} %bitcast.12, f32[128,128]{1,0:T(8,128)S(1)} %get-tuple-element.33.blocks), custom_call_target="tpu_custom_call" | custom-call | flops 5905580032 | bytes 8388608 | tf_op jit(solution)/shard_map/pallas_call | solution.py:397
  52.9 25.9 %all_to_all.16.refs_0_.answer = bf16[128,40,128]{2,1,0:T(8,128)(2,1)S(1)} all-to-all(bf16[128,40,128]{2,1,0:T(8,128)(2,1)S(1)} %shard_map.130), channel_id=1, replica_groups=mesh['gx'=4,'gy'=32] {'gy','gx'}, dimensions={0} | all-to-all | bytes 2621440 | tf_op jit(solution)/shard_map/all_to_all | solution.py:421
  78.7 1.8 %shard_map.131.token = f32[256,128]{1,0:T(8,128)} custom-call(bf16[128,40,128]{2,1,0:T(8,128)(2,1)S(1)} %all_to_all.16.refs_0_.answer, s32[128,128]{1,0:T(8,128)S(1)} %get-tuple-element.31.members.refs_1_, s32[128,128]{1,0:T(8,128)S(1)} %get-tuple-element.34.refs_2_, f32[8,128,128]{2,1,0:T(8,128)S(1)} %get-tuple-element.35.refs_3_, s32[1,128]{1,0:T(1,128)S(1)} %bitcast.11), custom_call_target="tpu_custom_call" | custom-call | flops 134217728 | bytes 4194304 | tf_op jit(solution)/shard_map/pallas_call | solution.py:397
  80.5 3.6 %all-to-all-start.2 = ((f32[128,2,128]{2,1,0:T(2,128)}), f32[128,2,128]{2,1,0:T(2,128)S(1)}, u32[]{:S(2)}, u32[]{:S(2)}) async-start(f32[128,2,128]{2,1,0:T(2,128)} %bitcast.7), calls=%async_computation.2 | async-start | bytes 262144 | tf_op jit(solution)/shard_map/all_to_all | solution.py:421
  84.1 1.7 %shard_map.132.partial = f32[32,32,256]{2,1,0:T(8,128)S(1)} custom-call(f32[32,32,256]{2,1,0:T(8,128)S(1)} %copy-done.1, f32[256,128]{1,0:T(8,128)} %shard_map.131.token), custom_call_target="tpu_custom_call" | custom-call | flops 67108864 | bytes 8388608 | tf_op jit(solution)/shard_map/pallas_call | solution.py:397
  85.8 2.5 %shard_map.133 = (f32[32,32,256]{2,1,0:T(8,128)}, f32[2,16,128]{2,1,0:T(8,128)S(1)}) custom-call(bf16[128,40,128]{2,1,0:T(8,128)(2,1)S(1)} %all_to_all.16.refs_0_.answer, s32[1,1024]{1,0:T(1,128)S(1)} %get-tuple-element.27.slot_row.refs_2_, f32[32,32,256]{2,1,0:T(8,128)S(1)} %shard_map.132.partial, f32[32,256]{1,0:T(8,128)S(1)} %collective-permute-done.x_before, ...), custom_call_target="tpu_custom_call" | custom-call | flops 1073741824 | bytes 12582912 | tf_op jit(solution)/shard_map/pallas_call | solution.py:397
  88.3 6.1 %all-to-all-done.2.received = f32[128,2,128]{2,1,0:T(2,128)S(1)} async-done(((f32[128,2,128]{2,1,0:T(2,128)}), f32[128,2,128]{2,1,0:T(2,128)S(1)}, u32[]{:S(2)}, u32[]{:S(2)}) %all-to-all-start.2) | async-done | bytes 131104 | tf_op jit(solution)/shard_map/all_to_all | solution.py:421
  94.3 0.9 shard_map.134
  (25 shorter events, 0.1 us)
Async XLA Ops:
  0.6 1.2 %copy-start = (f32[32,32,256]{2,1,0:T(8,128)S(1)}, f32[32,32,256]{2,1,0:T(8,128)}, u32[]{:S(2)}) copy-start(f32[32,32,256]{2,1,0:T(8,128)} %state.5) | copy-start | bytes 3145732
  1.9 5.6 %copy-start.7 = (s32[1024,1]{0,1:T(1,128)S(1)}, s32[1024,1]{0,1:T(1,128)}, u32[]{:S(2)}) copy-start(s32[1024,1]{0,1:T(1,128)} %param.12) | copy-start | bytes 12292
  2.1 6.8 %collective-permute-start = (f32[32,256]{1,0:T(8,128)S(1)}, f32[32,256]{1,0:T(8,128)S(1)}, u32[]{:S(2)}, u32[]{:S(2)}) collective-permute-start(f32[32,256]{1,0:T(8,128)S(1)} %get-tuple-element.21), channel_id=1, source_target_pairs={{0,32},{32,64},{64,96},{96,0},{1,33},{33,65},{65,97},{97,1},{2,34}... | collective-permute-start | bytes 98312 | tf_op jit(solution)/shard_map/ppermute | solution.py:417
  4.3 4.6 %collective-permute-start.1 = (f32[32,256]{1,0:T(8,128)S(1)}, f32[32,256]{1,0:T(8,128)S(1)}, u32[]{:S(2)}, u32[]{:S(2)}) collective-permute-start(f32[32,256]{1,0:T(8,128)S(1)} %get-tuple-element.20.token), channel_id=1, source_target_pairs={{0,96},{32,0},{64,32},{96,64},{1,97},{33,1},{65,33},{97,65},{2,98}... | collective-permute-start | bytes 98312 | tf_op jit(solution)/shard_map/ppermute | solution.py:417
  9.0 6.4 %collective-permute-start.2 = (f32[32,256]{1,0:T(8,128)S(1)}, f32[32,256]{1,0:T(8,128)S(1)}, u32[]{:S(2)}, u32[]{:S(2)}) collective-permute-start(f32[32,256]{1,0:T(8,128)S(1)} %get-tuple-element.28), channel_id=1, source_target_pairs={{0,1},{1,2},{2,3},{3,4},{4,5},{5,6},{6,7},{7,8},{8,9},{9,10},{10,1... | collective-permute-start | bytes 98312 | tf_op jit(solution)/shard_map/ppermute | solution.py:417
  11.6 3.7 %collective-permute-start.3 = (f32[32,256]{1,0:T(8,128)S(1)}, f32[32,256]{1,0:T(8,128)S(1)}, u32[]{:S(2)}, u32[]{:S(2)}) collective-permute-start(f32[32,256]{1,0:T(8,128)S(1)} %get-tuple-element.29), channel_id=1, source_target_pairs={{0,31},{1,0},{2,1},{3,2},{4,3},{5,4},{6,5},{7,6},{8,7},{9,8},{10,9... | collective-permute-start | bytes 98312 | tf_op jit(solution)/shard_map/ppermute | solution.py:417
  11.7 1.3 %copy-start.6 = (f32[128,256]{1,0:T(8,128)S(1)}, f32[128,256]{1,0:T(8,128)}, u32[]{:S(2)}) copy-start(f32[128,256]{1,0:T(8,128)} %refs_1_.2) | copy-start | bytes 393220
  11.7 1.3 %copy-start.10 = (s32[128]{0:T(128)S(1)}, s32[128]{0:T(128)}, u32[]{:S(2)}) copy-start(s32[128]{0:T(128)} %param.18) | copy-start | bytes 1540
  15.4 29.1 %copy-start.2 = (s32[128,1]{0,1:T(1,128)S(1)}, s32[128,1]{0,1:T(1,128)}, u32[]{:S(2)}) copy-start(s32[128,1]{0,1:T(1,128)} %param.19) | copy-start | bytes 1540
  15.4 29.1 %copy-start.5 = (bf16[1,256,1024]{2,1,0:T(8,128)(2,1)S(1)}, bf16[1,256,1024]{2,1,0:T(8,128)(2,1)}, u32[]{:S(2)}) copy-start(bf16[1,256,1024]{2,1,0:T(8,128)(2,1)} %refs_1_.3) | copy-start | bytes 1572868
  15.4 29.1 %copy-start.8 = (f32[1,1024]{1,0:T(1,128)S(1)}, f32[1,1024]{1,0:T(1,128)}, u32[]{:S(2)}) copy-start(f32[1,1024]{1,0:T(1,128)} %refs_2_.1) | copy-start | bytes 12292
  15.4 29.1 %copy-start.11 = (s32[128]{0:T(128)S(1)}, s32[128]{0:T(128)}, u32[]{:S(2)}) copy-start(s32[128]{0:T(128)} %param.20) | copy-start | bytes 1540
  44.5 1.6 %copy-start.3 = (bf16[1,1024,1024]{2,1,0:T(8,128)(2,1)S(1)}, bf16[1,1024,1024]{2,1,0:T(8,128)(2,1)}, u32[]{:S(2)}) copy-start(bf16[1,1024,1024]{2,1,0:T(8,128)(2,1)} %w_mid.1) | copy-start | bytes 6291460
  44.5 1.7 %copy-start.4 = (bf16[1,1024,264]{1,2,0:T(8,128)(2,1)S(1)}, bf16[1,1024,264]{1,2,0:T(8,128)(2,1)}, u32[]{:S(2)}) copy-start(bf16[1,1024,264]{1,2,0:T(8,128)(2,1)} %param.17) | copy-start | bytes 1622020
  44.5 1.7 %copy-start.9 = (f32[1,1024]{1,0:T(1,128)S(1)}, f32[1,1024]{1,0:T(1,128)}, u32[]{:S(2)}) copy-start(f32[1,1024]{1,0:T(1,128)} %b_mid.1) | copy-start | bytes 12292
  52.9 31.3 %copy-start.1 = (f32[32,32,256]{2,1,0:T(8,128)S(1)}, f32[32,32,256]{2,1,0:T(8,128)}, u32[]{:S(2)}) copy-start(f32[32,32,256]{2,1,0:T(8,128)} %state.5) | copy-start | bytes 3145732
  80.5 13.8 %all-to-all-start.2 = ((f32[128,2,128]{2,1,0:T(2,128)}), f32[128,2,128]{2,1,0:T(2,128)S(1)}, u32[]{:S(2)}, u32[]{:S(2)}) async-start(f32[128,2,128]{2,1,0:T(2,128)} %bitcast.7), calls=%async_computation.2 | async-start | bytes 262144 | tf_op jit(solution)/shard_map/all_to_all | solution.py:421

commit v6 on v5

--- a/solution.py
+++ b/solution.py
@@ -305,6 +305,10 @@
         out[part, :] = silu_of_half(dot(rows[part, :], w_half[...]) + b_half).astype(BF16)
 
 
+def message_parts():
+    return [((4 * h + q) * 128, 4 * q, 128 * h) for h in range(2) for q in range(4)]
+
+
 def dot_by_output(a, b):
     return lax.dot_general(a, b, (((1,), (1,)), ((), ())), preferred_element_type=F32)
 
@@ -314,26 +318,28 @@
     sources = step // 16
     lane = iota((step, 128), 1)
     own = lane // 8 == iota((step, 128), 0) % 16
-    line = iota((sources, 8, 128), 1)
+    line = iota((sources, 4, 128), 1)
     w_half[...] = w_mid[0] * jnp.asarray(0.5, BF16)
     w_flux[...] = jnp.concatenate([w_last[0, 256:264, :].astype(F32)] * 16).astype(BF16)
     b_half = 0.5 * b_mid[...]
     for b in range(first.shape[0] // step):
         hidden = dot(first[b * step : (b + 1) * step, :], w_half[...])
         hidden = silu_of_half(hidden + b_half).astype(BF16)
-        tends = dot_by_output(hidden, w_last[0, 0:256, :]).astype(BF16)
+        tends = dot_by_output(hidden, w_last[0, 0:256, :]).reshape(sources, 16, 256)
         part = slice(b * sources, (b + 1) * sources)
-        out[part, 0:16, :] = tends[:, :128].reshape(sources, 16, 128)
-        out[part, 16:32, :] = tends[:, 128:].reshape(sources, 16, 128)
+        for place, slot, feature in message_parts():
+            out[part, :, place : place + 128] = tends[
+                :, slot : slot + 4, feature : feature + 128
+            ].astype(BF16)
         flux = jnp.where(own, dot_by_output(hidden, w_flux[...]), 0.0)
         flux = jnp.sum(flux.reshape(sources, 16, 128), axis=1, keepdims=True)
         names = blocks[part, :].reshape(sources, 1, 128)
         tail = jnp.where(line == 0, flux, jnp.where(line == 1, names, 0.0))
-        out[part, 32:40, :] = tail.astype(BF16)
+        out[part, :, 1024:1152] = tail.astype(BF16)
 
 
 def contribution_kernel(sizes, answer, members, ranks, tiled, owner_row, send):
-    flux = answer[:, 32:40, :].astype(F32)[:, 0, :].astype(BF16)
+    flux = answer[:, :, 1024:1152].astype(F32)[:, 0, :].astype(BF16)
     spread = (iota((128, 128), 0) % 8 == iota((128, 128), 1) // 16).astype(F32).astype(BF16)
     lane = iota((128, 128), 1)
     group = lane // 8
@@ -364,6 +370,7 @@
     new_state,
     sums,
     rows,
+    wide,
     advanced,
 ):
     sources = answer.shape[0]
@@ -373,8 +380,11 @@
     half = 0.5 * STEP_DT
     advanced[:, 0, :] = advanced[:, 0, :] + half * y_before[...]
     advanced[:, size_y - 1, :] = advanced[:, size_y - 1, :] + half * y_after[...]
-    rows[:, 0:128] = answer[:, 0:16, :].reshape(slots, 128)
-    rows[:, 128:256] = answer[:, 16:32, :].reshape(slots, 128)
+    for place, slot, feature in message_parts():
+        wide[:, slot : slot + 4, feature : feature + 128] = answer[
+            :, :, place : place + 128
+        ].astype(F32)
+    rows[...] = wide[...].reshape(slots, features).astype(BF16)
     step = 128
     lines = step // size_y
     for b in range(size_x // lines):
@@ -382,7 +392,7 @@
         tends = dot(hot.astype(F32).astype(BF16), rows[...])
         part = slice(b * lines, (b + 1) * lines)
         new_state[part] = advanced[part] + tends.reshape(lines, size_y, features)
-    names = answer[:, 32:40, :].astype(F32)[:, 1, :]
+    names = answer[:, :, 1024:1152].astype(F32)[:, 1, :]
     lane = iota((sources, 128), 1)
     for j in range(2):
         hot = (names[:, j : j + 1].astype(jnp.int32) == lane).astype(F32)
@@ -538,7 +548,7 @@
     )
     (answered,) = call(
         second_kernel,
-        [((devices, 40, 128), BF16)],
+        [((devices, 4, 1152), BF16)],
         first,
         w_mid,
         bias_mid,
@@ -576,7 +586,11 @@
         y_after,
         nbytes=12 * MIB,
         flops=2 * slots * columns * features,
-        scratch=[pltpu.VMEM((slots, features), BF16), pltpu.VMEM(state.shape, F32)],
+        scratch=[
+            pltpu.VMEM((slots, features), BF16),
+            pltpu.VMEM((devices, 16, features), F32),
+            pltpu.VMEM(state.shape, F32),
+        ],
     )
     (ocean_total,) = call(
         ocean_kernel, [((OB_DEV, 128), F32)], ocean_got, sums, nbytes=MIB, flops=MIB

time: 95.5 us -> 94.1 us (0.985)
  blocking collectives: 54.5 us -> 53.1 us
    all_to_all x2, blocking collectives: 54.5 us -> 53.1 us  [exchange(): return lax.all_to_all(value, AXES, split_axis=0, concat_axis=0, tiled=True)]
  transfers between devices with their start and end apart: 5 -> 5, of which waited for: 1 -> 1; matrix products, arithmetic and copies ran while one was open for 0% -> 0% of each run, Pallas kernels for 11% -> 12%
where the time goes in v6:
time: 94.1 us; the launch traced here: 93.8 us
  blocking collectives  53.1 us (56%)
  Pallas kernels  22.6 us (24%)
  starting transfers between devices  10 us (11%)
  waiting for transfers between devices  5.84 us (6%)
  local copies, waits for them, and re-layouts  1.43 us (2%)
    all_to_all x2, blocking collectives, exchange(): return lax.all_to_all(value, AXES, split_axis=0, concat_axis=0, tiled=True)  53.1 us
    pallas_call x13, Pallas kernels, call(): pl.pallas_call(kernel, out_shape=[jax.ShapeDtypeStruct(s, d) for s, d in...  22.6 us
    ppermute x4, starting transfers between devices, shift(): lax.ppermute(value, axis, [(i, (i + step) % size) for i in range(size)])  6.4 us
    all_to_all x1, waiting for transfers between devices, exchange(): return lax.all_to_all(value, AXES, split_axis=0, concat_axis=0, tiled=True)  5.83 us
    all_to_all x1, starting transfers between devices, exchange(): return lax.all_to_all(value, AXES, split_axis=0, concat_axis=0, tiled=True)  3.6 us
  transfers between devices with their start and end apart: 5, of which 1 were waited for; matrix products, arithmetic and copies ran while one was open for 0% of the time, Pallas kernels for 12%

profile of v6, /device:TPU:1, one launch (start us, length us, event | category | flops | bytes accessed | tf_op | source)
XLA Modules:
  0.0 93.8 jit_solution(16149903988210678203)
XLA Ops:
  0.6 0.0 copy-start
  0.6 1.2 %copy-done = f32[32,32,256]{2,1,0:T(8,128)S(1)} copy-done((f32[32,32,256]{2,1,0:T(8,128)S(1)}, f32[32,32,256]{2,1,0:T(8,128)}, u32[]{:S(2)}) %copy-start) | copy-done | bytes 1048600
  1.9 0.3 shard_map.122
  2.1 2.2 %collective-permute-start = (f32[32,256]{1,0:T(8,128)S(1)}, f32[32,256]{1,0:T(8,128)S(1)}, u32[]{:S(2)}, u32[]{:S(2)}) collective-permute-start(f32[32,256]{1,0:T(8,128)S(1)} %get-tuple-element.21), channel_id=1, source_target_pairs={{0,32},{32,64},{64,96},{96,0},{1,33},{33,65},{65,97},{97,1},{2,34}... | collective-permute-start | bytes 98312 | tf_op jit(solution)/shard_map/ppermute | solution.py:427
  4.3 1.5 %collective-permute-start.1 = (f32[32,256]{1,0:T(8,128)S(1)}, f32[32,256]{1,0:T(8,128)S(1)}, u32[]{:S(2)}, u32[]{:S(2)}) collective-permute-start(f32[32,256]{1,0:T(8,128)S(1)} %get-tuple-element.20.token), channel_id=1, source_target_pairs={{0,96},{32,0},{64,32},{96,64},{1,97},{33,1},{65,33},{97,65},{2,98}... | collective-permute-start | bytes 98312 | tf_op jit(solution)/shard_map/ppermute | solution.py:427
  5.8 1.7 %shard_map.123.partial = f32[32,32,256]{2,1,0:T(8,128)S(1)} custom-call(f32[32,32,256]{2,1,0:T(8,128)S(1)} %copy-done, f32[32,256]{1,0:T(8,128)S(1)} %get-tuple-element.20.token), custom_call_target="tpu_custom_call" | custom-call | flops 67108864 | bytes 8388608 | tf_op jit(solution)/shard_map/pallas_call | solution.py:407
  7.5 1.4 %shard_map.124 = (s32[1,1024]{1,0:T(1,128)S(1)}, bf16[2048,1024]{1,0:T(8,128)(2,1)S(1)}, bf16[2048,128]{1,0:T(8,128)(2,1)S(1)}) custom-call(s32[1,1024]{1,0:T(1,128)S(1)} %bitcast.13), custom_call_target="tpu_custom_call" | custom-call | flops 67108864 | bytes 8388608 | tf_op jit(solution)/shard_map/pallas_call | solution.py:407
  9.0 2.7 %collective-permute-start.2 = (f32[32,256]{1,0:T(8,128)S(1)}, f32[32,256]{1,0:T(8,128)S(1)}, u32[]{:S(2)}, u32[]{:S(2)}) collective-permute-start(f32[32,256]{1,0:T(8,128)S(1)} %get-tuple-element.28), channel_id=1, source_target_pairs={{0,1},{1,2},{2,3},{3,4},{4,5},{5,6},{6,7},{7,8},{8,9},{9,10},{10,1... | collective-permute-start | bytes 98312 | tf_op jit(solution)/shard_map/ppermute | solution.py:427
  11.7 1.3 %shard_map.125 = (bf16[2048,256]{1,0:T(8,128)(2,1)S(1)}, f32[64,256]{1,0:T(8,128)S(1)}) custom-call(f32[32,32,256]{2,1,0:T(8,128)S(1)} %shard_map.123.partial, f32[32,256]{1,0:T(8,128)S(1)} %collective-permute-done.x_before, f32[32,256]{1,0:T(8,128)S(1)} %collective-permute-done.1.x_after, bf16[2048,1024]{1,0:T(8,128)(2,1)S(1)} %get-tuple-element.22.hot_rows), custom_call_target="tpu_custom_call" | custom-call | flops 1073741824 | bytes 8388608 | tf_op jit(solution)/shard_map/pallas_call | solution.py:407
  13.0 2.3 %shard_map.127 = (s32[128,128]{1,0:T(8,128)S(1)}, s32[128,128]{1,0:T(8,128)S(1)}, f32[8,128,128]{2,1,0:T(8,128)S(1)}) custom-call(s32[1,128]{1,0:T(1,128)S(1)} %bitcast.14, f32[128,256]{1,0:T(8,128)S(1)} %copy-done.6, s32[1,1024]{1,0:T(1,128)S(1)} %get-tuple-element.27.slot_row.refs_2_, f32[64,256]{1,0:T(8,128)S(1)} %get-tuple-element.24.refs_3_.sides), custom_call_target="tpu_custom_call" | custom-call | flops 1073741824 | bytes 12582912 | tf_op jit(solution)/shard_map/pallas_call | solution.py:407
  15.4 0.0 copy-start.2
  15.4 0.4 shard_map.128
  15.8 28.6 %all_to_all.15 = bf16[128,16,256]{2,1,0:T(8,128)(2,1)S(1)} all-to-all(bf16[128,16,256]{2,1,0:T(8,128)(2,1)S(1)} %bitcast.8), channel_id=1, replica_groups=mesh['gx'=4,'gy'=32] {'gy','gx'}, dimensions={0} | all-to-all | bytes 2097152 | tf_op jit(solution)/shard_map/all_to_all | solution.py:431
  44.5 1.5 %shard_map.129 = (bf16[2048,1024]{1,0:T(8,128)(2,1)S(1)}, f32[128,128]{1,0:T(8,128)S(1)}) custom-call(bf16[2048,256]{1,0:T(8,128)(2,1)S(1)} %bitcast.9, bf16[1,256,1024]{2,1,0:T(8,128)(2,1)S(1)} %copy-done.5, f32[1,1024]{1,0:T(1,128)S(1)} %copy-done.8, s32[1,128]{1,0:T(1,128)S(1)} %bitcast.10, s32[1,128]{1,0:T(1,128)S(1)} %bitcast.15), custom_call_target="tpu_custom_call" | custom-call | flops 1073741824 | bytes 6291456 | tf_op jit(solution)/shard_map/pallas_call | solution.py:407
  46.0 0.1 copy-done.3
  46.1 0.1 copy-done.4
  46.2 6.7 %shard_map.130 = bf16[128,4,1152]{2,1,0:T(4,128)(2,1)S(1)} custom-call(bf16[2048,1024]{1,0:T(8,128)(2,1)S(1)} %get-tuple-element.32.first, bf16[1,1024,1024]{2,1,0:T(8,128)(2,1)S(1)} %copy-done.3, f32[1,1024]{1,0:T(1,128)S(1)} %copy-done.9, bf16[1,264,1024]{2,1,0:T(8,128)(2,1)S(1)} %bitcast.12, f32[128,128]{1,0:T(8,128)S(1)} %get-tuple-element.33.blocks), custom_call_target="tpu_custom_call" | custom-call | flops 5905580032 | bytes 8388608 | tf_op jit(solution)/shard_map/pallas_call | solution.py:407
  52.9 24.5 %all_to_all.16.refs_0_.answer = bf16[128,4,1152]{2,1,0:T(4,128)(2,1)S(1)} all-to-all(bf16[128,4,1152]{2,1,0:T(4,128)(2,1)S(1)} %shard_map.130), channel_id=1, replica_groups=mesh['gx'=4,'gy'=32] {'gy','gx'}, dimensions={0} | all-to-all | bytes 2359296 | tf_op jit(solution)/shard_map/all_to_all | solution.py:431
  77.3 1.8 %shard_map.131.token = f32[256,128]{1,0:T(8,128)} custom-call(bf16[128,4,1152]{2,1,0:T(4,128)(2,1)S(1)} %all_to_all.16.refs_0_.answer, s32[128,128]{1,0:T(8,128)S(1)} %get-tuple-element.31.members.refs_1_, s32[128,128]{1,0:T(8,128)S(1)} %get-tuple-element.34.refs_2_, f32[8,128,128]{2,1,0:T(8,128)S(1)} %get-tuple-element.35.refs_3_, s32[1,128]{1,0:T(1,128)S(1)} %bitcast.11), custom_call_target="tpu_custom_call" | custom-call | flops 134217728 | bytes 4194304 | tf_op jit(solution)/shard_map/pallas_call | solution.py:407
  79.1 3.6 %all-to-all-start.2 = ((f32[128,2,128]{2,1,0:T(2,128)}), f32[128,2,128]{2,1,0:T(2,128)S(1)}, u32[]{:S(2)}, u32[]{:S(2)}) async-start(f32[128,2,128]{2,1,0:T(2,128)} %bitcast.7), calls=%async_computation.2 | async-start | bytes 262144 | tf_op jit(solution)/shard_map/all_to_all | solution.py:431
  82.7 1.7 %shard_map.132.partial = f32[32,32,256]{2,1,0:T(8,128)S(1)} custom-call(f32[32,32,256]{2,1,0:T(8,128)S(1)} %copy-done.1, f32[256,128]{1,0:T(8,128)} %shard_map.131.token), custom_call_target="tpu_custom_call" | custom-call | flops 67108864 | bytes 8388608 | tf_op jit(solution)/shard_map/pallas_call | solution.py:407
  84.4 2.7 %shard_map.133 = (f32[32,32,256]{2,1,0:T(8,128)}, f32[2,16,128]{2,1,0:T(8,128)S(1)}) custom-call(bf16[128,4,1152]{2,1,0:T(4,128)(2,1)S(1)} %all_to_all.16.refs_0_.answer, s32[1,1024]{1,0:T(1,128)S(1)} %get-tuple-element.27.slot_row.refs_2_, f32[32,32,256]{2,1,0:T(8,128)S(1)} %shard_map.132.partial, f32[32,256]{1,0:T(8,128)S(1)} %collective-permute-done.x_before, ...), custom_call_target="tpu_custom_call" | custom-call | flops 1073741824 | bytes 12582912 | tf_op jit(solution)/shard_map/pallas_call | solution.py:407
  87.1 5.8 %all-to-all-done.2.received = f32[128,2,128]{2,1,0:T(2,128)S(1)} async-done(((f32[128,2,128]{2,1,0:T(2,128)}), f32[128,2,128]{2,1,0:T(2,128)S(1)}, u32[]{:S(2)}, u32[]{:S(2)}) %all-to-all-start.2) | async-done | bytes 131104 | tf_op jit(solution)/shard_map/all_to_all | solution.py:431
  92.9 0.9 shard_map.134
  (25 shorter events, 0.1 us)
Async XLA Ops:
  0.6 1.2 %copy-start = (f32[32,32,256]{2,1,0:T(8,128)S(1)}, f32[32,32,256]{2,1,0:T(8,128)}, u32[]{:S(2)}) copy-start(f32[32,32,256]{2,1,0:T(8,128)} %state.5) | copy-start | bytes 3145732
  1.9 5.6 %copy-start.7 = (s32[1024,1]{0,1:T(1,128)S(1)}, s32[1024,1]{0,1:T(1,128)}, u32[]{:S(2)}) copy-start(s32[1024,1]{0,1:T(1,128)} %param.12) | copy-start | bytes 12292
  2.1 6.8 %collective-permute-start = (f32[32,256]{1,0:T(8,128)S(1)}, f32[32,256]{1,0:T(8,128)S(1)}, u32[]{:S(2)}, u32[]{:S(2)}) collective-permute-start(f32[32,256]{1,0:T(8,128)S(1)} %get-tuple-element.21), channel_id=1, source_target_pairs={{0,32},{32,64},{64,96},{96,0},{1,33},{33,65},{65,97},{97,1},{2,34}... | collective-permute-start | bytes 98312 | tf_op jit(solution)/shard_map/ppermute | solution.py:427
  4.3 4.6 %collective-permute-start.1 = (f32[32,256]{1,0:T(8,128)S(1)}, f32[32,256]{1,0:T(8,128)S(1)}, u32[]{:S(2)}, u32[]{:S(2)}) collective-permute-start(f32[32,256]{1,0:T(8,128)S(1)} %get-tuple-element.20.token), channel_id=1, source_target_pairs={{0,96},{32,0},{64,32},{96,64},{1,97},{33,1},{65,33},{97,65},{2,98}... | collective-permute-start | bytes 98312 | tf_op jit(solution)/shard_map/ppermute | solution.py:427
  9.0 6.4 %collective-permute-start.2 = (f32[32,256]{1,0:T(8,128)S(1)}, f32[32,256]{1,0:T(8,128)S(1)}, u32[]{:S(2)}, u32[]{:S(2)}) collective-permute-start(f32[32,256]{1,0:T(8,128)S(1)} %get-tuple-element.28), channel_id=1, source_target_pairs={{0,1},{1,2},{2,3},{3,4},{4,5},{5,6},{6,7},{7,8},{8,9},{9,10},{10,1... | collective-permute-start | bytes 98312 | tf_op jit(solution)/shard_map/ppermute | solution.py:427
  11.6 3.7 %collective-permute-start.3 = (f32[32,256]{1,0:T(8,128)S(1)}, f32[32,256]{1,0:T(8,128)S(1)}, u32[]{:S(2)}, u32[]{:S(2)}) collective-permute-start(f32[32,256]{1,0:T(8,128)S(1)} %get-tuple-element.29), channel_id=1, source_target_pairs={{0,31},{1,0},{2,1},{3,2},{4,3},{5,4},{6,5},{7,6},{8,7},{9,8},{10,9... | collective-permute-start | bytes 98312 | tf_op jit(solution)/shard_map/ppermute | solution.py:427
  11.7 1.3 %copy-start.6 = (f32[128,256]{1,0:T(8,128)S(1)}, f32[128,256]{1,0:T(8,128)}, u32[]{:S(2)}) copy-start(f32[128,256]{1,0:T(8,128)} %refs_1_.2) | copy-start | bytes 393220
  11.7 1.3 %copy-start.10 = (s32[128]{0:T(128)S(1)}, s32[128]{0:T(128)}, u32[]{:S(2)}) copy-start(s32[128]{0:T(128)} %param.18) | copy-start | bytes 1540
  15.4 29.1 %copy-start.2 = (s32[128,1]{0,1:T(1,128)S(1)}, s32[128,1]{0,1:T(1,128)}, u32[]{:S(2)}) copy-start(s32[128,1]{0,1:T(1,128)} %param.19) | copy-start | bytes 1540
  15.4 29.1 %copy-start.5 = (bf16[1,256,1024]{2,1,0:T(8,128)(2,1)S(1)}, bf16[1,256,1024]{2,1,0:T(8,128)(2,1)}, u32[]{:S(2)}) copy-start(bf16[1,256,1024]{2,1,0:T(8,128)(2,1)} %refs_1_.3) | copy-start | bytes 1572868
  15.4 29.1 %copy-start.8 = (f32[1,1024]{1,0:T(1,128)S(1)}, f32[1,1024]{1,0:T(1,128)}, u32[]{:S(2)}) copy-start(f32[1,1024]{1,0:T(1,128)} %refs_2_.1) | copy-start | bytes 12292
  15.4 29.1 %copy-start.11 = (s32[128]{0:T(128)S(1)}, s32[128]{0:T(128)}, u32[]{:S(2)}) copy-start(s32[128]{0:T(128)} %param.20) | copy-start | bytes 1540
  44.5 1.6 %copy-start.3 = (bf16[1,1024,1024]{2,1,0:T(8,128)(2,1)S(1)}, bf16[1,1024,1024]{2,1,0:T(8,128)(2,1)}, u32[]{:S(2)}) copy-start(bf16[1,1024,1024]{2,1,0:T(8,128)(2,1)} %w_mid.1) | copy-start | bytes 6291460
  44.5 1.7 %copy-start.4 = (bf16[1,1024,264]{1,2,0:T(8,128)(2,1)S(1)}, bf16[1,1024,264]{1,2,0:T(8,128)(2,1)}, u32[]{:S(2)}) copy-start(bf16[1,1024,264]{1,2,0:T(8,128)(2,1)} %param.17) | copy-start | bytes 1622020
  44.5 1.7 %copy-start.9 = (f32[1,1024]{1,0:T(1,128)S(1)}, f32[1,1024]{1,0:T(1,128)}, u32[]{:S(2)}) copy-start(f32[1,1024]{1,0:T(1,128)} %b_mid.1) | copy-start | bytes 12292
  52.9 29.8 %copy-start.1 = (f32[32,32,256]{2,1,0:T(8,128)S(1)}, f32[32,32,256]{2,1,0:T(8,128)}, u32[]{:S(2)}) copy-start(f32[32,32,256]{2,1,0:T(8,128)} %state.5) | copy-start | bytes 3145732
  79.1 13.8 %all-to-all-start.2 = ((f32[128,2,128]{2,1,0:T(2,128)}), f32[128,2,128]{2,1,0:T(2,128)S(1)}, u32[]{:S(2)}, u32[]{:S(2)}) async-start(f32[128,2,128]{2,1,0:T(2,128)} %bitcast.7), calls=%async_computation.2 | async-start | bytes 262144 | tf_op jit(solution)/shard_map/all_to_all | solution.py:431

commit v7 on v6

--- a/solution.py
+++ b/solution.py
@@ -306,7 +306,7 @@
 
 
 def message_parts():
-    return [((4 * h + q) * 128, 4 * q, 128 * h) for h in range(2) for q in range(4)]
+    return [((8 * h + q) * 128, 2 * q, 128 * h) for h in range(2) for q in range(8)]
 
 
 def dot_by_output(a, b):
@@ -318,7 +318,7 @@
     sources = step // 16
     lane = iota((step, 128), 1)
     own = lane // 8 == iota((step, 128), 0) % 16
-    line = iota((sources, 4, 128), 1)
+    line = iota((sources, 2, 128), 1)
     w_half[...] = w_mid[0] * jnp.asarray(0.5, BF16)
     w_flux[...] = jnp.concatenate([w_last[0, 256:264, :].astype(F32)] * 16).astype(BF16)
     b_half = 0.5 * b_mid[...]
@@ -329,17 +329,17 @@
         part = slice(b * sources, (b + 1) * sources)
         for place, slot, feature in message_parts():
             out[part, :, place : place + 128] = tends[
-                :, slot : slot + 4, feature : feature + 128
+                :, slot : slot + 2, feature : feature + 128
             ].astype(BF16)
         flux = jnp.where(own, dot_by_output(hidden, w_flux[...]), 0.0)
         flux = jnp.sum(flux.reshape(sources, 16, 128), axis=1, keepdims=True)
         names = blocks[part, :].reshape(sources, 1, 128)
         tail = jnp.where(line == 0, flux, jnp.where(line == 1, names, 0.0))
-        out[part, :, 1024:1152] = tail.astype(BF16)
+        out[part, :, 2048:2176] = tail.astype(BF16)
 
 
 def contribution_kernel(sizes, answer, members, ranks, tiled, owner_row, send):
-    flux = answer[:, :, 1024:1152].astype(F32)[:, 0, :].astype(BF16)
+    flux = answer[:, :, 2048:2176].astype(F32)[:, 0, :].astype(BF16)
     spread = (iota((128, 128), 0) % 8 == iota((128, 128), 1) // 16).astype(F32).astype(BF16)
     lane = iota((128, 128), 1)
     group = lane // 8
@@ -381,7 +381,7 @@
     advanced[:, 0, :] = advanced[:, 0, :] + half * y_before[...]
     advanced[:, size_y - 1, :] = advanced[:, size_y - 1, :] + half * y_after[...]
     for place, slot, feature in message_parts():
-        wide[:, slot : slot + 4, feature : feature + 128] = answer[
+        wide[:, slot : slot + 2, feature : feature + 128] = answer[
             :, :, place : place + 128
         ].astype(F32)
     rows[...] = wide[...].reshape(slots, features).astype(BF16)
@@ -392,7 +392,7 @@
         tends = dot(hot.astype(F32).astype(BF16), rows[...])
         part = slice(b * lines, (b + 1) * lines)
         new_state[part] = advanced[part] + tends.reshape(lines, size_y, features)
-    names = answer[:, :, 1024:1152].astype(F32)[:, 1, :]
+    names = answer[:, :, 2048:2176].astype(F32)[:, 1, :]
     lane = iota((sources, 128), 1)
     for j in range(2):
         hot = (names[:, j : j + 1].astype(jnp.int32) == lane).astype(F32)
@@ -548,7 +548,7 @@
     )
     (answered,) = call(
         second_kernel,
-        [((devices, 4, 1152), BF16)],
+        [((devices, 2, 2176), BF16)],
         first,
         w_mid,
         bias_mid,

time: 94.1 us -> 93.6 us (level)
    pallas_call x13, Pallas kernels: 22.6 us -> 23.5 us  [call(): pl.pallas_call(kernel, out_shape=[jax.ShapeDtypeStruct(s, d) for s, d in...]
  transfers between devices with their start and end apart: 5 -> 5, of which waited for: 1 -> 1; matrix products, arithmetic and copies ran while one was open for 0% -> 0% of each run, Pallas kernels for 12% -> 13%
where the time goes in v7:
time: 93.6 us; the launch traced here: 93.3 us
  blocking collectives  52.4 us (56%)
  Pallas kernels  23.5 us (25%)
  starting transfers between devices  10 us (11%)
  waiting for transfers between devices  5.11 us (5%)
  local copies, waits for them, and re-layouts  1.43 us (2%)
    all_to_all x2, blocking collectives, exchange(): return lax.all_to_all(value, AXES, split_axis=0, concat_axis=0, tiled=True)  52.4 us
    pallas_call x13, Pallas kernels, call(): pl.pallas_call(kernel, out_shape=[jax.ShapeDtypeStruct(s, d) for s, d in...  23.5 us
    ppermute x4, starting transfers between devices, shift(): lax.ppermute(value, axis, [(i, (i + step) % size) for i in range(size)])  6.4 us
    all_to_all x1, waiting for transfers between devices, exchange(): return lax.all_to_all(value, AXES, split_axis=0, concat_axis=0, tiled=True)  5.09 us
    all_to_all x1, starting transfers between devices, exchange(): return lax.all_to_all(value, AXES, split_axis=0, concat_axis=0, tiled=True)  3.6 us
  transfers between devices with their start and end apart: 5, of which 1 were waited for; matrix products, arithmetic and copies ran while one was open for 0% of the time, Pallas kernels for 13%

profile of v7, /device:TPU:1, one launch (start us, length us, event | category | flops | bytes accessed | tf_op | source)
XLA Modules:
  0.0 93.3 jit_solution(15245094225883023983)
XLA Ops:
  0.6 0.0 copy-start
  0.6 1.2 %copy-done = f32[32,32,256]{2,1,0:T(8,128)S(1)} copy-done((f32[32,32,256]{2,1,0:T(8,128)S(1)}, f32[32,32,256]{2,1,0:T(8,128)}, u32[]{:S(2)}) %copy-start) | copy-done | bytes 1048600
  1.9 0.3 shard_map.122
  2.1 2.2 %collective-permute-start = (f32[32,256]{1,0:T(8,128)S(1)}, f32[32,256]{1,0:T(8,128)S(1)}, u32[]{:S(2)}, u32[]{:S(2)}) collective-permute-start(f32[32,256]{1,0:T(8,128)S(1)} %get-tuple-element.21), channel_id=1, source_target_pairs={{0,32},{32,64},{64,96},{96,0},{1,33},{33,65},{65,97},{97,1},{2,34}... | collective-permute-start | bytes 98312 | tf_op jit(solution)/shard_map/ppermute | solution.py:427
  4.3 1.5 %collective-permute-start.1 = (f32[32,256]{1,0:T(8,128)S(1)}, f32[32,256]{1,0:T(8,128)S(1)}, u32[]{:S(2)}, u32[]{:S(2)}) collective-permute-start(f32[32,256]{1,0:T(8,128)S(1)} %get-tuple-element.20.token), channel_id=1, source_target_pairs={{0,96},{32,0},{64,32},{96,64},{1,97},{33,1},{65,33},{97,65},{2,98}... | collective-permute-start | bytes 98312 | tf_op jit(solution)/shard_map/ppermute | solution.py:427
  5.8 1.7 %shard_map.123.partial = f32[32,32,256]{2,1,0:T(8,128)S(1)} custom-call(f32[32,32,256]{2,1,0:T(8,128)S(1)} %copy-done, f32[32,256]{1,0:T(8,128)S(1)} %get-tuple-element.20.token), custom_call_target="tpu_custom_call" | custom-call | flops 67108864 | bytes 8388608 | tf_op jit(solution)/shard_map/pallas_call | solution.py:407
  7.5 1.4 %shard_map.124 = (s32[1,1024]{1,0:T(1,128)S(1)}, bf16[2048,1024]{1,0:T(8,128)(2,1)S(1)}, bf16[2048,128]{1,0:T(8,128)(2,1)S(1)}) custom-call(s32[1,1024]{1,0:T(1,128)S(1)} %bitcast.13), custom_call_target="tpu_custom_call" | custom-call | flops 67108864 | bytes 8388608 | tf_op jit(solution)/shard_map/pallas_call | solution.py:407
  9.0 2.7 %collective-permute-start.2 = (f32[32,256]{1,0:T(8,128)S(1)}, f32[32,256]{1,0:T(8,128)S(1)}, u32[]{:S(2)}, u32[]{:S(2)}) collective-permute-start(f32[32,256]{1,0:T(8,128)S(1)} %get-tuple-element.28), channel_id=1, source_target_pairs={{0,1},{1,2},{2,3},{3,4},{4,5},{5,6},{6,7},{7,8},{8,9},{9,10},{10,1... | collective-permute-start | bytes 98312 | tf_op jit(solution)/shard_map/ppermute | solution.py:427
  11.7 1.3 %shard_map.125 = (bf16[2048,256]{1,0:T(8,128)(2,1)S(1)}, f32[64,256]{1,0:T(8,128)S(1)}) custom-call(f32[32,32,256]{2,1,0:T(8,128)S(1)} %shard_map.123.partial, f32[32,256]{1,0:T(8,128)S(1)} %collective-permute-done.x_before, f32[32,256]{1,0:T(8,128)S(1)} %collective-permute-done.1.x_after, bf16[2048,1024]{1,0:T(8,128)(2,1)S(1)} %get-tuple-element.22.hot_rows), custom_call_target="tpu_custom_call" | custom-call | flops 1073741824 | bytes 8388608 | tf_op jit(solution)/shard_map/pallas_call | solution.py:407
  13.0 2.3 %shard_map.127 = (s32[128,128]{1,0:T(8,128)S(1)}, s32[128,128]{1,0:T(8,128)S(1)}, f32[8,128,128]{2,1,0:T(8,128)S(1)}) custom-call(s32[1,128]{1,0:T(1,128)S(1)} %bitcast.14, f32[128,256]{1,0:T(8,128)S(1)} %copy-done.6, s32[1,1024]{1,0:T(1,128)S(1)} %get-tuple-element.27.slot_row.refs_2_, f32[64,256]{1,0:T(8,128)S(1)} %get-tuple-element.24.refs_3_.sides), custom_call_target="tpu_custom_call" | custom-call | flops 1073741824 | bytes 12582912 | tf_op jit(solution)/shard_map/pallas_call | solution.py:407
  15.4 0.0 copy-start.2
  15.4 0.4 shard_map.128
  15.8 28.6 %all_to_all.15 = bf16[128,16,256]{2,1,0:T(8,128)(2,1)S(1)} all-to-all(bf16[128,16,256]{2,1,0:T(8,128)(2,1)S(1)} %bitcast.8), channel_id=1, replica_groups=mesh['gx'=4,'gy'=32] {'gy','gx'}, dimensions={0} | all-to-all | bytes 2097152 | tf_op jit(solution)/shard_map/all_to_all | solution.py:431
  44.5 1.5 %shard_map.129 = (bf16[2048,1024]{1,0:T(8,128)(2,1)S(1)}, f32[128,128]{1,0:T(8,128)S(1)}) custom-call(bf16[2048,256]{1,0:T(8,128)(2,1)S(1)} %bitcast.9, bf16[1,256,1024]{2,1,0:T(8,128)(2,1)S(1)} %copy-done.5, f32[1,1024]{1,0:T(1,128)S(1)} %copy-done.8, s32[1,128]{1,0:T(1,128)S(1)} %bitcast.10, s32[1,128]{1,0:T(1,128)S(1)} %bitcast.15), custom_call_target="tpu_custom_call" | custom-call | flops 1073741824 | bytes 6291456 | tf_op jit(solution)/shard_map/pallas_call | solution.py:407
  46.0 0.1 copy-done.3
  46.1 0.1 copy-done.4
  46.2 6.9 %shard_map.130 = bf16[128,2,2176]{2,1,0:T(2,128)(2,1)S(1)} custom-call(bf16[2048,1024]{1,0:T(8,128)(2,1)S(1)} %get-tuple-element.32.first, bf16[1,1024,1024]{2,1,0:T(8,128)(2,1)S(1)} %copy-done.3, f32[1,1024]{1,0:T(1,128)S(1)} %copy-done.9, bf16[1,264,1024]{2,1,0:T(8,128)(2,1)S(1)} %bitcast.12, f32[128,128]{1,0:T(8,128)S(1)} %get-tuple-element.33.blocks), custom_call_target="tpu_custom_call" | custom-call | flops 5905580032 | bytes 8388608 | tf_op jit(solution)/shard_map/pallas_call | solution.py:407
  53.1 23.8 %all_to_all.16.refs_0_.answer = bf16[128,2,2176]{2,1,0:T(2,128)(2,1)S(1)} all-to-all(bf16[128,2,2176]{2,1,0:T(2,128)(2,1)S(1)} %shard_map.130), channel_id=1, replica_groups=mesh['gx'=4,'gy'=32] {'gy','gx'}, dimensions={0} | all-to-all | bytes 2228224 | tf_op jit(solution)/shard_map/all_to_all | solution.py:431
  76.8 1.8 %shard_map.131.token = f32[256,128]{1,0:T(8,128)} custom-call(bf16[128,2,2176]{2,1,0:T(2,128)(2,1)S(1)} %all_to_all.16.refs_0_.answer, s32[128,128]{1,0:T(8,128)S(1)} %get-tuple-element.31.members.refs_1_, s32[128,128]{1,0:T(8,128)S(1)} %get-tuple-element.34.refs_2_, f32[8,128,128]{2,1,0:T(8,128)S(1)} %get-tuple-element.35.refs_3_, s32[1,128]{1,0:T(1,128)S(1)} %bitcast.11), custom_call_target="tpu_custom_call" | custom-call | flops 134217728 | bytes 4194304 | tf_op jit(solution)/shard_map/pallas_call | solution.py:407
  78.6 3.6 %all-to-all-start.2 = ((f32[128,2,128]{2,1,0:T(2,128)}), f32[128,2,128]{2,1,0:T(2,128)S(1)}, u32[]{:S(2)}, u32[]{:S(2)}) async-start(f32[128,2,128]{2,1,0:T(2,128)} %bitcast.7), calls=%async_computation.2 | async-start | bytes 262144 | tf_op jit(solution)/shard_map/all_to_all | solution.py:431
  82.2 1.7 %shard_map.132.partial = f32[32,32,256]{2,1,0:T(8,128)S(1)} custom-call(f32[32,32,256]{2,1,0:T(8,128)S(1)} %copy-done.1, f32[256,128]{1,0:T(8,128)} %shard_map.131.token), custom_call_target="tpu_custom_call" | custom-call | flops 67108864 | bytes 8388608 | tf_op jit(solution)/shard_map/pallas_call | solution.py:407
  83.9 3.4 %shard_map.133 = (f32[32,32,256]{2,1,0:T(8,128)}, f32[2,16,128]{2,1,0:T(8,128)S(1)}) custom-call(bf16[128,2,2176]{2,1,0:T(2,128)(2,1)S(1)} %all_to_all.16.refs_0_.answer, s32[1,1024]{1,0:T(1,128)S(1)} %get-tuple-element.27.slot_row.refs_2_, f32[32,32,256]{2,1,0:T(8,128)S(1)} %shard_map.132.partial, f32[32,256]{1,0:T(8,128)S(1)} %collective-permute-done.x_before, ...), custom_call_target="tpu_custom_call" | custom-call | flops 1073741824 | bytes 12582912 | tf_op jit(solution)/shard_map/pallas_call | solution.py:407
  87.3 5.1 %all-to-all-done.2.received = f32[128,2,128]{2,1,0:T(2,128)S(1)} async-done(((f32[128,2,128]{2,1,0:T(2,128)}), f32[128,2,128]{2,1,0:T(2,128)S(1)}, u32[]{:S(2)}, u32[]{:S(2)}) %all-to-all-start.2) | async-done | bytes 131104 | tf_op jit(solution)/shard_map/all_to_all | solution.py:431
  92.4 0.9 shard_map.134
  (25 shorter events, 0.1 us)
Async XLA Ops:
  0.6 1.2 %copy-start = (f32[32,32,256]{2,1,0:T(8,128)S(1)}, f32[32,32,256]{2,1,0:T(8,128)}, u32[]{:S(2)}) copy-start(f32[32,32,256]{2,1,0:T(8,128)} %state.5) | copy-start | bytes 3145732
  1.9 5.6 %copy-start.7 = (s32[1024,1]{0,1:T(1,128)S(1)}, s32[1024,1]{0,1:T(1,128)}, u32[]{:S(2)}) copy-start(s32[1024,1]{0,1:T(1,128)} %param.12) | copy-start | bytes 12292
  2.1 6.8 %collective-permute-start = (f32[32,256]{1,0:T(8,128)S(1)}, f32[32,256]{1,0:T(8,128)S(1)}, u32[]{:S(2)}, u32[]{:S(2)}) collective-permute-start(f32[32,256]{1,0:T(8,128)S(1)} %get-tuple-element.21), channel_id=1, source_target_pairs={{0,32},{32,64},{64,96},{96,0},{1,33},{33,65},{65,97},{97,1},{2,34}... | collective-permute-start | bytes 98312 | tf_op jit(solution)/shard_map/ppermute | solution.py:427
  4.3 4.6 %collective-permute-start.1 = (f32[32,256]{1,0:T(8,128)S(1)}, f32[32,256]{1,0:T(8,128)S(1)}, u32[]{:S(2)}, u32[]{:S(2)}) collective-permute-start(f32[32,256]{1,0:T(8,128)S(1)} %get-tuple-element.20.token), channel_id=1, source_target_pairs={{0,96},{32,0},{64,32},{96,64},{1,97},{33,1},{65,33},{97,65},{2,98}... | collective-permute-start | bytes 98312 | tf_op jit(solution)/shard_map/ppermute | solution.py:427
  9.0 6.4 %collective-permute-start.2 = (f32[32,256]{1,0:T(8,128)S(1)}, f32[32,256]{1,0:T(8,128)S(1)}, u32[]{:S(2)}, u32[]{:S(2)}) collective-permute-start(f32[32,256]{1,0:T(8,128)S(1)} %get-tuple-element.28), channel_id=1, source_target_pairs={{0,1},{1,2},{2,3},{3,4},{4,5},{5,6},{6,7},{7,8},{8,9},{9,10},{10,1... | collective-permute-start | bytes 98312 | tf_op jit(solution)/shard_map/ppermute | solution.py:427
  11.6 3.7 %collective-permute-start.3 = (f32[32,256]{1,0:T(8,128)S(1)}, f32[32,256]{1,0:T(8,128)S(1)}, u32[]{:S(2)}, u32[]{:S(2)}) collective-permute-start(f32[32,256]{1,0:T(8,128)S(1)} %get-tuple-element.29), channel_id=1, source_target_pairs={{0,31},{1,0},{2,1},{3,2},{4,3},{5,4},{6,5},{7,6},{8,7},{9,8},{10,9... | collective-permute-start | bytes 98312 | tf_op jit(solution)/shard_map/ppermute | solution.py:427
  11.7 1.3 %copy-start.6 = (f32[128,256]{1,0:T(8,128)S(1)}, f32[128,256]{1,0:T(8,128)}, u32[]{:S(2)}) copy-start(f32[128,256]{1,0:T(8,128)} %refs_1_.2) | copy-start | bytes 393220
  11.7 1.3 %copy-start.10 = (s32[128]{0:T(128)S(1)}, s32[128]{0:T(128)}, u32[]{:S(2)}) copy-start(s32[128]{0:T(128)} %param.18) | copy-start | bytes 1540
  15.4 29.1 %copy-start.2 = (s32[128,1]{0,1:T(1,128)S(1)}, s32[128,1]{0,1:T(1,128)}, u32[]{:S(2)}) copy-start(s32[128,1]{0,1:T(1,128)} %param.19) | copy-start | bytes 1540
  15.4 29.1 %copy-start.5 = (bf16[1,256,1024]{2,1,0:T(8,128)(2,1)S(1)}, bf16[1,256,1024]{2,1,0:T(8,128)(2,1)}, u32[]{:S(2)}) copy-start(bf16[1,256,1024]{2,1,0:T(8,128)(2,1)} %refs_1_.3) | copy-start | bytes 1572868
  15.4 29.1 %copy-start.8 = (f32[1,1024]{1,0:T(1,128)S(1)}, f32[1,1024]{1,0:T(1,128)}, u32[]{:S(2)}) copy-start(f32[1,1024]{1,0:T(1,128)} %refs_2_.1) | copy-start | bytes 12292
  15.4 29.1 %copy-start.11 = (s32[128]{0:T(128)S(1)}, s32[128]{0:T(128)}, u32[]{:S(2)}) copy-start(s32[128]{0:T(128)} %param.20) | copy-start | bytes 1540
  44.5 1.6 %copy-start.3 = (bf16[1,1024,1024]{2,1,0:T(8,128)(2,1)S(1)}, bf16[1,1024,1024]{2,1,0:T(8,128)(2,1)}, u32[]{:S(2)}) copy-start(bf16[1,1024,1024]{2,1,0:T(8,128)(2,1)} %w_mid.1) | copy-start | bytes 6291460
  44.5 1.7 %copy-start.4 = (bf16[1,1024,264]{1,2,0:T(8,128)(2,1)S(1)}, bf16[1,1024,264]{1,2,0:T(8,128)(2,1)}, u32[]{:S(2)}) copy-start(bf16[1,1024,264]{1,2,0:T(8,128)(2,1)} %param.17) | copy-start | bytes 1622020
  44.5 1.7 %copy-start.9 = (f32[1,1024]{1,0:T(1,128)S(1)}, f32[1,1024]{1,0:T(1,128)}, u32[]{:S(2)}) copy-start(f32[1,1024]{1,0:T(1,128)} %b_mid.1) | copy-start | bytes 12292
  53.1 29.1 %copy-start.1 = (f32[32,32,256]{2,1,0:T(8,128)S(1)}, f32[32,32,256]{2,1,0:T(8,128)}, u32[]{:S(2)}) copy-start(f32[32,32,256]{2,1,0:T(8,128)} %state.5) | copy-start | bytes 3145732
  78.6 13.8 %all-to-all-start.2 = ((f32[128,2,128]{2,1,0:T(2,128)}), f32[128,2,128]{2,1,0:T(2,128)S(1)}, u32[]{:S(2)}, u32[]{:S(2)}) async-start(f32[128,2,128]{2,1,0:T(2,128)} %bitcast.7), calls=%async_computation.2 | async-start | bytes 262144 | tf_op jit(solution)/shard_map/all_to_all | solution.py:431

commit v8 on v7

--- a/solution.py
+++ b/solution.py
@@ -119,7 +119,7 @@
         out[...] = advect(lines[i], along_rows(lines[i]), across(lines, i))
 
 
-def sides_kernel(y_low, y_high, x_before, x_after, partial, slot_row, low, high):
+def sides_kernel(y_low, y_high, x_before, x_after, partial, low, high):
     size, features = y_low.shape
     row = iota((size, features), 0)
     for out, line, y in ((low, y_low, 0), (high, y_high, size - 1)):
@@ -178,7 +178,7 @@
     return device % size_gy * size_gx + device // size_gy
 
 
-def route_kernel(sizes, capacity, size_y, member_row, slot_row, hot_rows, hot_sides):
+def route_kernel(sizes, capacity, size_y, member_row, low, slot_row, hot_rows, hot_sides):
     columns = member_row.shape[1]
     size_x = columns // size_y
     earlier = (iota((128, 128), 0) < iota((128, 128), 1)).astype(F32).astype(BF16)
@@ -475,13 +475,6 @@
         )[0]
 
     partial = local(x_low)
-    slot_row, hot_rows, hot_sides = call(
-        lambda *refs: route_kernel(sizes, capacity, size_y, *refs),
-        [((1, columns), jnp.int32), ((slots, columns), BF16), ((slots, 128), BF16)],
-        group_member.reshape(1, columns),
-        nbytes=8 * MIB,
-        flops=64 * MIB,
-    )
     low, high = call(
         sides_kernel,
         [line] * 2,
@@ -490,10 +483,18 @@
         x_before,
         x_after,
         partial,
-        slot_row,
-        spaces={4: pl.ANY, 5: pl.ANY},
+        spaces={4: pl.ANY},
     )
     y_before, y_after = shift(high, "gy", 1), shift(low, "gy", -1)
+    slot_row, hot_rows, hot_sides = call(
+        lambda *refs: route_kernel(sizes, capacity, size_y, *refs),
+        [((1, columns), jnp.int32), ((slots, columns), BF16), ((slots, 128), BF16)],
+        group_member.reshape(1, columns),
+        low,
+        spaces={1: pl.ANY},
+        nbytes=8 * MIB,
+        flops=64 * MIB,
+    )
     inner, sides = call(
         inner_kernel,
         [((slots, features), BF16), ((2 * size_x, features), F32)],

time: 93.6 us -> 95 us (1.015)
  transfers between devices with their start and end apart: 5 -> 5, of which waited for: 1 -> 1; matrix products, arithmetic and copies ran while one was open for 0% -> 0% of each run, Pallas kernels for 13% -> 12%
where the time goes in v8:
time: 95 us; the launch traced here: 94.7 us
  blocking collectives  53.2 us (56%)
  Pallas kernels  23.6 us (25%)
  starting transfers between devices  10.6 us (11%)
  waiting for transfers between devices  5.11 us (5%)
  local copies, waits for them, and re-layouts  1.44 us (2%)
    all_to_all x2, blocking collectives, exchange(): return lax.all_to_all(value, AXES, split_axis=0, concat_axis=0, tiled=True)  53.2 us
    pallas_call x13, Pallas kernels, call(): pl.pallas_call(kernel, out_shape=[jax.ShapeDtypeStruct(s, d) for s, d in...  23.6 us
    ppermute x4, starting transfers between devices, shift(): lax.ppermute(value, axis, [(i, (i + step) % size) for i in range(size)])  6.96 us
    all_to_all x1, waiting for transfers between devices, exchange(): return lax.all_to_all(value, AXES, split_axis=0, concat_axis=0, tiled=True)  5.09 us
    all_to_all x1, starting transfers between devices, exchange(): return lax.all_to_all(value, AXES, split_axis=0, concat_axis=0, tiled=True)  3.6 us
  transfers between devices with their start and end apart: 5, of which 1 were waited for; matrix products, arithmetic and copies ran while one was open for 0% of the time, Pallas kernels for 12%

profile of v8, /device:TPU:1, one launch (start us, length us, event | category | flops | bytes accessed | tf_op | source)
XLA Modules:
  0.0 94.7 jit_solution(8142462345682216111)
XLA Ops:
  0.6 0.0 copy-start
  0.6 1.2 %copy-done = f32[32,32,256]{2,1,0:T(8,128)S(1)} copy-done((f32[32,32,256]{2,1,0:T(8,128)S(1)}, f32[32,32,256]{2,1,0:T(8,128)}, u32[]{:S(2)}) %copy-start) | copy-done | bytes 1048600
  1.9 0.3 shard_map.122
  2.1 2.2 %collective-permute-start = (f32[32,256]{1,0:T(8,128)S(1)}, f32[32,256]{1,0:T(8,128)S(1)}, u32[]{:S(2)}, u32[]{:S(2)}) collective-permute-start(f32[32,256]{1,0:T(8,128)S(1)} %get-tuple-element.21), channel_id=1, source_target_pairs={{0,32},{32,64},{64,96},{96,0},{1,33},{33,65},{65,97},{97,1},{2,34}... | collective-permute-start | bytes 98312 | tf_op jit(solution)/shard_map/ppermute | solution.py:427
  4.3 1.5 %collective-permute-start.1 = (f32[32,256]{1,0:T(8,128)S(1)}, f32[32,256]{1,0:T(8,128)S(1)}, u32[]{:S(2)}, u32[]{:S(2)}) collective-permute-start(f32[32,256]{1,0:T(8,128)S(1)} %get-tuple-element.20.token), channel_id=1, source_target_pairs={{0,96},{32,0},{64,32},{96,64},{1,97},{33,1},{65,33},{97,65},{2,98}... | collective-permute-start | bytes 98312 | tf_op jit(solution)/shard_map/ppermute | solution.py:427
  5.8 1.7 %shard_map.123.partial = f32[32,32,256]{2,1,0:T(8,128)S(1)} custom-call(f32[32,32,256]{2,1,0:T(8,128)S(1)} %copy-done, f32[32,256]{1,0:T(8,128)S(1)} %get-tuple-element.20.token), custom_call_target="tpu_custom_call" | custom-call | flops 67108864 | bytes 8388608 | tf_op jit(solution)/shard_map/pallas_call | solution.py:407
  7.6 3.2 %collective-permute-start.2 = (f32[32,256]{1,0:T(8,128)S(1)}, f32[32,256]{1,0:T(8,128)S(1)}, u32[]{:S(2)}, u32[]{:S(2)}) collective-permute-start(f32[32,256]{1,0:T(8,128)S(1)} %get-tuple-element.28), channel_id=1, source_target_pairs={{0,1},{1,2},{2,3},{3,4},{4,5},{5,6},{6,7},{7,8},{8,9},{9,10},{10,1... | collective-permute-start | bytes 98312 | tf_op jit(solution)/shard_map/ppermute | solution.py:427
  10.8 1.4 %shard_map.125 = (s32[1,1024]{1,0:T(1,128)S(1)}, bf16[2048,1024]{1,0:T(8,128)(2,1)S(1)}, bf16[2048,128]{1,0:T(8,128)(2,1)S(1)}) custom-call(s32[1,1024]{1,0:T(1,128)S(1)} %bitcast.13, f32[32,256]{1,0:T(8,128)S(1)} %get-tuple-element.24.refs_1_), custom_call_target="tpu_custom_call" | custom-call | flops 67108864 | bytes 8388608 | tf_op jit(solution)/shard_map/pallas_call | solution.py:407
  12.2 0.0 copy-start.6
  12.2 1.3 %shard_map.126 = (bf16[2048,256]{1,0:T(8,128)(2,1)S(1)}, f32[64,256]{1,0:T(8,128)S(1)}) custom-call(f32[32,32,256]{2,1,0:T(8,128)S(1)} %shard_map.123.partial, f32[32,256]{1,0:T(8,128)S(1)} %collective-permute-done.x_before, f32[32,256]{1,0:T(8,128)S(1)} %collective-permute-done.1.x_after, bf16[2048,1024]{1,0:T(8,128)(2,1)S(1)} %get-tuple-element.25.hot_rows), custom_call_target="tpu_custom_call" | custom-call | flops 1073741824 | bytes 8388608 | tf_op jit(solution)/shard_map/pallas_call | solution.py:407
  13.6 2.3 %shard_map.127 = (s32[128,128]{1,0:T(8,128)S(1)}, s32[128,128]{1,0:T(8,128)S(1)}, f32[8,128,128]{2,1,0:T(8,128)S(1)}) custom-call(s32[1,128]{1,0:T(1,128)S(1)} %bitcast.14, f32[128,256]{1,0:T(8,128)S(1)} %copy-done.6, s32[1,1024]{1,0:T(1,128)S(1)} %get-tuple-element.30.refs_2_.slot_row, f32[64,256]{1,0:T(8,128)S(1)} %get-tuple-element.27.refs_3_.sides), custom_call_target="tpu_custom_call" | custom-call | flops 1073741824 | bytes 12582912 | tf_op jit(solution)/shard_map/pallas_call | solution.py:407
  16.0 0.4 shard_map.128
  16.4 29.5 %all_to_all.15 = bf16[128,16,256]{2,1,0:T(8,128)(2,1)S(1)} all-to-all(bf16[128,16,256]{2,1,0:T(8,128)(2,1)S(1)} %bitcast.8), channel_id=1, replica_groups=mesh['gx'=4,'gy'=32] {'gy','gx'}, dimensions={0} | all-to-all | bytes 2097152 | tf_op jit(solution)/shard_map/all_to_all | solution.py:431
  45.9 1.5 %shard_map.129 = (bf16[2048,1024]{1,0:T(8,128)(2,1)S(1)}, f32[128,128]{1,0:T(8,128)S(1)}) custom-call(bf16[2048,256]{1,0:T(8,128)(2,1)S(1)} %bitcast.9, bf16[1,256,1024]{2,1,0:T(8,128)(2,1)S(1)} %copy-done.5, f32[1,1024]{1,0:T(1,128)S(1)} %copy-done.8, s32[1,128]{1,0:T(1,128)S(1)} %bitcast.10, s32[1,128]{1,0:T(1,128)S(1)} %bitcast.15), custom_call_target="tpu_custom_call" | custom-call | flops 1073741824 | bytes 6291456 | tf_op jit(solution)/shard_map/pallas_call | solution.py:407
  47.4 0.1 copy-done.3
  47.5 0.1 copy-done.4
  47.6 6.9 %shard_map.130 = bf16[128,2,2176]{2,1,0:T(2,128)(2,1)S(1)} custom-call(bf16[2048,1024]{1,0:T(8,128)(2,1)S(1)} %get-tuple-element.32.first, bf16[1,1024,1024]{2,1,0:T(8,128)(2,1)S(1)} %copy-done.3, f32[1,1024]{1,0:T(1,128)S(1)} %copy-done.9, bf16[1,264,1024]{2,1,0:T(8,128)(2,1)S(1)} %bitcast.12, f32[128,128]{1,0:T(8,128)S(1)} %get-tuple-element.33.blocks), custom_call_target="tpu_custom_call" | custom-call | flops 5905580032 | bytes 8388608 | tf_op jit(solution)/shard_map/pallas_call | solution.py:407
  54.5 23.8 %all_to_all.16.refs_0_.answer = bf16[128,2,2176]{2,1,0:T(2,128)(2,1)S(1)} all-to-all(bf16[128,2,2176]{2,1,0:T(2,128)(2,1)S(1)} %shard_map.130), channel_id=1, replica_groups=mesh['gx'=4,'gy'=32] {'gy','gx'}, dimensions={0} | all-to-all | bytes 2228224 | tf_op jit(solution)/shard_map/all_to_all | solution.py:431
  78.3 1.8 %shard_map.131.token = f32[256,128]{1,0:T(8,128)} custom-call(bf16[128,2,2176]{2,1,0:T(2,128)(2,1)S(1)} %all_to_all.16.refs_0_.answer, s32[128,128]{1,0:T(8,128)S(1)} %get-tuple-element.31.members.refs_1_, s32[128,128]{1,0:T(8,128)S(1)} %get-tuple-element.34.refs_2_, f32[8,128,128]{2,1,0:T(8,128)S(1)} %get-tuple-element.35.refs_3_, s32[1,128]{1,0:T(1,128)S(1)} %bitcast.11), custom_call_target="tpu_custom_call" | custom-call | flops 134217728 | bytes 4194304 | tf_op jit(solution)/shard_map/pallas_call | solution.py:407
  80.0 3.6 %all-to-all-start.2 = ((f32[128,2,128]{2,1,0:T(2,128)}), f32[128,2,128]{2,1,0:T(2,128)S(1)}, u32[]{:S(2)}, u32[]{:S(2)}) async-start(f32[128,2,128]{2,1,0:T(2,128)} %bitcast.7), calls=%async_computation.2 | async-start | bytes 262144 | tf_op jit(solution)/shard_map/all_to_all | solution.py:431
  83.7 1.7 %shard_map.132.partial = f32[32,32,256]{2,1,0:T(8,128)S(1)} custom-call(f32[32,32,256]{2,1,0:T(8,128)S(1)} %copy-done.1, f32[256,128]{1,0:T(8,128)} %shard_map.131.token), custom_call_target="tpu_custom_call" | custom-call | flops 67108864 | bytes 8388608 | tf_op jit(solution)/shard_map/pallas_call | solution.py:407
  85.3 3.4 %shard_map.133 = (f32[32,32,256]{2,1,0:T(8,128)}, f32[2,16,128]{2,1,0:T(8,128)S(1)}) custom-call(bf16[128,2,2176]{2,1,0:T(2,128)(2,1)S(1)} %all_to_all.16.refs_0_.answer, s32[1,1024]{1,0:T(1,128)S(1)} %get-tuple-element.30.refs_2_.slot_row, f32[32,32,256]{2,1,0:T(8,128)S(1)} %shard_map.132.partial, f32[32,256]{1,0:T(8,128)S(1)} %collective-permute-done.x_before, ...), custom_call_target="tpu_custom_call" | custom-call | flops 1073741824 | bytes 12582912 | tf_op jit(solution)/shard_map/pallas_call | solution.py:407
  88.8 5.1 %all-to-all-done.2.received = f32[128,2,128]{2,1,0:T(2,128)S(1)} async-done(((f32[128,2,128]{2,1,0:T(2,128)}), f32[128,2,128]{2,1,0:T(2,128)S(1)}, u32[]{:S(2)}, u32[]{:S(2)}) %all-to-all-start.2) | async-done | bytes 131104 | tf_op jit(solution)/shard_map/all_to_all | solution.py:431
  93.9 0.9 shard_map.134
  (25 shorter events, 0.1 us)
Async XLA Ops:
  0.6 1.2 %copy-start = (f32[32,32,256]{2,1,0:T(8,128)S(1)}, f32[32,32,256]{2,1,0:T(8,128)}, u32[]{:S(2)}) copy-start(f32[32,32,256]{2,1,0:T(8,128)} %state.5) | copy-start | bytes 3145732
  1.9 9.0 %copy-start.7 = (s32[1024,1]{0,1:T(1,128)S(1)}, s32[1024,1]{0,1:T(1,128)}, u32[]{:S(2)}) copy-start(s32[1024,1]{0,1:T(1,128)} %param.12) | copy-start | bytes 12292
  2.1 5.4 %collective-permute-start = (f32[32,256]{1,0:T(8,128)S(1)}, f32[32,256]{1,0:T(8,128)S(1)}, u32[]{:S(2)}, u32[]{:S(2)}) collective-permute-start(f32[32,256]{1,0:T(8,128)S(1)} %get-tuple-element.21), channel_id=1, source_target_pairs={{0,32},{32,64},{64,96},{96,0},{1,33},{33,65},{65,97},{97,1},{2,34}... | collective-permute-start | bytes 98312 | tf_op jit(solution)/shard_map/ppermute | solution.py:427
  4.3 3.2 %collective-permute-start.1 = (f32[32,256]{1,0:T(8,128)S(1)}, f32[32,256]{1,0:T(8,128)S(1)}, u32[]{:S(2)}, u32[]{:S(2)}) collective-permute-start(f32[32,256]{1,0:T(8,128)S(1)} %get-tuple-element.20.token), channel_id=1, source_target_pairs={{0,96},{32,0},{64,32},{96,64},{1,97},{33,1},{65,33},{97,65},{2,98}... | collective-permute-start | bytes 98312 | tf_op jit(solution)/shard_map/ppermute | solution.py:427
  7.6 8.4 %collective-permute-start.2 = (f32[32,256]{1,0:T(8,128)S(1)}, f32[32,256]{1,0:T(8,128)S(1)}, u32[]{:S(2)}, u32[]{:S(2)}) collective-permute-start(f32[32,256]{1,0:T(8,128)S(1)} %get-tuple-element.28), channel_id=1, source_target_pairs={{0,1},{1,2},{2,3},{3,4},{4,5},{5,6},{6,7},{7,8},{8,9},{9,10},{10,1... | collective-permute-start | bytes 98312 | tf_op jit(solution)/shard_map/ppermute | solution.py:427
  10.8 5.1 %collective-permute-start.3 = (f32[32,256]{1,0:T(8,128)S(1)}, f32[32,256]{1,0:T(8,128)S(1)}, u32[]{:S(2)}, u32[]{:S(2)}) collective-permute-start(f32[32,256]{1,0:T(8,128)S(1)} %get-tuple-element.24.refs_1_), channel_id=1, source_target_pairs={{0,31},{1,0},{2,1},{3,2},{4,3},{5,4},{6,5},{7,6},{8,7},{9,8},{10,9... | collective-permute-start | bytes 98312 | tf_op jit(solution)/shard_map/ppermute | solution.py:427
  12.2 1.4 %copy-start.6 = (f32[128,256]{1,0:T(8,128)S(1)}, f32[128,256]{1,0:T(8,128)}, u32[]{:S(2)}) copy-start(f32[128,256]{1,0:T(8,128)} %refs_1_.2) | copy-start | bytes 393220
  12.2 1.4 %copy-start.10 = (s32[128]{0:T(128)S(1)}, s32[128]{0:T(128)}, u32[]{:S(2)}) copy-start(s32[128]{0:T(128)} %param.18) | copy-start | bytes 1540
  15.9 30.0 %copy-start.2 = (s32[128,1]{0,1:T(1,128)S(1)}, s32[128,1]{0,1:T(1,128)}, u32[]{:S(2)}) copy-start(s32[128,1]{0,1:T(1,128)} %param.19) | copy-start | bytes 1540
  16.0 30.0 %copy-start.5 = (bf16[1,256,1024]{2,1,0:T(8,128)(2,1)S(1)}, bf16[1,256,1024]{2,1,0:T(8,128)(2,1)}, u32[]{:S(2)}) copy-start(bf16[1,256,1024]{2,1,0:T(8,128)(2,1)} %refs_1_.3) | copy-start | bytes 1572868
  16.0 30.0 %copy-start.8 = (f32[1,1024]{1,0:T(1,128)S(1)}, f32[1,1024]{1,0:T(1,128)}, u32[]{:S(2)}) copy-start(f32[1,1024]{1,0:T(1,128)} %refs_2_.1) | copy-start | bytes 12292
  16.0 30.0 %copy-start.11 = (s32[128]{0:T(128)S(1)}, s32[128]{0:T(128)}, u32[]{:S(2)}) copy-start(s32[128]{0:T(128)} %param.20) | copy-start | bytes 1540
  45.9 1.6 %copy-start.3 = (bf16[1,1024,1024]{2,1,0:T(8,128)(2,1)S(1)}, bf16[1,1024,1024]{2,1,0:T(8,128)(2,1)}, u32[]{:S(2)}) copy-start(bf16[1,1024,1024]{2,1,0:T(8,128)(2,1)} %w_mid.1) | copy-start | bytes 6291460
  45.9 1.7 %copy-start.4 = (bf16[1,1024,264]{1,2,0:T(8,128)(2,1)S(1)}, bf16[1,1024,264]{1,2,0:T(8,128)(2,1)}, u32[]{:S(2)}) copy-start(bf16[1,1024,264]{1,2,0:T(8,128)(2,1)} %param.17) | copy-start | bytes 1622020
  45.9 1.7 %copy-start.9 = (f32[1,1024]{1,0:T(1,128)S(1)}, f32[1,1024]{1,0:T(1,128)}, u32[]{:S(2)}) copy-start(f32[1,1024]{1,0:T(1,128)} %b_mid.1) | copy-start | bytes 12292
  54.5 29.1 %copy-start.1 = (f32[32,32,256]{2,1,0:T(8,128)S(1)}, f32[32,32,256]{2,1,0:T(8,128)}, u32[]{:S(2)}) copy-start(f32[32,32,256]{2,1,0:T(8,128)} %state.5) | copy-start | bytes 3145732
  80.0 13.8 %all-to-all-start.2 = ((f32[128,2,128]{2,1,0:T(2,128)}), f32[128,2,128]{2,1,0:T(2,128)S(1)}, u32[]{:S(2)}, u32[]{:S(2)}) async-start(f32[128,2,128]{2,1,0:T(2,128)} %bitcast.7), calls=%async_computation.2 | async-start | bytes 262144 | tf_op jit(solution)/shard_map/all_to_all | solution.py:431
